TPU v7x, 256 devices: a whole 4x4x8 slice. The times are simulated.
256 devices in a mesh: wide: 32 (over x, z), narrow: 8 (over y, core).
Axes of the slice: x: 4, y: 4, z: 8, core: 2. Of those that a mesh axis runs over, the one named last changes fastest.
Arguments:
- tokens: bfloat16 [1024, 8192], P('wide', 'narrow'), may hold values from -6 to 6
- gate_matrix: bfloat16 [8192, 28672], P('narrow', 'wide'), may hold values from -0.0625 to 0.0625
- up_matrix: bfloat16 [8192, 28672], P('narrow', 'wide'), may hold values from -0.0625 to 0.0625
- down_matrix: bfloat16 [28672, 8192], P('wide', 'narrow'), may hold values from -0.03125 to 0.03125
- adapter_down_factors: bfloat16 [8192, 256, 64], P('narrow', 'wide'), may hold values from -0.0625 to 0.0625
- adapter_up_factors: bfloat16 [256, 64, 28672], P('narrow', None, 'wide'), may hold values from -0.75 to 0.75
- adapter_index_rows: int32 [1024], replicated, may hold values from 0 to 255
Outputs:
- mixed: bfloat16 [1024, 8192], P('wide', 'narrow')
All inputs are finite; a program needn't handle non-finite values.
Results may differ from a plain program's by a relative error of at most 0.0054.
Values may be sent and summed in bfloat16 or wider, within the bound.
No kernel may reach another device: no remote copies, remote signals or barrier semaphores. Data moves between devices by JAX's collectives and lax.ppermute only.
A program may use at most 128 MiB of HBM per device.

v0:
```python
import jax
import jax.numpy as jnp
from jax import lax
from jax.sharding import PartitionSpec as P


def body(
    tokens,
    gate_matrix,
    up_matrix,
    down_matrix,
    adapter_down_factors,
    adapter_up_factors,
    adapter_index_rows,
):
    wide_index = lax.axis_index("wide")
    narrow_index = lax.axis_index("narrow")
    model_width_block = gate_matrix.shape[0]
    hidden_unit_block = gate_matrix.shape[1]
    kept_lower_factor = adapter_down_factors.shape[1]
    rank_extent = adapter_down_factors.shape[2]
    kept_upper_factor = adapter_up_factors.shape[0]
    requests = adapter_index_rows.shape[0]
    joined = jnp.concatenate(
        [
            gate_matrix,
            up_matrix,
            adapter_down_factors.reshape(model_width_block, kept_lower_factor * rank_extent),
        ],
        axis=1,
    )
    partial_all = jnp.dot(
        lax.all_gather(tokens, "wide", axis=0, tiled=True),
        joined,
        preferred_element_type=jnp.float32,
    )
    gate_part = partial_all[:, :hidden_unit_block]
    up_part = partial_all[:, hidden_unit_block : 2 * hidden_unit_block]
    shrink = partial_all[:, 2 * hidden_unit_block :].reshape(
        requests, kept_lower_factor, rank_extent
    )
    local_a = adapter_index_rows - wide_index * kept_lower_factor
    pick_a = (local_a[:, None] == jnp.arange(kept_lower_factor, dtype=jnp.int32)[None, :]).astype(
        jnp.float32
    )
    low_part = jnp.sum(shrink * pick_a[:, :, None], axis=1)
    low = lax.psum(low_part, ("wide", "narrow")).astype(jnp.bfloat16)
    local_b = adapter_index_rows - narrow_index * kept_upper_factor
    pick_b = (local_b[:, None] == jnp.arange(kept_upper_factor, dtype=jnp.int32)[None, :]).astype(
        jnp.bfloat16
    )
    adapter_spread = (pick_b[:, :, None] * low[:, None, :]).reshape(
        requests, kept_upper_factor * rank_extent
    )
    up_part = up_part + jnp.dot(
        adapter_spread,
        adapter_up_factors.reshape(kept_upper_factor * rank_extent, hidden_unit_block),
        preferred_element_type=jnp.float32,
    )
    gate_sum, up_sum = lax.psum((gate_part, up_part), "narrow")
    hidden = (jax.nn.silu(gate_sum) * up_sum).astype(jnp.bfloat16)
    mixed = lax.psum_scatter(
        jnp.dot(hidden, down_matrix, preferred_element_type=jnp.float32),
        "wide",
        scatter_dimension=0,
        tiled=True,
    )
    return mixed.astype(jnp.bfloat16)


def solution(mesh):
    placed = (
        P("wide", "narrow"),
        P("narrow", "wide"),
        P("narrow", "wide"),
        P("wide", "narrow"),
        P("narrow", "wide", None),
        P("narrow", None, "wide"),
        P(),
    )
    return jax.shard_map(
        body, mesh=mesh, in_specs=placed, out_specs=P("wide", "narrow"), check_vma=False
    )
```

profile of v0, /device:TPU:9, one launch (start us, length us, event | category | flops | bytes accessed | tf_op | source)
XLA Modules:
  0.0 513.6 jit_solution(1606778415883881894)
XLA Ops:
  6.5 0.0 copy-start
  6.5 0.0 all-gather.2.cloned.1.call-start
  6.5 0.7 all-gather.2.cloned.1.call-update
  7.3 0.0 all-reduce.4.cloned.1.call-start
  7.3 1.5 copy.11
  8.8 0.7 broadcast_subtract_fusion.1
  9.5 77.3 %all-gather.2.cloned.1.call-done = bf16[1024,1024]{1,0:T(8,128)(2,1)} async-done(((bf16[32,1024]{1,0:T(8,128)(2,1)}), bf16[1024,1024]{1,0:T(8,128)(2,1)}) %all-gather.2.cloned.1.call-update) | async-done | bytes 2097168 | tf_op jit(solution)/shard_map/all_gather | solution.py:33
  86.8 7.8 %convolution_bitcast_fusion = f32[1024,2304]{0,1:T(8,128)S(1)} fusion(bf16[1024,1024]{1,0:T(8,128)(2,1)} %all-gather.2.cloned.1.call-done, bf16[1024,512]{1,0:T(8,128)(2,1)S(1)} %copy.11, bf16[1024,896]{1,0:T(8,128)(2,1)} %param.9, bf16[1024,896]{1,0:T(8,128)(2,1)} %param.8), kind=kOutput, calls=%fused_computation | convolution fusion | flops 4845993984 | bytes 16252928 | tf_op jit(solution)/shard_map/dot_general | solution.py:32
  94.7 0.0 copy-start.1
  94.7 0.2 slice.14
  94.9 2.4 slice.12
  97.4 2.1 copy-done.1
  99.4 0.3 multiply_reduce_fusion
  99.7 77.9 %all-reduce.5 = bf16[1024,64]{0,1:T(8,128)(2,1)S(1)} all-reduce(f32[1024,64]{0,1:T(8,128)S(1)} %multiply_reduce_fusion), channel_id=1, replica_groups=mesh['wide'=32,'narrow'=8] {'wide','narrow'}, use_global_device_ids=true, to_apply=%region_2.0 | all-reduce | flops 65536 | bytes 393216 | tf_op jit(solution)/shard_map/psum | solution.py:47
  177.6 8.1 %slice_add_fusion = f32[1024,896]{0,1:T(8,128)} fusion(f32[1024,2304]{0,1:T(8,128)} %copy-done.1, bf16[32,64,896]{2,1,0:T(8,128)(2,1)} %param.12, bf16[1024,64]{0,1:T(8,128)(2,1)S(1)} %all-reduce.5, bf16[1024,32]{0,1:T(8,128)(2,1)S(1)} %fusion.12), kind=kOutput, calls=%fused_computation.8 | convolution fusion | flops 3761111040 | bytes 11206656 | tf_op jit(solution)/shard_map/dot_general | solution.py:55
  185.8 0.0 all-reduce.4.cloned.1.call-update
  185.8 0.2 reduce-scatter.2.cloned.1.call-start
  186.0 95.3 %all-reduce.4.cloned.1.call-done = (f32[1024,896]{0,1:T(8,128)}, f32[1024,896]{0,1:T(8,128)}) async-done(((f32[1024,896]{0,1:T(8,128)}, f32[1024,896]{0,1:T(8,128)}), (f32[1024,896]{0,1:T(8,128)}, f32[1024,896]{0,1:T(8,128)})) %all-reduce.4.cloned.1.call-update) | async-done | bytes 7340048 | tf_op jit(solution)/shard_map/psum | solution.py:60
  281.3 0.0 copy-done
  281.3 7.5 %fusion.9 = f32[1024,1024]{1,0:T(8,128)} fusion(bf16[896,1024]{1,0:T(8,128)(2,1)S(1)} %copy-done, f32[1024,896]{0,1:T(8,128)} %get-tuple-element.5, f32[1024,896]{0,1:T(8,128)} %get-tuple-element.6), kind=kOutput, calls=%fused_computation.13 | convolution fusion | flops 1884553216 | bytes 13369344 | tf_op jit(solution)/shard_map/dot_general | solution.py:63
  288.8 0.0 reduce-scatter.2.cloned.1.call-update
  288.8 216.7 %reduce-scatter.2.cloned.1.call-done = f32[32,1024]{1,0:T(8,128)} async-done(((f32[1024,1024]{1,0:T(8,128)}), f32[32,1024]{1,0:T(8,128)}) %reduce-scatter.2.cloned.1.call-update) | async-done | bytes 131088 | tf_op jit(solution)/shard_map/reduce_scatter | solution.py:62
  505.5 1.5 convert_element_type.27
  (2 shorter events, 0.0 us)
Async XLA Ops:
  6.5 274.8 %copy-start = (bf16[896,1024]{1,0:T(8,128)(2,1)S(1)}, bf16[896,1024]{1,0:T(8,128)(2,1)}, u32[]{:S(2)}) copy-start(bf16[896,1024]{1,0:T(8,128)(2,1)} %param.10) | copy-start | bytes 5505028
  6.5 80.3 %all-gather.2.cloned.1.call-start = ((), (), s32[]{:S(2)}) async-start(), calls=%async_computation.1 | async-start | bytes 2162688 | tf_op jit(solution)/shard_map/all_gather | solution.py:33
  7.3 274.0 %all-reduce.4.cloned.1.call-start = ((), (), s32[]{:S(2)}) async-start(), calls=%async_computation.3 | async-start | bytes 14680064 | tf_op jit(solution)/shard_map/psum | solution.py:60
  94.7 4.7 copy-start.1
  185.8 319.7 %reduce-scatter.2.cloned.1.call-start = ((), (), s32[]{:S(2)}) async-start(), calls=%async_computation.2 | async-start | bytes 4325376 | tf_op jit(solution)/shard_map/reduce_scatter | solution.py:62
Sparse Core Ops, SparseCore 0:
  10.0 76.8 all-gather.1
  185.9 95.3 all-reduce.3
  289.0 216.5 reduce-scatter.1
where the time goes:
time: 519 us; the launch traced here: 514 us
  waiting for transfers between devices  390 us (75%)
  blocking collectives  77.9 us (15%)
  matrix products  23.5 us (5%)
  between operations  13.2 us (3%)
  local copies, waits for them, and re-layouts  6.22 us (1%)
    reduce_scatter x1, waiting for transfers between devices, body(): lax.psum_scatter(jnp.dot(hidden, down_matrix, preferred_element_type=jnp....  217 us
    psum x1, waiting for transfers between devices, body(): gate_sum, up_sum = lax.psum((gate_part, up_part), 'narrow')  95.3 us
    psum x1, blocking collectives, body(): low = lax.psum(low_part, ('wide', 'narrow')).astype(jnp.bfloat16)  77.9 us
    all_gather x1, waiting for transfers between devices, body(): lax.all_gather(tokens, 'wide', axis=0, tiled=True)  77.3 us
  transfers between devices with their start and end apart: 3, of which 3 were waited for; matrix products, arithmetic and copies ran while one was open for 0% of the time, Pallas kernels for 0%

commit v1 on v0

v1 whole, which is shorter than its diff:
```python
import jax
import jax.numpy as jnp
from jax import lax
from jax.sharding import PartitionSpec as P

NX, NZ, NY, NC = 4, 8, 4, 2
F32, BF16 = jnp.float32, jnp.bfloat16


def x_shift(d):
    return [(x * NZ + z, (x + d) % NX * NZ + z) for x in range(NX) for z in range(NZ)]


def y_shift(d):
    return [(y * NC + c, (y + d) % NY * NC + c) for y in range(NY) for c in range(NC)]


def home_move(k):
    return [
        ((x * NZ + z) * 8 + y * NC + c, ((y + k) % NY * NZ + z) * 8 + x * NC + c)
        for x in range(NX)
        for z in range(NZ)
        for y in range(NY)
        for c in range(NC)
    ]


Z_GROUPS = [[x * NZ + z for z in range(NZ)] for x in range(NX)]
CORE_SWAP = [(i, i ^ 1) for i in range(NY * NC)]


def core(v):
    return lax.ppermute(v, "narrow", CORE_SWAP)


def block(v, i):
    return lax.dynamic_index_in_dim(v, i, 0, keepdims=False)


def roll(v, by):
    return lax.dynamic_slice_in_dim(jnp.concatenate([v, v], 0), by, v.shape[0], 0)


def dot(a, b):
    return jnp.dot(a, b, preferred_element_type=F32)


def body(tokens, gate, up, down, a, b, index):
    w, n = lax.axis_index("wide"), lax.axis_index("narrow")
    x, y, c = w // NZ, n // NC, n % NC
    width, hid = gate.shape
    rank = a.shape[2]
    own_a, own_b = a.shape[1], b.shape[0]
    half = tokens.shape[0] // 2
    rows = NZ * half

    near = lax.dynamic_slice_in_dim(tokens, c * half, half, 0)
    far = core(lax.dynamic_slice_in_dim(tokens, (1 - c) * half, half, 0))
    gate_s, up_s, b_s, down_s = core(gate), core(up), core(b), core(down)
    a2 = a.reshape(width, own_a * rank)
    a_s = core(a2)

    shard = jnp.concatenate([near, far], 1)
    t0 = lax.all_to_all(
        jnp.broadcast_to(shard, (NZ,) + shard.shape), "wide", 0, 0, tiled=True, axis_index_groups=Z_GROUPS
    ).reshape(rows, 2 * width)
    t = jnp.concatenate([t0] + [lax.ppermute(t0, "wide", x_shift(-d)) for d in (1, 2, 3)], 0)
    t_n, t_f = t[:, :width], t[:, width:]

    index_rel = roll(block(index.reshape(NX, NZ, 2, half).transpose(2, 0, 1, 3), c).reshape(NX, rows), x)
    flat = index_rel.reshape(NX * rows)

    shrink = (dot(t_n, a2) + dot(t_f, a_s)).reshape(NX * rows, own_a, rank)
    pick = (flat[:, None] == w * own_a + jnp.arange(own_a, dtype=jnp.int32)[None]).astype(F32)
    low_part = jnp.sum(shrink * pick[:, :, None], 1).reshape(NX, rows, rank)
    low = 0.0
    for k in range(NY):
        low = low + lax.ppermute(block(low_part, (y + k - x) % NX), ("wide", "narrow"), home_move(k))
    low = low.astype(BF16)
    low = lax.all_to_all(
        jnp.broadcast_to(low, (NX * NZ,) + low.shape), "wide", 0, 0, tiled=True
    ).reshape(NX, NZ, rows, rank)
    low = roll(jnp.sum(low.astype(F32), 1).astype(BF16), x).reshape(NX * rows, rank)

    def reduce_y(part):
        part = part.reshape(NY, rows, hid)
        total = block(part, y)
        for d in (1, 2, 3):
            total = total + lax.ppermute(block(part, (y + d) % NY).astype(BF16), "narrow", y_shift(d)).astype(F32)
        return total

    gate_sum = reduce_y(dot(t_n, gate) + dot(t_f, gate_s))
    up_part = dot(t_n, up) + dot(t_f, up_s)
    for home, table in ((n, b), (n ^ 1, b_s)):
        mask = (flat[:, None] == home * own_b + jnp.arange(own_b, dtype=jnp.int32)[None]).astype(BF16)
        spread = (mask[:, :, None] * low[:, None, :]).reshape(NX * rows, own_b * rank)
        up_part = up_part + dot(spread, table.reshape(own_b * rank, hid))
    up_sum = reduce_y(up_part)
    hidden = (jax.nn.silu(gate_sum) * up_sum).astype(BF16)

    parts = jnp.stack([hidden] + [lax.ppermute(hidden, "narrow", y_shift(-d)) for d in (1, 2, 3)])
    h = roll(parts, (NY - y) % NY).reshape(NX * rows, hid)
    mixed = jnp.concatenate([dot(h, down), dot(h, down_s)], 1).reshape(NX, rows, 2 * width)
    total = mixed[0]
    for d in (1, 2, 3):
        total = total + lax.ppermute(mixed[d].astype(BF16), "wide", x_shift(d)).astype(F32)
    total = lax.all_to_all(
        total.astype(BF16).reshape(NZ, half, 2 * width), "wide", 0, 0, tiled=True, axis_index_groups=Z_GROUPS
    )
    total = jnp.sum(total.astype(F32), 0).astype(BF16)
    mine, other = total[:, :width], core(total[:, width:])
    return jnp.where(c == 0, jnp.concatenate([mine, other], 0), jnp.concatenate([other, mine], 0))


def solution(mesh):
    placed = (
        P("wide", "narrow"),
        P("narrow", "wide"),
        P("narrow", "wide"),
        P("wide", "narrow"),
        P("narrow", "wide", None),
        P("narrow", None, "wide"),
        P(),
    )
    return jax.shard_map(body, mesh=mesh, in_specs=placed, out_specs=P("wide", "narrow"), check_vma=False)
```

time: 519 us -> 209 us (0.40)
  the two profiles are of different devices: /device:TPU:9 before, /device:TPU:1 now
where the time goes in v1:
time: 209 us; the launch traced here: 208 us
  waiting for transfers between devices  87.2 us (42%)
  starting transfers between devices  51.8 us (25%)
  matrix products  30.5 us (15%)
  blocking collectives  22.5 us (11%)
  local copies, waits for them, and re-layouts  11.2 us (5%)
  other arithmetic  4.52 us (2%)
    dot_general x10, matrix products, dot(): return jnp.dot(a, b, preferred_element_type=F32)  30.5 us
    ppermute x3, waiting for transfers between devices, body(): lax.ppermute(mixed[d].astype(BF16), 'wide', x_shift(d)).astype(F32)  25.5 us
    all_to_all x1, blocking collectives, body(): lax.all_to_all(total.astype(BF16).reshape(NZ, half, 2 * width), 'wide', 0...  22.5 us
    ppermute x3, waiting for transfers between devices, body(): lax.ppermute(t0, 'wide', x_shift(-d))  20.2 us
    all_to_all x1, waiting for transfers between devices, body(): lax.all_to_all(jnp.broadcast_to(shard, (NZ,) + shard.shape), 'wide', 0, 0...  17 us
    ppermute x3, waiting for transfers between devices, body(): lax.ppermute(hidden, 'narrow', y_shift(-d))  11.4 us
    ppermute x6, waiting for transfers between devices, reduce_y(): lax.ppermute(block(part, (y + d) % NY).astype(BF16), 'narrow', y_shift(d))  11.4 us
    ppermute x7, starting transfers between devices, core(): return lax.ppermute(v, 'narrow', CORE_SWAP)  11.2 us
  transfers between devices with their start and end apart: 28, of which 14 were waited for; matrix products, arithmetic and copies ran while one was open for 19% of the time, Pallas kernels for 0%

profile of v1, /device:TPU:1, one launch (start us, length us, event | category | flops | bytes accessed | tf_op | source)
XLA Modules:
  0.0 208.1 jit_solution(7004740010821175855)
XLA Ops:
  0.8 3.2 %collective-permute-start = (bf16[16,1024]{1,0:T(8,128)(2,1)S(1)}, bf16[16,1024]{1,0:T(8,128)(2,1)S(1)}, u32[]{:S(2)}, u32[]{:S(2)}) collective-permute-start(bf16[16,1024]{1,0:T(8,128)(2,1)S(1)} %get-tuple-element.23), channel_id=1, source_target_pairs={{0,1},{1,0},{2,3},{3,2},{4,5},{5,4},{6,7},{7,6},{8,9},{9,8},{10,11... | collective-permute-start | bytes 98312 | tf_op jit(solution)/shard_map/ppermute | solution.py:33
  4.0 0.9 collective-permute-done
  4.9 0.9 broadcast_in_dim.4
  5.8 6.4 %all-to-all-start = ((bf16[8,16,2048]{2,1,0:T(8,128)(2,1)}), bf16[8,16,2048]{2,1,0:T(8,128)(2,1)S(1)}, u32[]{:S(2)}, u32[]{:S(2)}) async-start(bf16[8,16,2048]{2,1,0:T(8,128)(2,1)} %broadcast_in_dim.4), calls=%async_computation | async-start | bytes 1048576 | tf_op jit(solution)/shard_map/all_to_all | solution.py:64
  13.2 17.0 %all-to-all-done = bf16[8,16,2048]{2,1,0:T(8,128)(2,1)S(1)} async-done(((bf16[8,16,2048]{2,1,0:T(8,128)(2,1)}), bf16[8,16,2048]{2,1,0:T(8,128)(2,1)S(1)}, u32[]{:S(2)}, u32[]{:S(2)}) %all-to-all-start) | async-done | bytes 524320 | tf_op jit(solution)/shard_map/all_to_all | solution.py:64
  30.2 1.2 collective-permute-start.3
  31.4 2.5 %collective-permute-start.2 = (bf16[128,2048]{1,0:T(8,128)(2,1)S(1)}, bf16[128,2048]{1,0:T(8,128)(2,1)S(1)}, u32[]{:S(2)}, u32[]{:S(2)}) collective-permute-start(bf16[128,2048]{1,0:T(8,128)(2,1)S(1)} %bitcast.89), channel_id=1, source_target_pairs={{0,128},{8,136},{16,144},{24,152},{32,160},{40,168},{48,176},{56,1... | collective-permute-start | bytes 1572872 | tf_op jit(solution)/shard_map/ppermute | solution.py:67
  33.8 1.2 collective-permute-start.1
  35.1 9.3 %collective-permute-done.3 = bf16[128,2048]{1,0:T(8,128)(2,1)S(1)} collective-permute-done((bf16[128,2048]{1,0:T(8,128)(2,1)S(1)}, bf16[128,2048]{1,0:T(8,128)(2,1)S(1)}, u32[]{:S(2)}, u32[]{:S(2)}) %collective-permute-start.3) | collective-permute-done | bytes 524320 | tf_op jit(solution)/shard_map/ppermute | solution.py:67
  44.4 1.3 collective-permute-start.14
  45.7 10.9 %collective-permute-done.2 = bf16[128,2048]{1,0:T(8,128)(2,1)S(1)} collective-permute-done((bf16[128,2048]{1,0:T(8,128)(2,1)S(1)}, bf16[128,2048]{1,0:T(8,128)(2,1)S(1)}, u32[]{:S(2)}, u32[]{:S(2)}) %collective-permute-start.2) | collective-permute-done | bytes 524320 | tf_op jit(solution)/shard_map/ppermute | solution.py:67
  56.6 1.3 collective-permute-start.4
  58.1 2.0 fusion.16
  60.1 2.0 convolution_add_fusion.1
  62.4 1.6 collective-permute-start.13
  63.9 3.8 %collective-permute-start.12 = (f32[128,64]{0,1:T(8,128)S(1)}, f32[128,64]{0,1:T(8,128)S(1)}, u32[]{:S(2)}, u32[]{:S(2)}) collective-permute-start(f32[128,64]{0,1:T(8,128)S(1)} %bitcast.98), channel_id=1, source_target_pairs={{0,128},{1,129},{2,192},{3,193},{4,0},{5,1},{6,64},{7,65},{8,136},... | collective-permute-start | bytes 98312 | tf_op jit(solution)/shard_map/ppermute | solution.py:78
  69.1 2.6 %collective-permute-start.11 = (f32[128,64]{0,1:T(8,128)S(1)}, f32[128,64]{0,1:T(8,128)S(1)}, u32[]{:S(2)}, u32[]{:S(2)}) collective-permute-start(f32[128,64]{0,1:T(8,128)S(1)} %bitcast.96), channel_id=1, source_target_pairs={{0,64},{1,65},{2,128},{3,129},{4,192},{5,193},{6,0},{7,1},{8,72},{... | collective-permute-start | bytes 98312 | tf_op jit(solution)/shard_map/ppermute | solution.py:78
  71.7 4.1 %fusion.23 = f32[512,896]{1,0:T(8,128)} fusion(bf16[1024,896]{1,0:T(8,128)(2,1)} %param.9, bf16[512,2048]{1,0:T(8,128)(2,1)S(1)} %pad_maximum_fusion.1), kind=kOutput, calls=%fused_computation.30 | convolution fusion | flops 939524096 | bytes 4718592 | tf_op jit(solution)/shard_map/dot_general | solution.py:45
  75.8 0.9 broadcast_in_dim.5
  76.7 9.2 %all-to-all-start.1 = ((bf16[32,128,64]{1,2,0:T(8,128)(2,1)}), bf16[32,128,64]{1,2,0:T(8,128)(2,1)S(1)}, u32[]{:S(2)}, u32[]{:S(2)}) async-start(bf16[32,128,64]{1,2,0:T(8,128)(2,1)} %broadcast_in_dim.5), calls=%async_computation.1 | async-start | bytes 1048576 | tf_op jit(solution)/shard_map/all_to_all | solution.py:80
  86.0 2.7 %fusion.20 = f32[512,896]{1,0:T(8,128)S(1)} fusion(bf16[1024,896]{1,0:T(8,128)(2,1)} %collective-permute-done.4, bf16[512,2048]{1,0:T(8,128)(2,1)S(1)} %pad_maximum_fusion.1), kind=kOutput, calls=%fused_computation.27 | convolution fusion | flops 939524096 | bytes 4718592 | tf_op jit(solution)/shard_map/dot_general | solution.py:45
  88.7 2.8 %convolution_add_fusion = f32[512,896]{1,0:T(8,128)S(1)} fusion(f32[512,896]{1,0:T(8,128)S(1)} %fusion.20, bf16[1024,896]{1,0:T(8,128)(2,1)} %param.8, bf16[512,2048]{1,0:T(8,128)(2,1)S(1)} %pad_maximum_fusion.1), kind=kOutput, calls=%fused_computation.11 | convolution fusion | flops 939982848 | bytes 6553600 | tf_op jit(solution)/shard_map/dot_general | solution.py:45
  91.5 1.0 fusion.32
  92.5 2.6 %collective-permute-start.6 = (bf16[128,896]{1,0:T(8,128)(2,1)}, bf16[128,896]{1,0:T(8,128)(2,1)S(1)}, u32[]{:S(2)}, u32[]{:S(2)}) collective-permute-start(bf16[128,896]{1,0:T(8,128)(2,1)} %get-tuple-element.12), channel_id=1, source_target_pairs={{0,4},{1,5},{2,6},{3,7},{4,0},{5,1},{6,2},{7,3},{8,12},{9,13},{10,... | collective-permute-start | bytes 688136 | tf_op jit(solution)/shard_map/ppermute | solution.py:89
  95.1 0.9 collective-permute-start.5
  95.9 4.0 %fusion.18 = f32[512,896]{1,0:T(8,128)} fusion(bf16[1024,896]{1,0:T(8,128)(2,1)} %collective-permute-done.8, bf16[512,2048]{1,0:T(8,128)(2,1)S(1)} %pad_maximum_fusion.1), kind=kOutput, calls=%fused_computation.25 | convolution fusion | flops 939524096 | bytes 4718592 | tf_op jit(solution)/shard_map/dot_general | solution.py:45
  100.1 4.6 %fusion.3 = f32[512,896,1]{1,0,2:T(8,128)S(1)} fusion(bf16[32,64,896]{2,1,0:T(8,128)(2,1)} %param.12, bf16[512,64]{0,1:T(8,128)(2,1)S(1)} %copy_bitcast_fusion, bf16[512,32]{0,1:T(8,128)(2,1)} %get-tuple-element.25), kind=kOutput, calls=%fused_computation.7 | convolution fusion | flops 1880096768 | bytes 5603328 | tf_op jit(solution)/shard_map/dot_general | solution.py:45
  104.7 4.4 %bitcast_add_fusion = f32[512,896]{1,0:T(8,128)S(1)} fusion(f32[512,896,1]{1,0,2:T(8,128)S(1)} %fusion.3, f32[512,896]{1,0:T(8,128)S(1)} %copy-done, f32[512,896]{1,0:T(8,128)S(1)} %copy-done.1, bf16[32,64,896]{2,1,0:T(8,128)(2,1)} %collective-permute-done.14, bf16[512,32]{0,1:T(8,128)(2,1)S(1)} %copy-done.3, bf16[512,64]{0,1:T(8,128)(2,1)S(1)} %copy_bitcast_fusion), kind=kOutput, calls=%fused_computation.9 | convolution fusion | flops 1881473024 | bytes 11108352 | tf_op jit(solution)/shard_map/dot_general | solution.py:45
  109.2 0.9 fusion.35
  110.0 1.8 collective-permute-start.17
  112.5 0.9 collective-permute-start.15
  113.3 4.6 %collective-permute-done.17 = bf16[128,896]{1,0:T(8,128)(2,1)S(1)} collective-permute-done((bf16[128,896]{1,0:T(8,128)(2,1)}, bf16[128,896]{1,0:T(8,128)(2,1)S(1)}, u32[]{:S(2)}, u32[]{:S(2)}) %collective-permute-start.17) | collective-permute-done | bytes 229408 | tf_op jit(solution)/shard_map/ppermute | solution.py:89
  118.5 6.2 %collective-permute-done.15 = bf16[128,896]{1,0:T(8,128)(2,1)S(1)} collective-permute-done((bf16[128,896]{1,0:T(8,128)(2,1)S(1)}, bf16[128,896]{1,0:T(8,128)(2,1)S(1)}, u32[]{:S(2)}, u32[]{:S(2)}) %collective-permute-start.15) | collective-permute-done | bytes 229408 | tf_op jit(solution)/shard_map/ppermute | solution.py:89
  124.7 2.0 bitcast_dynamic-update-slice_fusion.6
  126.7 2.4 %collective-permute-start.21 = (bf16[896,1024]{1,0:T(8,128)(2,1)}, bf16[896,1024]{1,0:T(8,128)(2,1)S(1)}, u32[]{:S(2)}, u32[]{:S(2)}) collective-permute-start(bf16[896,1024]{1,0:T(8,128)(2,1)} %param.10), channel_id=1, source_target_pairs={{0,1},{1,0},{2,3},{3,2},{4,5},{5,4},{6,7},{7,6},{8,9},{9,8},{10,11... | collective-permute-start | bytes 5505032 | tf_op jit(solution)/shard_map/ppermute | solution.py:33
  130.3 1.7 collective-permute-done.18
  132.7 5.2 %collective-permute-done.19 = bf16[128,896]{1,0:T(8,128)(2,1)S(1)} collective-permute-done((bf16[128,896]{1,0:T(8,128)(2,1)S(1)}, bf16[128,896]{1,0:T(8,128)(2,1)S(1)}, u32[]{:S(2)}, u32[]{:S(2)}) %collective-permute-start.19) | collective-permute-done | bytes 229408 | tf_op jit(solution)/shard_map/ppermute | solution.py:101
  138.6 4.5 %collective-permute-done.20 = bf16[128,896]{1,0:T(8,128)(2,1)S(1)} collective-permute-done((bf16[128,896]{1,0:T(8,128)(2,1)S(1)}, bf16[128,896]{1,0:T(8,128)(2,1)S(1)}, u32[]{:S(2)}, u32[]{:S(2)}) %collective-permute-start.20) | collective-permute-done | bytes 229408 | tf_op jit(solution)/shard_map/ppermute | solution.py:101
  146.7 1.3 constant_dynamic-slice_fusion
  147.9 2.8 %fusion.44 = f32[512,1024]{1,0:T(8,128)S(1)} fusion(bf16[512,896]{1,0:T(8,128)(2,1)S(1)} %bitcast.92, bf16[896,1024]{1,0:T(8,128)(2,1)} %param.10), kind=kOutput, calls=%fused_computation.89 | convolution fusion | flops 939524096 | bytes 4849664 | tf_op jit(solution)/shard_map/dot_general | solution.py:45
  150.7 1.3 fusion.45
  152.4 2.4 %collective-permute-start.24 = (bf16[128,2048]{1,0:T(8,128)(2,1)S(1)}, bf16[128,2048]{1,0:T(8,128)(2,1)S(1)}, u32[]{:S(2)}, u32[]{:S(2)}) collective-permute-start(bf16[128,2048]{1,0:T(8,128)(2,1)S(1)} %get-tuple-element.8), channel_id=1, source_target_pairs={{0,192},{8,200},{16,208},{24,216},{32,224},{40,232},{48,240},{56,2... | collective-permute-start | bytes 1572872 | tf_op jit(solution)/shard_map/ppermute | solution.py:106
  155.9 10.4 %collective-permute-done.24 = bf16[128,2048]{1,0:T(8,128)(2,1)S(1)} collective-permute-done((bf16[128,2048]{1,0:T(8,128)(2,1)S(1)}, bf16[128,2048]{1,0:T(8,128)(2,1)S(1)}, u32[]{:S(2)}, u32[]{:S(2)}) %collective-permute-start.24) | collective-permute-done | bytes 524320 | tf_op jit(solution)/shard_map/ppermute | solution.py:106
  166.3 2.8 %collective-permute-done.23 = bf16[128,2048]{1,0:T(8,128)(2,1)S(1)} collective-permute-done((bf16[128,2048]{1,0:T(8,128)(2,1)S(1)}, bf16[128,2048]{1,0:T(8,128)(2,1)S(1)}, u32[]{:S(2)}, u32[]{:S(2)}) %collective-permute-start.23) | collective-permute-done | bytes 524320 | tf_op jit(solution)/shard_map/ppermute | solution.py:106
  169.1 12.3 %collective-permute-done.22 = bf16[128,2048]{1,0:T(8,128)(2,1)S(1)} collective-permute-done((bf16[128,2048]{1,0:T(8,128)(2,1)S(1)}, bf16[128,2048]{1,0:T(8,128)(2,1)S(1)}, u32[]{:S(2)}, u32[]{:S(2)}) %collective-permute-start.22) | collective-permute-done | bytes 524320 | tf_op jit(solution)/shard_map/ppermute | solution.py:106
  181.7 22.5 %all_to_all.15 = bf16[8,16,2048]{2,1,0:T(8,128)(2,1)S(1)} all-to-all(bf16[8,16,2048]{2,1,0:T(8,128)(2,1)S(1)} %bitcast.87), channel_id=1, replica_groups={{0,8,16,24,32,40,48,56},{64,72,80,88,96,104,112,120},{128,136,144,152,1..., dimensions={0} | all-to-all | bytes 1048576 | tf_op jit(solution)/shard_map/all_to_all | solution.py:107
  204.3 2.2 %collective-permute-start.25 = (bf16[16,1024]{1,0:T(8,128)(2,1)S(1)}, bf16[16,1024]{1,0:T(8,128)(2,1)S(1)}, u32[]{:S(2)}, u32[]{:S(2)}) collective-permute-start(bf16[16,1024]{1,0:T(8,128)(2,1)S(1)} %get-tuple-element.21), channel_id=1, source_target_pairs={{0,1},{1,0},{2,3},{3,2},{4,5},{5,4},{6,7},{7,6},{8,9},{9,8},{10,11... | collective-permute-start | bytes 98312 | tf_op jit(solution)/shard_map/ppermute | solution.py:33
  206.5 0.9 collective-permute-done.25
  (66 shorter events, 13.9 us)
Async XLA Ops:
  0.0 12.9 %copy-start.4 = (s32[1024]{0:T(1024)S(1)}, s32[1024]{0:T(1024)}, u32[]{:S(2)}) copy-start(s32[1024]{0:T(1024)} %param.13) | copy-start | bytes 12292
  0.8 4.1 %collective-permute-start = (bf16[16,1024]{1,0:T(8,128)(2,1)S(1)}, bf16[16,1024]{1,0:T(8,128)(2,1)S(1)}, u32[]{:S(2)}, u32[]{:S(2)}) collective-permute-start(bf16[16,1024]{1,0:T(8,128)(2,1)S(1)} %get-tuple-element.23), channel_id=1, source_target_pairs={{0,1},{1,0},{2,3},{3,2},{4,5},{5,4},{6,7},{7,6},{8,9},{9,8},{10,11... | collective-permute-start | bytes 98312 | tf_op jit(solution)/shard_map/ppermute | solution.py:33
  5.8 24.4 %all-to-all-start = ((bf16[8,16,2048]{2,1,0:T(8,128)(2,1)}), bf16[8,16,2048]{2,1,0:T(8,128)(2,1)S(1)}, u32[]{:S(2)}, u32[]{:S(2)}) async-start(bf16[8,16,2048]{2,1,0:T(8,128)(2,1)} %broadcast_in_dim.4), calls=%async_computation | async-start | bytes 1048576 | tf_op jit(solution)/shard_map/all_to_all | solution.py:64
  12.2 45.9 %collective-permute-start.9 = (bf16[1024,512]{0,1:T(8,128)(2,1)}, bf16[1024,512]{0,1:T(8,128)(2,1)}, u32[]{:S(2)}, u32[]{:S(2)}) collective-permute-start(bf16[1024,512]{0,1:T(8,128)(2,1)} %bitcast.7), channel_id=1, source_target_pairs={{0,1},{1,0},{2,3},{3,2},{4,5},{5,4},{6,7},{7,6},{8,9},{9,8},{10,11... | collective-permute-start | bytes 3145736 | tf_op jit(solution)/shard_map/ppermute | solution.py:33
  12.8 83.1 %collective-permute-start.8 = (bf16[1024,896]{1,0:T(8,128)(2,1)}, bf16[1024,896]{1,0:T(8,128)(2,1)}, u32[]{:S(2)}, u32[]{:S(2)}) collective-permute-start(bf16[1024,896]{1,0:T(8,128)(2,1)} %param.9), channel_id=1, source_target_pairs={{0,1},{1,0},{2,3},{3,2},{4,5},{5,4},{6,7},{7,6},{8,9},{9,8},{10,11... | collective-permute-start | bytes 5505032 | tf_op jit(solution)/shard_map/ppermute | solution.py:33
  30.2 14.2 %collective-permute-start.3 = (bf16[128,2048]{1,0:T(8,128)(2,1)S(1)}, bf16[128,2048]{1,0:T(8,128)(2,1)S(1)}, u32[]{:S(2)}, u32[]{:S(2)}) collective-permute-start(bf16[128,2048]{1,0:T(8,128)(2,1)S(1)} %bitcast.88), channel_id=1, source_target_pairs={{0,64},{8,72},{16,80},{24,88},{32,96},{40,104},{48,112},{56,120},{... | collective-permute-start | bytes 1572872 | tf_op jit(solution)/shard_map/ppermute | solution.py:67
  31.4 25.2 %collective-permute-start.2 = (bf16[128,2048]{1,0:T(8,128)(2,1)S(1)}, bf16[128,2048]{1,0:T(8,128)(2,1)S(1)}, u32[]{:S(2)}, u32[]{:S(2)}) collective-permute-start(bf16[128,2048]{1,0:T(8,128)(2,1)S(1)} %bitcast.89), channel_id=1, source_target_pairs={{0,128},{8,136},{16,144},{24,152},{32,160},{40,168},{48,176},{56,1... | collective-permute-start | bytes 1572872 | tf_op jit(solution)/shard_map/ppermute | solution.py:67
  33.8 24.1 %collective-permute-start.1 = (bf16[128,2048]{1,0:T(8,128)(2,1)S(1)}, bf16[128,2048]{1,0:T(8,128)(2,1)S(1)}, u32[]{:S(2)}, u32[]{:S(2)}) collective-permute-start(bf16[128,2048]{1,0:T(8,128)(2,1)S(1)} %bitcast.90), channel_id=1, source_target_pairs={{0,192},{8,200},{16,208},{24,216},{32,224},{40,232},{48,240},{56,2... | collective-permute-start | bytes 1572872 | tf_op jit(solution)/shard_map/ppermute | solution.py:67
  44.4 60.3 %collective-permute-start.14 = (bf16[32,64,896]{2,1,0:T(8,128)(2,1)}, bf16[32,64,896]{2,1,0:T(8,128)(2,1)}, u32[]{:S(2)}, u32[]{:S(2)}) collective-permute-start(bf16[32,64,896]{2,1,0:T(8,128)(2,1)} %param.12), channel_id=1, source_target_pairs={{0,1},{1,0},{2,3},{3,2},{4,5},{5,4},{6,7},{7,6},{8,9},{9,8},{10,11... | collective-permute-start | bytes 11010056 | tf_op jit(solution)/shard_map/ppermute | solution.py:33
  56.6 29.4 %collective-permute-start.4 = (bf16[1024,896]{1,0:T(8,128)(2,1)}, bf16[1024,896]{1,0:T(8,128)(2,1)}, u32[]{:S(2)}, u32[]{:S(2)}) collective-permute-start(bf16[1024,896]{1,0:T(8,128)(2,1)} %param.8), channel_id=1, source_target_pairs={{0,1},{1,0},{2,3},{3,2},{4,5},{5,4},{6,7},{7,6},{8,9},{9,8},{10,11... | collective-permute-start | bytes 5505032 | tf_op jit(solution)/shard_map/ppermute | solution.py:33
  62.4 6.1 %collective-permute-start.13 = (f32[128,64]{0,1:T(8,128)S(1)}, f32[128,64]{0,1:T(8,128)S(1)}, u32[]{:S(2)}, u32[]{:S(2)}) collective-permute-start(f32[128,64]{0,1:T(8,128)S(1)} %bitcast.99), channel_id=1, source_target_pairs={{0,192},{1,193},{2,0},{3,1},{4,64},{5,65},{6,128},{7,129},{8,200},... | collective-permute-start | bytes 98312 | tf_op jit(solution)/shard_map/ppermute | solution.py:78
  63.9 5.2 %collective-permute-start.12 = (f32[128,64]{0,1:T(8,128)S(1)}, f32[128,64]{0,1:T(8,128)S(1)}, u32[]{:S(2)}, u32[]{:S(2)}) collective-permute-start(f32[128,64]{0,1:T(8,128)S(1)} %bitcast.98), channel_id=1, source_target_pairs={{0,128},{1,129},{2,192},{3,193},{4,0},{5,1},{6,64},{7,65},{8,136},... | collective-permute-start | bytes 98312 | tf_op jit(solution)/shard_map/ppermute | solution.py:78
  68.5 7.3 %collective-permute-start.10 = (f32[128,64]{0,1:T(8,128)S(1)}, f32[128,64]{0,1:T(8,128)S(1)}, u32[]{:S(2)}, u32[]{:S(2)}) collective-permute-start(f32[128,64]{0,1:T(8,128)S(1)} %bitcast.97), channel_id=1, source_target_pairs={{0,0},{1,1},{2,64},{3,65},{4,128},{5,129},{6,192},{7,193},{8,8},{9... | collective-permute-start | bytes 98312 | tf_op jit(solution)/shard_map/ppermute | solution.py:78
  69.1 6.7 %collective-permute-start.11 = (f32[128,64]{0,1:T(8,128)S(1)}, f32[128,64]{0,1:T(8,128)S(1)}, u32[]{:S(2)}, u32[]{:S(2)}) collective-permute-start(f32[128,64]{0,1:T(8,128)S(1)} %bitcast.96), channel_id=1, source_target_pairs={{0,64},{1,65},{2,128},{3,129},{4,192},{5,193},{6,0},{7,1},{8,72},{... | collective-permute-start | bytes 98312 | tf_op jit(solution)/shard_map/ppermute | solution.py:78
  76.7 23.2 %all-to-all-start.1 = ((bf16[32,128,64]{1,2,0:T(8,128)(2,1)}), bf16[32,128,64]{1,2,0:T(8,128)(2,1)S(1)}, u32[]{:S(2)}, u32[]{:S(2)}) async-start(bf16[32,128,64]{1,2,0:T(8,128)(2,1)} %broadcast_in_dim.5), calls=%async_computation.1 | async-start | bytes 1048576 | tf_op jit(solution)/shard_map/all_to_all | solution.py:80
  91.5 4.5 %copy-start.2 = (f32[512,896]{1,0:T(8,128)}, f32[512,896]{1,0:T(8,128)S(1)}, u32[]{:S(2)}) copy-start(f32[512,896]{1,0:T(8,128)S(1)} %convolution_add_fusion) | copy-start | bytes 5505028
  92.5 20.0 %collective-permute-start.7 = (bf16[128,896]{1,0:T(8,128)(2,1)S(1)}, bf16[128,896]{1,0:T(8,128)(2,1)S(1)}, u32[]{:S(2)}, u32[]{:S(2)}) collective-permute-start(bf16[128,896]{1,0:T(8,128)(2,1)S(1)} %get-tuple-element.11), channel_id=1, source_target_pairs={{0,6},{1,7},{2,0},{3,1},{4,2},{5,3},{6,4},{7,5},{8,14},{9,15},{10,... | collective-permute-start | bytes 688136 | tf_op jit(solution)/shard_map/ppermute | solution.py:89
  92.5 20.9 %collective-permute-start.6 = (bf16[128,896]{1,0:T(8,128)(2,1)}, bf16[128,896]{1,0:T(8,128)(2,1)S(1)}, u32[]{:S(2)}, u32[]{:S(2)}) collective-permute-start(bf16[128,896]{1,0:T(8,128)(2,1)} %get-tuple-element.12), channel_id=1, source_target_pairs={{0,4},{1,5},{2,6},{3,7},{4,0},{5,1},{6,2},{7,3},{8,12},{9,13},{10,... | collective-permute-start | bytes 688136 | tf_op jit(solution)/shard_map/ppermute | solution.py:89
  95.1 18.3 %collective-permute-start.5 = (bf16[128,896]{1,0:T(8,128)(2,1)}, bf16[128,896]{1,0:T(8,128)(2,1)S(1)}, u32[]{:S(2)}, u32[]{:S(2)}) collective-permute-start(bf16[128,896]{1,0:T(8,128)(2,1)} %get-tuple-element.10), channel_id=1, source_target_pairs={{0,2},{1,3},{2,4},{3,5},{4,6},{5,7},{6,0},{7,1},{8,10},{9,11},{10,... | collective-permute-start | bytes 688136 | tf_op jit(solution)/shard_map/ppermute | solution.py:89
  100.1 4.6 %copy-start = (f32[512,896]{1,0:T(8,128)S(1)}, f32[512,896]{1,0:T(8,128)}, u32[]{:S(2)}) copy-start(f32[512,896]{1,0:T(8,128)} %fusion.23) | copy-start | bytes 5505028
  100.1 4.6 %copy-start.1 = (f32[512,896]{1,0:T(8,128)S(1)}, f32[512,896]{1,0:T(8,128)}, u32[]{:S(2)}) copy-start(f32[512,896]{1,0:T(8,128)} %fusion.18) | copy-start | bytes 5505028
  100.1 4.6 %copy-start.3 = (bf16[512,32]{0,1:T(8,128)(2,1)S(1)}, bf16[512,32]{0,1:T(8,128)(2,1)}, u32[]{:S(2)}) copy-start(bf16[512,32]{0,1:T(8,128)(2,1)} %get-tuple-element.24) | copy-start | bytes 98308
  110.0 7.9 %collective-permute-start.17 = (bf16[128,896]{1,0:T(8,128)(2,1)}, bf16[128,896]{1,0:T(8,128)(2,1)S(1)}, u32[]{:S(2)}, u32[]{:S(2)}) collective-permute-start(bf16[128,896]{1,0:T(8,128)(2,1)} %get-tuple-element.14), channel_id=1, source_target_pairs={{0,6},{1,7},{2,0},{3,1},{4,2},{5,3},{6,4},{7,5},{8,14},{9,15},{10,... | collective-permute-start | bytes 688136 | tf_op jit(solution)/shard_map/ppermute | solution.py:89
  111.8 6.7 %collective-permute-start.16 = (bf16[128,896]{1,0:T(8,128)(2,1)}, bf16[128,896]{1,0:T(8,128)(2,1)S(1)}, u32[]{:S(2)}, u32[]{:S(2)}) collective-permute-start(bf16[128,896]{1,0:T(8,128)(2,1)} %get-tuple-element.15), channel_id=1, source_target_pairs={{0,4},{1,5},{2,6},{3,7},{4,0},{5,1},{6,2},{7,3},{8,12},{9,13},{10,... | collective-permute-start | bytes 688136 | tf_op jit(solution)/shard_map/ppermute | solution.py:89
  112.5 12.2 %collective-permute-start.15 = (bf16[128,896]{1,0:T(8,128)(2,1)S(1)}, bf16[128,896]{1,0:T(8,128)(2,1)S(1)}, u32[]{:S(2)}, u32[]{:S(2)}) collective-permute-start(bf16[128,896]{1,0:T(8,128)(2,1)S(1)} %get-tuple-element.13), channel_id=1, source_target_pairs={{0,2},{1,3},{2,4},{3,5},{4,6},{5,7},{6,0},{7,1},{8,10},{9,11},{10,... | collective-permute-start | bytes 688136 | tf_op jit(solution)/shard_map/ppermute | solution.py:89
  126.7 5.3 %collective-permute-start.18 = (bf16[128,896]{1,0:T(8,128)(2,1)S(1)}, bf16[128,896]{1,0:T(8,128)(2,1)S(1)}, u32[]{:S(2)}, u32[]{:S(2)}) collective-permute-start(bf16[128,896]{1,0:T(8,128)(2,1)S(1)} %get-tuple-element.6), channel_id=1, source_target_pairs={{0,6},{1,7},{2,0},{3,1},{4,2},{5,3},{6,4},{7,5},{8,14},{9,15},{10,... | collective-permute-start | bytes 688136 | tf_op jit(solution)/shard_map/ppermute | solution.py:101
  126.7 24.0 %collective-permute-start.21 = (bf16[896,1024]{1,0:T(8,128)(2,1)}, bf16[896,1024]{1,0:T(8,128)(2,1)S(1)}, u32[]{:S(2)}, u32[]{:S(2)}) collective-permute-start(bf16[896,1024]{1,0:T(8,128)(2,1)} %param.10), channel_id=1, source_target_pairs={{0,1},{1,0},{2,3},{3,2},{4,5},{5,4},{6,7},{7,6},{8,9},{9,8},{10,11... | collective-permute-start | bytes 5505032 | tf_op jit(solution)/shard_map/ppermute | solution.py:33
  129.1 8.8 %collective-permute-start.19 = (bf16[128,896]{1,0:T(8,128)(2,1)S(1)}, bf16[128,896]{1,0:T(8,128)(2,1)S(1)}, u32[]{:S(2)}, u32[]{:S(2)}) collective-permute-start(bf16[128,896]{1,0:T(8,128)(2,1)S(1)} %get-tuple-element.6), channel_id=1, source_target_pairs={{0,4},{1,5},{2,6},{3,7},{4,0},{5,1},{6,2},{7,3},{8,12},{9,13},{10,... | collective-permute-start | bytes 688136 | tf_op jit(solution)/shard_map/ppermute | solution.py:101
  129.8 13.3 %collective-permute-start.20 = (bf16[128,896]{1,0:T(8,128)(2,1)S(1)}, bf16[128,896]{1,0:T(8,128)(2,1)S(1)}, u32[]{:S(2)}, u32[]{:S(2)}) collective-permute-start(bf16[128,896]{1,0:T(8,128)(2,1)S(1)} %get-tuple-element.6), channel_id=1, source_target_pairs={{0,2},{1,3},{2,4},{3,5},{4,6},{5,7},{6,0},{7,1},{8,10},{9,11},{10,... | collective-permute-start | bytes 688136 | tf_op jit(solution)/shard_map/ppermute | solution.py:101
  152.4 13.9 %collective-permute-start.24 = (bf16[128,2048]{1,0:T(8,128)(2,1)S(1)}, bf16[128,2048]{1,0:T(8,128)(2,1)S(1)}, u32[]{:S(2)}, u32[]{:S(2)}) collective-permute-start(bf16[128,2048]{1,0:T(8,128)(2,1)S(1)} %get-tuple-element.8), channel_id=1, source_target_pairs={{0,192},{8,200},{16,208},{24,216},{32,224},{40,232},{48,240},{56,2... | collective-permute-start | bytes 1572872 | tf_op jit(solution)/shard_map/ppermute | solution.py:106
  154.8 14.3 %collective-permute-start.23 = (bf16[128,2048]{1,0:T(8,128)(2,1)S(1)}, bf16[128,2048]{1,0:T(8,128)(2,1)S(1)}, u32[]{:S(2)}, u32[]{:S(2)}) collective-permute-start(bf16[128,2048]{1,0:T(8,128)(2,1)S(1)} %get-tuple-element.9), channel_id=1, source_target_pairs={{0,128},{8,136},{16,144},{24,152},{32,160},{40,168},{48,176},{56,1... | collective-permute-start | bytes 1572872 | tf_op jit(solution)/shard_map/ppermute | solution.py:106
  155.3 26.1 %collective-permute-start.22 = (bf16[128,2048]{1,0:T(8,128)(2,1)S(1)}, bf16[128,2048]{1,0:T(8,128)(2,1)S(1)}, u32[]{:S(2)}, u32[]{:S(2)}) collective-permute-start(bf16[128,2048]{1,0:T(8,128)(2,1)S(1)} %get-tuple-element.7), channel_id=1, source_target_pairs={{0,64},{8,72},{16,80},{24,88},{32,96},{40,104},{48,112},{56,120},{... | collective-permute-start | bytes 1572872 | tf_op jit(solution)/shard_map/ppermute | solution.py:106
  204.3 3.1 %collective-permute-start.25 = (bf16[16,1024]{1,0:T(8,128)(2,1)S(1)}, bf16[16,1024]{1,0:T(8,128)(2,1)S(1)}, u32[]{:S(2)}, u32[]{:S(2)}) collective-permute-start(bf16[16,1024]{1,0:T(8,128)(2,1)S(1)} %get-tuple-element.21), channel_id=1, source_target_pairs={{0,1},{1,0},{2,3},{3,2},{4,5},{5,4},{6,7},{7,6},{8,9},{9,8},{10,11... | collective-permute-start | bytes 98312 | tf_op jit(solution)/shard_map/ppermute | solution.py:33

commit v2 on v1

v2 whole, which is shorter than its diff:
```python
import functools

import jax
import jax.numpy as jnp
from jax import lax
from jax.experimental import pallas as pl
from jax.experimental.pallas import tpu as pltpu
from jax.sharding import PartitionSpec as P

NX, NZ, NY, NC = 4, 8, 4, 2
F32, BF16 = jnp.float32, jnp.bfloat16
VMEM_LIMIT = 60 * 1024 * 1024


def device(x, z, y, c):
    return (x % NX * NZ + z % NZ) * NY * NC + y % NY * NC + c


def send_x(v, d):
    return lax.ppermute(v, "wide", [(x * NZ + z, (x + d) % NX * NZ + z) for x in range(NX) for z in range(NZ)])


def send_z(v, d):
    return lax.ppermute(v, "wide", [(x * NZ + z, x * NZ + (z + d) % NZ) for x in range(NX) for z in range(NZ)])


def send_y(v, d):
    return lax.ppermute(v, "narrow", [(y * NC + c, (y + d) % NY * NC + c) for y in range(NY) for c in range(NC)])


def send_pair(v):
    return lax.ppermute(v, "wide", [(i, i ^ 1) for i in range(NX * NZ)])


def send_home(v):
    cells = [(x, z, y, c) for x in range(NX) for z in range(NZ) for y in range(NY) for c in range(NC)]
    moves = [(device(x, z, y, c), device(y, z, x, c)) for x, z, y, c in cells]
    return lax.ppermute(v, ("wide", "narrow"), moves)


def core(v):
    return lax.ppermute(v, "narrow", [(i, i ^ 1) for i in range(NY * NC)])


Y_GROUPS = [[y * NC + c for y in range(NY)] for c in range(NC)]


def dot(a, b):
    return jnp.dot(a, b, preferred_element_type=F32)


SMEM = pl.BlockSpec(memory_space=pltpu.SMEM)
VMEM = pl.BlockSpec(memory_space=pltpu.VMEM)


def params():
    return pltpu.CompilerParams(vmem_limit_bytes=VMEM_LIMIT)


def together(*v):
    return lax.optimization_barrier(v)


def pick_kernel(place, q0, q1, q2, q3, keep, give):
    c = place[3]
    half = q0.shape[0] // 2
    for k, ref in enumerate((q0, q1, q2, q3)):
        at = slice(k * half, (k + 1) * half)
        keep[at, :] = ref[pl.ds(pl.multiple_of(c * half, half), half), :]
        give[at, :] = ref[pl.ds(pl.multiple_of((1 - c) * half, half), half), :]


def shrink_kernel(own, rank, place, index, p0, p1, p2, p3, q0, q1, a_n, a_f, t, low):
    x, z, first = place[0], place[1], place[4]
    half = t.shape[0] // (NX * NZ)
    width = a_n.shape[0]
    quads = NZ // 2

    def put(ref, at, dx, pair, k, columns):
        from_z = ((z ^ pair) + 2 * k) % NZ
        row = pl.multiple_of(((x + dx) % NX * NZ + from_z) * half, half)
        t[pl.ds(row, half), columns] = ref[at * half : (at + 1) * half, :]

    for dx, ref in enumerate((p0, p1, p2, p3)):
        for pair in range(2):
            for k in range(quads):
                put(ref, pair * quads + k, dx, pair, k, slice(0, width))
    for pair, ref in enumerate((q0, q1)):
        for dx in range(NX):
            for k in range(quads):
                put(ref, dx * quads + k, dx, pair, k, slice(width, 2 * width))
    s = dot(t[:, :width], a_n[...]) + dot(t[:, width:], a_f[...])
    total = jnp.zeros((t.shape[0], rank), F32)
    for k in range(own):
        total = jnp.where(index[...] == first + k, s[:, k * rank : (k + 1) * rank], total)
    total = total.reshape(NX, NZ * half, rank)
    some = NZ * half // 2
    low[...] = jnp.concatenate([total[:, :some], total[:, some:]], 2)


def gate_kernel(place, t, w_n, w_f, mine, o1, o2, o3):
    y = place[2]
    rows, width = mine.shape[0], w_n.shape[0]
    for e, ref in enumerate((mine, o1, o2, o3)):
        at = pl.ds(pl.multiple_of((y + e) % NY * rows, rows), rows)
        part = dot(t[at, :width], w_n[...]) + dot(t[at, width:], w_f[...])
        ref[...] = part.astype(ref.dtype)


def base_kernel(t, w_n, w_f, up):
    width = w_n.shape[0]
    up[...] = dot(t[:, :width], w_n[...]) + dot(t[:, width:], w_f[...])


def up_kernel(rank, place, index, low, up, b_n, b_f, mine, o1, o2, o3, total, wide_low):
    k, y = pl.program_id(0), place[2]
    step = b_n.shape[0]
    count = step // rank
    rows = mine.shape[0]

    @pl.when(k == 0)
    def _():
        v = jnp.sum(low[...].astype(F32).reshape(NX, NZ, rows // 2, 2 * rank), 1)
        v = jnp.concatenate([v[:, :, :rank], v[:, :, rank:]], 1).reshape(NX * rows, rank)
        wide_low[...] = jnp.concatenate([v] * count, 1)
        total[...] = up[...]

    group = (lax.broadcasted_iota(jnp.int32, (NX * rows, step), 1) >> (rank.bit_length() - 1)) + k * count
    own = index[...] - place[5]
    far = index[...] - place[6]
    spread_n = jnp.where(own == group, wide_low[...], 0.0).astype(BF16)
    spread_f = jnp.where(far == group, wide_low[...], 0.0).astype(BF16)
    total[...] += dot(spread_n, b_n[...]) + dot(spread_f, b_f[...])

    @pl.when(k == pl.num_programs(0) - 1)
    def _():
        for e, ref in enumerate((mine, o1, o2, o3)):
            at = pl.ds(pl.multiple_of((y + e) % NY * rows, rows), rows)
            ref[...] = total[at, :].astype(ref.dtype)


def mix_kernel(place, h0, h1, h2, h3, d_n, d_f, near0, near1, near2, near3, far0, far1, h):
    x, z, y = place[0], place[1], place[2]
    half = h0.shape[0] // NZ
    quads = NZ // 2
    for e, ref in enumerate((h0, h1, h2, h3)):
        dx = (y + e - x + NX) % NX
        for pair in range(2):
            for k in range(quads):
                to_z = ((z ^ pair) + 2 * k) % NZ
                to = pl.multiple_of(((dx * 2 + pair) * quads + k) * half, half)
                h[pl.ds(to, half), :] = ref[pl.ds(pl.multiple_of(to_z * half, half), half), :]
    rows = NZ * half
    near = dot(h[...], d_n[...])
    for dx, ref in enumerate((near0, near1, near2, near3)):
        ref[...] = near[dx * rows : (dx + 1) * rows].astype(ref.dtype)
    far = dot(h[...], d_f[...])
    some = rows // 2
    for dx in range(NX):
        for pair, ref in enumerate((far0, far1)):
            at = (dx * 2 + pair) * some
            ref[dx * some : (dx + 1) * some, :] = far[at : at + some].astype(ref.dtype)


def body(tokens, gate, up, down, a, b, index):
    w, n = lax.axis_index("wide"), lax.axis_index("narrow")
    x, z, y, c = w // NZ, w % NZ, n // NC, n % NC
    width, hid = gate.shape
    own_a, rank, own_b = a.shape[1], a.shape[2], b.shape[0]
    half = tokens.shape[0] // 2
    rows = NZ * half
    everyone = NX * rows
    shape = jax.ShapeDtypeStruct

    a_n = a.reshape(width, own_a * rank)
    b_n = b.reshape(own_b * rank, hid)
    place = jnp.stack([x, z, y, c, w * own_a, n * own_b, (n ^ 1) * own_b]).astype(jnp.int32)
    column = lax.dynamic_index_in_dim(index.reshape(NX * NZ, 2, half), c, 1, keepdims=False).reshape(everyone, 1)

    *quad, b_f, gate_f, place, column = together(
        *[send_z(tokens, -2 * k) for k in (1, 2, 3)], core(b_n), core(gate), place, column
    )
    near, far = pl.pallas_call(
        pick_kernel,
        out_shape=(shape((rows // 2, width), BF16),) * 2,
        in_specs=[SMEM] + [VMEM] * 4,
        out_specs=(VMEM,) * 2,
        compiler_params=params(),
        name="pick",
    )(place, tokens, *quad)
    a_n, far, near = together(a_n, far, near)
    far, a_f, up = together(core(far), core(a_n), up)
    pair, *fars, up_f = together(send_pair(near), *[send_x(far, -d) for d in (1, 2, 3)], core(up))
    down, near, pair = together(down, near, pair)
    near = jnp.concatenate([near, pair], 0)
    far = jnp.concatenate([far] + fars, 0)
    *pieces, down_f = together(near, *[send_x(near, -d) for d in (1, 2, 3)], far, send_pair(far), core(down))
    t, low = pl.pallas_call(
        functools.partial(shrink_kernel, own_a, rank),
        out_shape=(shape((everyone, 2 * width), BF16),) + (shape((NX, rows // 2, 2 * rank), F32),),
        in_specs=[SMEM] + [VMEM] * 9,
        out_specs=(VMEM,) * 2,
        compiler_params=params(),
        name="shrink",
    )(place, column, *pieces, a_n, a_f)

    blocks = (shape((rows, hid), F32),) + (shape((rows, hid), BF16),) * 3

    def reduce_y(mine, *others):
        for e, part in enumerate(others, 1):
            mine = mine + send_y(part, e).astype(F32)
        return mine

    gates = pl.pallas_call(
        gate_kernel,
        out_shape=blocks,
        in_specs=[SMEM] + [VMEM] * 3,
        out_specs=(VMEM,) * 4,
        compiler_params=params(),
        name="gate",
    )(place, t, gate, gate_f)

    low, *gates = together(
        lax.all_to_all(low, "narrow", 0, 0, tiled=True, axis_index_groups=Y_GROUPS), *gates
    )
    low, t, *gates = together(send_home(jnp.sum(low, 0).astype(BF16)), t, *gates)
    low = lax.all_to_all(jnp.broadcast_to(low, (NX * NZ,) + low.shape), "wide", 0, 0, tiled=True)

    up_part = pl.pallas_call(
        base_kernel,
        out_shape=shape((everyone, hid), F32),
        in_specs=[VMEM] * 3,
        out_specs=VMEM,
        compiler_params=params(),
        name="base",
    )(t, up, up_f)
    gate_sum = reduce_y(*gates)
    steps = 4
    part = pl.BlockSpec((own_b * rank // steps, hid), lambda k: (k, 0))
    fixed = lambda *dims: pl.BlockSpec(dims, lambda k: (0,) * len(dims))
    up_sum = reduce_y(
        *pl.pallas_call(
            functools.partial(up_kernel, rank),
            out_shape=blocks,
            grid=(steps,),
            in_specs=[SMEM, fixed(everyone, 1), fixed(*low.shape), fixed(everyone, hid), part, part],
            out_specs=(fixed(rows, hid),) * 4,
            scratch_shapes=[pltpu.VMEM((everyone, hid), F32), pltpu.VMEM((everyone, own_b * rank // steps), F32)],
            compiler_params=params(),
            name="up",
        )(place, column, low, up_part, b_n, b_f)
    )
    hidden = (jax.nn.silu(gate_sum) * up_sum).astype(BF16)

    some = everyone // 2
    near, n1, n2, n3, far, f1 = pl.pallas_call(
        mix_kernel,
        out_shape=(shape((rows, width), F32),)
        + (shape((rows, width), BF16),) * 3
        + (shape((some, width), F32), shape((some, width), BF16)),
        in_specs=[SMEM] + [VMEM] * 6,
        out_specs=(VMEM,) * 6,
        scratch_shapes=[pltpu.VMEM((everyone, hid), BF16)],
        compiler_params=params(),
        name="mix",
    )(place, hidden, *[send_y(hidden, -e) for e in (1, 2, 3)], down, down_f)
    n1, n2, n3, f1 = together(send_x(n1, 1), send_x(n2, 2), send_x(n3, 3), send_pair(f1))
    near = near + n1.astype(F32) + n2.astype(F32) + n3.astype(F32)
    far = (far + f1.astype(F32)).reshape(NX, rows // 2, width)
    n1, f1, f2, f3 = together(
        send_pair(near[rows // 2 :].astype(BF16)), *[send_x(far[d].astype(BF16), d) for d in (1, 2, 3)]
    )
    near = near[: rows // 2] + n1.astype(F32)
    far = far[0] + f1.astype(F32) + f2.astype(F32) + f3.astype(F32)
    both = jnp.concatenate([near, far], 1).reshape(NZ // 2, half, 2 * width)
    total = both[0]
    for v in together(*[send_z(both[k].astype(BF16), 2 * k) for k in (1, 2, 3)]):
        total = total + v.astype(F32)
    total = total.astype(BF16)
    mine, other = total[:, :width], core(total[:, width:])
    return jnp.where(c == 0, jnp.concatenate([mine, other], 0), jnp.concatenate([other, mine], 0))


def solution(mesh):
    placed = (
        P("wide", "narrow"),
        P("narrow", "wide"),
        P("narrow", "wide"),
        P("wide", "narrow"),
        P("narrow", "wide", None),
        P("narrow", None, "wide"),
        P(),
    )
    return jax.shard_map(body, mesh=mesh, in_specs=placed, out_specs=P("wide", "narrow"), check_vma=False)
```

time: 209 us -> 190 us (0.909)
  the two profiles are of different devices: /device:TPU:1 before, /device:TPU:9 now
where the time goes in v2:
time: 190 us; the launch traced here: 189 us
  starting transfers between devices  81.7 us (43%)
  waiting for transfers between devices  61.7 us (32%)
  Pallas kernels  33.9 us (18%)
  local copies, waits for them, and re-layouts  8.35 us (4%)
  other arithmetic  3.5 us (2%)
    ppermute x12, waiting for transfers between devices, send_x(): lax.ppermute(v, 'wide', [(x * NZ + z, (x + d) % NX * NZ + z) for x in ran...  30.2 us
    ppermute x12, starting transfers between devices, send_x(): lax.ppermute(v, 'wide', [(x * NZ + z, (x + d) % NX * NZ + z) for x in ran...  23.8 us
    ppermute x6, starting transfers between devices, send_z(): lax.ppermute(v, 'wide', [(x * NZ + z, x * NZ + (z + d) % NZ) for x in ran...  18.1 us
    ppermute x9, waiting for transfers between devices, send_y(): lax.ppermute(v, 'narrow', [(y * NC + c, (y + d) % NY * NC + c) for y in r...  12.9 us
    all_to_all x1, starting transfers between devices, body(): lax.all_to_all(jnp.broadcast_to(low, (NX * NZ,) + low.shape), 'wide', 0,...  12.2 us
    ppermute x6, waiting for transfers between devices, send_z(): lax.ppermute(v, 'wide', [(x * NZ + z, x * NZ + (z + d) % NZ) for x in ran...  9.82 us
    pallas_call x1, Pallas kernels, body(): pl.pallas_call(functools.partial(up_kernel, rank), out_shape=blocks, grid...  9.23 us
    ppermute x9, starting transfers between devices, send_y(): lax.ppermute(v, 'narrow', [(y * NC + c, (y + d) % NY * NC + c) for y in r...  8 us
  transfers between devices with their start and end apart: 41, of which 23 were waited for; matrix products, arithmetic and copies ran while one was open for 2% of the time, Pallas kernels for 11%

profile of v2, /device:TPU:9, one launch (start us, length us, event | category | flops | bytes accessed | tf_op | source)
XLA Modules:
  0.0 189.5 jit_solution(11141102684308037388)
XLA Ops:
  0.8 6.9 %collective-permute-start.1 = (bf16[32,1024]{1,0:T(8,128)(2,1)}, bf16[32,1024]{1,0:T(8,128)(2,1)S(1)}, u32[]{:S(2)}, u32[]{:S(2)}) collective-permute-start(bf16[32,1024]{1,0:T(8,128)(2,1)} %q0.1), channel_id=1, source_target_pairs={{0,32},{8,40},{16,48},{24,56},{32,0},{40,8},{48,16},{56,24},{64,96... | collective-permute-start | bytes 196616 | tf_op jit(solution)/shard_map/ppermute | solution.py:24
  7.7 2.4 %collective-permute-start.2 = (bf16[32,1024]{1,0:T(8,128)(2,1)}, bf16[32,1024]{1,0:T(8,128)(2,1)S(1)}, u32[]{:S(2)}, u32[]{:S(2)}) collective-permute-start(bf16[32,1024]{1,0:T(8,128)(2,1)} %q0.1), channel_id=1, source_target_pairs={{0,16},{8,24},{16,32},{24,40},{32,48},{40,56},{48,0},{56,8},{64,80... | collective-permute-start | bytes 196616 | tf_op jit(solution)/shard_map/ppermute | solution.py:24
  11.6 3.5 %collective-permute-done.q1 = bf16[32,1024]{1,0:T(8,128)(2,1)S(1)} collective-permute-done((bf16[32,1024]{1,0:T(8,128)(2,1)}, bf16[32,1024]{1,0:T(8,128)(2,1)S(1)}, u32[]{:S(2)}, u32[]{:S(2)}) %collective-permute-start) | collective-permute-done | bytes 65568 | tf_op jit(solution)/shard_map/ppermute | solution.py:24
  15.7 1.7 pick.1
  17.4 1.5 copy.9.a_n
  19.7 2.4 %collective-permute-done.6 = bf16[64,1024]{1,0:T(8,128)(2,1)S(1)} collective-permute-done((bf16[64,1024]{1,0:T(8,128)(2,1)S(1)}, bf16[64,1024]{1,0:T(8,128)(2,1)S(1)}, u32[]{:S(2)}, u32[]{:S(2)}) %collective-permute-start.6) | collective-permute-done | bytes 131104 | tf_op jit(solution)/shard_map/ppermute | solution.py:42
  24.9 2.5 %collective-permute-start.9 = (bf16[64,1024]{1,0:T(8,128)(2,1)S(1)}, bf16[64,1024]{1,0:T(8,128)(2,1)S(1)}, u32[]{:S(2)}, u32[]{:S(2)}) collective-permute-start(bf16[64,1024]{1,0:T(8,128)(2,1)S(1)} %collective-permute-done.6), channel_id=1, source_target_pairs={{0,128},{8,136},{16,144},{24,152},{32,160},{40,168},{48,176},{56,1... | collective-permute-start | bytes 393224 | tf_op jit(solution)/shard_map/ppermute | solution.py:20
  29.6 3.8 %collective-permute-done.9 = bf16[64,1024]{1,0:T(8,128)(2,1)S(1)} collective-permute-done((bf16[64,1024]{1,0:T(8,128)(2,1)S(1)}, bf16[64,1024]{1,0:T(8,128)(2,1)S(1)}, u32[]{:S(2)}, u32[]{:S(2)}) %collective-permute-start.9) | collective-permute-done | bytes 131104 | tf_op jit(solution)/shard_map/ppermute | solution.py:20
  33.4 1.4 collective-permute-start.16
  37.5 2.1 %collective-permute-start.13 = (bf16[128,1024]{1,0:T(8,128)(2,1)}, bf16[128,1024]{1,0:T(8,128)(2,1)}, u32[]{:S(2)}, u32[]{:S(2)}) collective-permute-start(bf16[128,1024]{1,0:T(8,128)(2,1)} %constant_dynamic-update-slice_fusion.p0), channel_id=1, source_target_pairs={{0,128},{8,136},{16,144},{24,152},{32,160},{40,168},{48,176},{56,1... | collective-permute-start | bytes 786440 | tf_op jit(solution)/shard_map/ppermute | solution.py:20
  39.6 1.3 collective-permute-start.12
  41.7 3.8 %collective-permute-done.14.p3 = bf16[128,1024]{1,0:T(8,128)(2,1)} collective-permute-done((bf16[128,1024]{1,0:T(8,128)(2,1)}, bf16[128,1024]{1,0:T(8,128)(2,1)}, u32[]{:S(2)}, u32[]{:S(2)}) %collective-permute-start.14) | collective-permute-done | bytes 262176 | tf_op jit(solution)/shard_map/ppermute | solution.py:20
  45.5 6.1 %collective-permute-done.13.p2 = bf16[128,1024]{1,0:T(8,128)(2,1)} collective-permute-done((bf16[128,1024]{1,0:T(8,128)(2,1)}, bf16[128,1024]{1,0:T(8,128)(2,1)}, u32[]{:S(2)}, u32[]{:S(2)}) %collective-permute-start.13) | collective-permute-done | bytes 262176 | tf_op jit(solution)/shard_map/ppermute | solution.py:20
  51.7 4.8 %shrink.1 = (bf16[512,2048]{1,0:T(8,128)(2,1)}, f32[4,64,128]{2,1,0:T(8,128)}) custom-call(s32[7]{0:T(128)} %stack.31.place, s32[512,1]{1,0:T(8,128)} %copy.10.index, bf16[128,1024]{1,0:T(8,128)(2,1)} %constant_dynamic-update-slice_fusion.p0, bf16[128,1024]{1,0:T(8,128)(2,1)} %collective-permute-done.12.p1, bf16[128,1024]{1,0:T(8,128)(2,1)} %collective-permute-done.13.p2, ...), custom_call_target="tpu_custom_call" | custom-call | tf_op jit(solution)/shard_map/shrink/pallas_call | solution.py:198
  56.5 4.4 %all-to-all-start = ((f32[4,64,128]{2,1,0:T(8,128)}), f32[4,64,128]{2,1,0:T(8,128)S(1)}, u32[]{:S(2)}, u32[]{:S(2)}) async-start(f32[4,64,128]{2,1,0:T(8,128)} %get-tuple-element.99), calls=%async_computation | async-start | bytes 262144 | tf_op jit(solution)/shard_map/all_to_all | solution.py:224
  60.9 5.7 %gate.1 = (f32[128,896]{1,0:T(8,128)}, bf16[128,896]{1,0:T(8,128)(2,1)}, bf16[128,896]{1,0:T(8,128)(2,1)}, bf16[128,896]{1,0:T(8,128)(2,1)}) custom-call(s32[7]{0:T(128)} %stack.31.place, bf16[512,2048]{1,0:T(8,128)(2,1)} %get-tuple-element.116.t, bf16[1024,896]{1,0:T(8,128)(2,1)} %w_n.1, bf16[1024,896]{1,0:T(8,128)(2,1)} %collective-permute-done.4.w_f), custom_call_target="tpu_custom_call" | custom-call | tf_op jit(solution)/shard_map/gate/pallas_call | solution.py:214
  66.6 3.5 %collective-permute-start.17 = (bf16[64,128]{1,0:T(8,128)(2,1)S(1)}, bf16[64,128]{1,0:T(8,128)(2,1)S(1)}, u32[]{:S(2)}, u32[]{:S(2)}) collective-permute-start(bf16[64,128]{1,0:T(8,128)(2,1)S(1)} %reduce_sum.9), channel_id=1, source_target_pairs={{0,0},{1,1},{2,64},{3,65},{4,128},{5,129},{6,192},{7,193},{8,8},{9... | collective-permute-start | bytes 49160 | tf_op jit(solution)/shard_map/ppermute | solution.py:38
  70.1 1.9 %collective-permute-done.17 = bf16[64,128]{1,0:T(8,128)(2,1)S(1)} collective-permute-done((bf16[64,128]{1,0:T(8,128)(2,1)S(1)}, bf16[64,128]{1,0:T(8,128)(2,1)S(1)}, u32[]{:S(2)}, u32[]{:S(2)}) %collective-permute-start.17) | collective-permute-done | bytes 16416 | tf_op jit(solution)/shard_map/ppermute | solution.py:38
  72.9 12.2 %all-to-all-start.1 = ((bf16[32,64,128]{2,1,0:T(8,128)(2,1)}), bf16[32,64,128]{2,1,0:T(8,128)(2,1)S(1)}, u32[]{:S(2)}, u32[]{:S(2)}) async-start(bf16[32,64,128]{2,1,0:T(8,128)(2,1)} %broadcast_in_dim.3), calls=%async_computation.1 | async-start | bytes 1048576 | tf_op jit(solution)/shard_map/all_to_all | solution.py:227
  86.3 1.4 collective-permute-start.20
  87.7 6.3 %base.1.up = f32[512,896]{1,0:T(8,128)} custom-call(bf16[512,2048]{1,0:T(8,128)(2,1)} %get-tuple-element.116.t, bf16[1024,896]{1,0:T(8,128)(2,1)} %w_n.2, bf16[1024,896]{1,0:T(8,128)(2,1)} %collective-permute-done.11.w_f), custom_call_target="tpu_custom_call" | custom-call | tf_op jit(solution)/shard_map/base/pallas_call | solution.py:229
  94.0 3.6 %all-to-all-done.1.low = bf16[32,64,128]{2,1,0:T(8,128)(2,1)S(1)} async-done(((bf16[32,64,128]{2,1,0:T(8,128)(2,1)}), bf16[32,64,128]{2,1,0:T(8,128)(2,1)S(1)}, u32[]{:S(2)}, u32[]{:S(2)}) %all-to-all-start.1) | async-done | bytes 524320 | tf_op jit(solution)/shard_map/all_to_all | solution.py:227
  98.5 9.2 %up.1 = (f32[128,896]{1,0:T(8,128)}, bf16[128,896]{1,0:T(8,128)(2,1)}, bf16[128,896]{1,0:T(8,128)(2,1)}, bf16[128,896]{1,0:T(8,128)(2,1)}) custom-call(s32[7]{0:T(128)} %stack.31.place, s32[512,1]{1,0:T(8,128)} %copy.10.index, bf16[32,64,128]{2,1,0:T(8,128)(2,1)} %copy-done.1, f32[512,896]{1,0:T(8,128)} %base.1.up, bf16[2048,896]{1,0:T(8,128)(2,1)} %bitcast.10, ...), custom_call_target="tpu_custom_call" | custom-call | tf_op jit(solution)/shard_map/up/pallas_call | solution.py:242
  108.4 1.6 collective-permute-start.23
  110.1 2.7 %collective-permute-done.21 = bf16[128,896]{1,0:T(8,128)(2,1)S(1)} collective-permute-done((bf16[128,896]{1,0:T(8,128)(2,1)}, bf16[128,896]{1,0:T(8,128)(2,1)S(1)}, u32[]{:S(2)}, u32[]{:S(2)}) %collective-permute-start.21) | collective-permute-done | bytes 229408 | tf_op jit(solution)/shard_map/ppermute | solution.py:28
  112.8 1.7 collective-permute-done.22
  114.5 2.2 %collective-permute-done.23 = bf16[128,896]{1,0:T(8,128)(2,1)S(1)} collective-permute-done((bf16[128,896]{1,0:T(8,128)(2,1)}, bf16[128,896]{1,0:T(8,128)(2,1)S(1)}, u32[]{:S(2)}, u32[]{:S(2)}) %collective-permute-start.23) | collective-permute-done | bytes 229408 | tf_op jit(solution)/shard_map/ppermute | solution.py:28
  116.8 1.3 multiply_convert_fusion.h0
  119.5 1.6 collective-permute-start.24
  121.2 2.3 %collective-permute-done.26.h3 = bf16[128,896]{1,0:T(8,128)(2,1)S(1)} collective-permute-done((bf16[128,896]{1,0:T(8,128)(2,1)S(1)}, bf16[128,896]{1,0:T(8,128)(2,1)S(1)}, u32[]{:S(2)}, u32[]{:S(2)}) %collective-permute-start.26) | collective-permute-done | bytes 229408 | tf_op jit(solution)/shard_map/ppermute | solution.py:28
  123.5 2.1 %collective-permute-done.25.h2 = bf16[128,896]{1,0:T(8,128)(2,1)S(1)} collective-permute-done((bf16[128,896]{1,0:T(8,128)(2,1)S(1)}, bf16[128,896]{1,0:T(8,128)(2,1)S(1)}, u32[]{:S(2)}, u32[]{:S(2)}) %collective-permute-start.25) | collective-permute-done | bytes 229408 | tf_op jit(solution)/shard_map/ppermute | solution.py:28
  125.6 1.9 collective-permute-done.24.h1
  128.1 6.1 %mix.1 = (f32[128,1024]{1,0:T(8,128)}, bf16[128,1024]{1,0:T(8,128)(2,1)}, bf16[128,1024]{1,0:T(8,128)(2,1)}, bf16[128,1024]{1,0:T(8,128)(2,1)}, f32[256,1024]{1,0:T(8,128)}, /*index=5*/bf16[256,1024]{1,0:T(8,128)(2,1)}) custom-call(s32[7]{0:T(128)} %stack.31.place, bf16[128,896]{1,0:T(8,128)(2,1)} %copy-done.5, bf16[128,896]{1,0:T(8,128)(2,1)} %copy-done.10, ...), custom_call_target="tpu_custom_call" | custom-call | tf_op jit(solution)/shard_map/mix/pallas_call | solution.py:256
  134.2 4.8 %collective-permute-start.30 = (bf16[256,1024]{1,0:T(8,128)(2,1)}, bf16[256,1024]{1,0:T(8,128)(2,1)S(1)}, u32[]{:S(2)}, u32[]{:S(2)}) collective-permute-start(bf16[256,1024]{1,0:T(8,128)(2,1)} %get-tuple-element.128), channel_id=1, source_target_pairs={{0,8},{8,0},{16,24},{24,16},{32,40},{40,32},{48,56},{56,48},{64,72... | collective-permute-start | bytes 1572872 | tf_op jit(solution)/shard_map/ppermute | solution.py:32
  139.1 6.6 %collective-permute-start.27 = (bf16[128,1024]{1,0:T(8,128)(2,1)}, bf16[128,1024]{1,0:T(8,128)(2,1)S(1)}, u32[]{:S(2)}, u32[]{:S(2)}) collective-permute-start(bf16[128,1024]{1,0:T(8,128)(2,1)} %get-tuple-element.125), channel_id=1, source_target_pairs={{0,64},{8,72},{16,80},{24,88},{32,96},{40,104},{48,112},{56,120},{... | collective-permute-start | bytes 786440 | tf_op jit(solution)/shard_map/ppermute | solution.py:20
  145.7 1.8 collective-permute-start.28
  147.5 2.0 %collective-permute-start.29 = (bf16[128,1024]{1,0:T(8,128)(2,1)}, bf16[128,1024]{1,0:T(8,128)(2,1)S(1)}, u32[]{:S(2)}, u32[]{:S(2)}) collective-permute-start(bf16[128,1024]{1,0:T(8,128)(2,1)} %get-tuple-element.127), channel_id=1, source_target_pairs={{0,192},{8,200},{16,208},{24,216},{32,224},{40,232},{48,240},{56,2... | collective-permute-start | bytes 786440 | tf_op jit(solution)/shard_map/ppermute | solution.py:20
  149.4 2.0 %collective-permute-done.27 = bf16[128,1024]{1,0:T(8,128)(2,1)S(1)} collective-permute-done((bf16[128,1024]{1,0:T(8,128)(2,1)}, bf16[128,1024]{1,0:T(8,128)(2,1)S(1)}, u32[]{:S(2)}, u32[]{:S(2)}) %collective-permute-start.27) | collective-permute-done | bytes 262176 | tf_op jit(solution)/shard_map/ppermute | solution.py:20
  151.5 6.7 %collective-permute-done.28 = bf16[128,1024]{1,0:T(8,128)(2,1)S(1)} collective-permute-done((bf16[128,1024]{1,0:T(8,128)(2,1)}, bf16[128,1024]{1,0:T(8,128)(2,1)S(1)}, u32[]{:S(2)}, u32[]{:S(2)}) %collective-permute-start.28) | collective-permute-done | bytes 262176 | tf_op jit(solution)/shard_map/ppermute | solution.py:20
  160.1 3.3 %collective-permute-start.34 = (bf16[64,1024]{1,0:T(8,128)(2,1)S(1)}, bf16[64,1024]{1,0:T(8,128)(2,1)S(1)}, u32[]{:S(2)}, u32[]{:S(2)}) collective-permute-start(bf16[64,1024]{1,0:T(8,128)(2,1)S(1)} %get-tuple-element.143), channel_id=1, source_target_pairs={{0,192},{8,200},{16,208},{24,216},{32,224},{40,232},{48,240},{56,2... | collective-permute-start | bytes 393224 | tf_op jit(solution)/shard_map/ppermute | solution.py:20
  164.2 2.7 %collective-permute-done.34 = bf16[64,1024]{1,0:T(8,128)(2,1)S(1)} collective-permute-done((bf16[64,1024]{1,0:T(8,128)(2,1)S(1)}, bf16[64,1024]{1,0:T(8,128)(2,1)S(1)}, u32[]{:S(2)}, u32[]{:S(2)}) %collective-permute-start.34) | collective-permute-done | bytes 131104 | tf_op jit(solution)/shard_map/ppermute | solution.py:20
  166.9 2.0 %collective-permute-done.33 = bf16[64,1024]{1,0:T(8,128)(2,1)S(1)} collective-permute-done((bf16[64,1024]{1,0:T(8,128)(2,1)S(1)}, bf16[64,1024]{1,0:T(8,128)(2,1)S(1)}, u32[]{:S(2)}, u32[]{:S(2)}) %collective-permute-start.33) | collective-permute-done | bytes 131104 | tf_op jit(solution)/shard_map/ppermute | solution.py:20
  168.8 2.1 %collective-permute-done.32 = bf16[64,1024]{1,0:T(8,128)(2,1)S(1)} collective-permute-done((bf16[64,1024]{1,0:T(8,128)(2,1)S(1)}, bf16[64,1024]{1,0:T(8,128)(2,1)S(1)}, u32[]{:S(2)}, u32[]{:S(2)}) %collective-permute-start.32) | collective-permute-done | bytes 131104 | tf_op jit(solution)/shard_map/ppermute | solution.py:20
  171.1 3.2 %collective-permute-start.37 = (bf16[16,2048]{1,0:T(8,128)(2,1)S(1)}, bf16[16,2048]{1,0:T(8,128)(2,1)S(1)}, u32[]{:S(2)}, u32[]{:S(2)}) collective-permute-start(bf16[16,2048]{1,0:T(8,128)(2,1)S(1)} %get-tuple-element.146), channel_id=1, source_target_pairs={{0,48},{8,56},{16,0},{24,8},{32,16},{40,24},{48,32},{56,40},{64,11... | collective-permute-start | bytes 196616 | tf_op jit(solution)/shard_map/ppermute | solution.py:24
  174.3 5.6 %collective-permute-start.36 = (bf16[16,2048]{1,0:T(8,128)(2,1)S(1)}, bf16[16,2048]{1,0:T(8,128)(2,1)S(1)}, u32[]{:S(2)}, u32[]{:S(2)}) collective-permute-start(bf16[16,2048]{1,0:T(8,128)(2,1)S(1)} %get-tuple-element.147), channel_id=1, source_target_pairs={{0,32},{8,40},{16,48},{24,56},{32,0},{40,8},{48,16},{56,24},{64,96... | collective-permute-start | bytes 196616 | tf_op jit(solution)/shard_map/ppermute | solution.py:24
  180.8 1.5 collective-permute-done.36
  182.2 4.0 %collective-permute-done.35 = bf16[16,2048]{1,0:T(8,128)(2,1)S(1)} collective-permute-done((bf16[16,2048]{1,0:T(8,128)(2,1)S(1)}, bf16[16,2048]{1,0:T(8,128)(2,1)S(1)}, u32[]{:S(2)}, u32[]{:S(2)}) %collective-permute-start.35) | collective-permute-done | bytes 65568 | tf_op jit(solution)/shard_map/ppermute | solution.py:24
  186.3 1.7 collective-permute-start.38
  (97 shorter events, 23.2 us)
Async XLA Ops:
  0.0 33.4 %copy-start.2 = (bf16[896,1024]{1,0:T(8,128)(2,1)S(1)}, bf16[896,1024]{1,0:T(8,128)(2,1)}, u32[]{:S(2)}) copy-start(bf16[896,1024]{1,0:T(8,128)(2,1)} %d_n) | copy-start | bytes 5505028
  0.0 15.1 %collective-permute-start.3 = (bf16[2048,896]{1,0:T(8,128)(2,1)}, bf16[2048,896]{1,0:T(8,128)(2,1)}, u32[]{:S(2)}, u32[]{:S(2)}) collective-permute-start(bf16[2048,896]{1,0:T(8,128)(2,1)} %bitcast.9), channel_id=1, source_target_pairs={{0,1},{1,0},{2,3},{3,2},{4,5},{5,4},{6,7},{7,6},{8,9},{9,8},{10,11... | collective-permute-start | bytes 11010056 | tf_op jit(solution)/shard_map/ppermute | solution.py:42
  0.7 14.4 %collective-permute-start.4 = (bf16[1024,896]{1,0:T(8,128)(2,1)}, bf16[1024,896]{1,0:T(8,128)(2,1)}, u32[]{:S(2)}, u32[]{:S(2)}) collective-permute-start(bf16[1024,896]{1,0:T(8,128)(2,1)} %w_n.1), channel_id=1, source_target_pairs={{0,1},{1,0},{2,3},{3,2},{4,5},{5,4},{6,7},{7,6},{8,9},{9,8},{10,11... | collective-permute-start | bytes 5505032 | tf_op jit(solution)/shard_map/ppermute | solution.py:42
  0.8 10.8 %collective-permute-start.1 = (bf16[32,1024]{1,0:T(8,128)(2,1)}, bf16[32,1024]{1,0:T(8,128)(2,1)S(1)}, u32[]{:S(2)}, u32[]{:S(2)}) collective-permute-start(bf16[32,1024]{1,0:T(8,128)(2,1)} %q0.1), channel_id=1, source_target_pairs={{0,32},{8,40},{16,48},{24,56},{32,0},{40,8},{48,16},{56,24},{64,96... | collective-permute-start | bytes 196616 | tf_op jit(solution)/shard_map/ppermute | solution.py:24
  7.7 7.4 %collective-permute-start = (bf16[32,1024]{1,0:T(8,128)(2,1)}, bf16[32,1024]{1,0:T(8,128)(2,1)S(1)}, u32[]{:S(2)}, u32[]{:S(2)}) collective-permute-start(bf16[32,1024]{1,0:T(8,128)(2,1)} %q0.1), channel_id=1, source_target_pairs={{0,48},{8,56},{16,0},{24,8},{32,16},{40,24},{48,32},{56,40},{64,11... | collective-permute-start | bytes 196616 | tf_op jit(solution)/shard_map/ppermute | solution.py:24
  7.7 7.4 %collective-permute-start.2 = (bf16[32,1024]{1,0:T(8,128)(2,1)}, bf16[32,1024]{1,0:T(8,128)(2,1)S(1)}, u32[]{:S(2)}, u32[]{:S(2)}) collective-permute-start(bf16[32,1024]{1,0:T(8,128)(2,1)} %q0.1), channel_id=1, source_target_pairs={{0,16},{8,24},{16,32},{24,40},{32,48},{40,56},{48,0},{56,8},{64,80... | collective-permute-start | bytes 196616 | tf_op jit(solution)/shard_map/ppermute | solution.py:24
  19.0 32.7 %copy-start = (bf16[1024,512]{1,0:T(8,128)(2,1)}, bf16[1024,512]{1,0:T(8,128)(2,1)S(1)}, u32[]{:S(2)}) copy-start(bf16[1024,512]{1,0:T(8,128)(2,1)S(1)} %copy.9.a_n) | copy-start | bytes 3145732
  19.0 3.1 %collective-permute-start.7 = (bf16[1024,512]{1,0:T(8,128)(2,1)S(1)}, bf16[1024,512]{1,0:T(8,128)(2,1)S(1)}, u32[]{:S(2)}, u32[]{:S(2)}) collective-permute-start(bf16[1024,512]{1,0:T(8,128)(2,1)S(1)} %copy.9.a_n), channel_id=1, source_target_pairs={{0,1},{1,0},{2,3},{3,2},{4,5},{5,4},{6,7},{7,6},{8,9},{9,8},{10,11... | collective-permute-start | bytes 3145736 | tf_op jit(solution)/shard_map/ppermute | solution.py:42
  19.6 2.5 %collective-permute-start.6 = (bf16[64,1024]{1,0:T(8,128)(2,1)S(1)}, bf16[64,1024]{1,0:T(8,128)(2,1)S(1)}, u32[]{:S(2)}, u32[]{:S(2)}) collective-permute-start(bf16[64,1024]{1,0:T(8,128)(2,1)S(1)} %copy-done.15), channel_id=1, source_target_pairs={{0,1},{1,0},{2,3},{3,2},{4,5},{5,4},{6,7},{7,6},{8,9},{9,8},{10,11... | collective-permute-start | bytes 393224 | tf_op jit(solution)/shard_map/ppermute | solution.py:42
  22.1 11.3 %copy-start.3 = (bf16[1024,512]{1,0:T(8,128)(2,1)}, bf16[1024,512]{1,0:T(8,128)(2,1)S(1)}, u32[]{:S(2)}) copy-start(bf16[1024,512]{1,0:T(8,128)(2,1)S(1)} %collective-permute-done.7.a_f) | copy-start | bytes 3145732
  22.1 11.3 %collective-permute-start.11 = (bf16[1024,896]{1,0:T(8,128)(2,1)}, bf16[1024,896]{1,0:T(8,128)(2,1)}, u32[]{:S(2)}, u32[]{:S(2)}) collective-permute-start(bf16[1024,896]{1,0:T(8,128)(2,1)} %w_n.2), channel_id=1, source_target_pairs={{0,1},{1,0},{2,3},{3,2},{4,5},{5,4},{6,7},{7,6},{8,9},{9,8},{10,11... | collective-permute-start | bytes 5505032 | tf_op jit(solution)/shard_map/ppermute | solution.py:42
  22.4 6.1 %collective-permute-start.5 = (bf16[64,1024]{1,0:T(8,128)(2,1)S(1)}, bf16[64,1024]{1,0:T(8,128)(2,1)S(1)}, u32[]{:S(2)}, u32[]{:S(2)}) collective-permute-start(bf16[64,1024]{1,0:T(8,128)(2,1)S(1)} %copy-done.11), channel_id=1, source_target_pairs={{0,8},{8,0},{16,24},{24,16},{32,40},{40,32},{48,56},{56,48},{64,72... | collective-permute-start | bytes 393224 | tf_op jit(solution)/shard_map/ppermute | solution.py:32
  23.7 5.9 %collective-permute-start.10 = (bf16[64,1024]{1,0:T(8,128)(2,1)S(1)}, bf16[64,1024]{1,0:T(8,128)(2,1)S(1)}, u32[]{:S(2)}, u32[]{:S(2)}) collective-permute-start(bf16[64,1024]{1,0:T(8,128)(2,1)S(1)} %collective-permute-done.6), channel_id=1, source_target_pairs={{0,64},{8,72},{16,80},{24,88},{32,96},{40,104},{48,112},{56,120},{... | collective-permute-start | bytes 393224 | tf_op jit(solution)/shard_map/ppermute | solution.py:20
  24.9 8.4 %collective-permute-start.9 = (bf16[64,1024]{1,0:T(8,128)(2,1)S(1)}, bf16[64,1024]{1,0:T(8,128)(2,1)S(1)}, u32[]{:S(2)}, u32[]{:S(2)}) collective-permute-start(bf16[64,1024]{1,0:T(8,128)(2,1)S(1)} %collective-permute-done.6), channel_id=1, source_target_pairs={{0,128},{8,136},{16,144},{24,152},{32,160},{40,168},{48,176},{56,1... | collective-permute-start | bytes 393224 | tf_op jit(solution)/shard_map/ppermute | solution.py:20
  27.4 6.0 %collective-permute-start.8 = (bf16[64,1024]{1,0:T(8,128)(2,1)S(1)}, bf16[64,1024]{1,0:T(8,128)(2,1)S(1)}, u32[]{:S(2)}, u32[]{:S(2)}) collective-permute-start(bf16[64,1024]{1,0:T(8,128)(2,1)S(1)} %collective-permute-done.6), channel_id=1, source_target_pairs={{0,192},{8,200},{16,208},{24,216},{32,224},{40,232},{48,240},{56,2... | collective-permute-start | bytes 393224 | tf_op jit(solution)/shard_map/ppermute | solution.py:20
  33.4 18.3 %collective-permute-start.16 = (bf16[896,1024]{1,0:T(8,128)(2,1)S(1)}, bf16[896,1024]{1,0:T(8,128)(2,1)}, u32[]{:S(2)}, u32[]{:S(2)}) collective-permute-start(bf16[896,1024]{1,0:T(8,128)(2,1)S(1)} %copy-done.2), channel_id=1, source_target_pairs={{0,1},{1,0},{2,3},{3,2},{4,5},{5,4},{6,7},{7,6},{8,9},{9,8},{10,11... | collective-permute-start | bytes 5505032 | tf_op jit(solution)/shard_map/ppermute | solution.py:42
  34.8 16.9 %copy-start.6 = (bf16[256,1024]{1,0:T(8,128)(2,1)}, bf16[256,1024]{1,0:T(8,128)(2,1)S(1)}, u32[]{:S(2)}) copy-start(bf16[256,1024]{1,0:T(8,128)(2,1)S(1)} %constant_dynamic-update-slice_fusion.2.q0) | copy-start | bytes 1572868
  34.8 16.8 %collective-permute-start.15 = (bf16[256,1024]{1,0:T(8,128)(2,1)S(1)}, bf16[256,1024]{1,0:T(8,128)(2,1)}, u32[]{:S(2)}, u32[]{:S(2)}) collective-permute-start(bf16[256,1024]{1,0:T(8,128)(2,1)S(1)} %constant_dynamic-update-slice_fusion.2.q0), channel_id=1, source_target_pairs={{0,8},{8,0},{16,24},{24,16},{32,40},{40,32},{48,56},{56,48},{64,72... | collective-permute-start | bytes 1572872 | tf_op jit(solution)/shard_map/ppermute | solution.py:32
  36.4 9.1 %collective-permute-start.14 = (bf16[128,1024]{1,0:T(8,128)(2,1)}, bf16[128,1024]{1,0:T(8,128)(2,1)}, u32[]{:S(2)}, u32[]{:S(2)}) collective-permute-start(bf16[128,1024]{1,0:T(8,128)(2,1)} %constant_dynamic-update-slice_fusion.p0), channel_id=1, source_target_pairs={{0,64},{8,72},{16,80},{24,88},{32,96},{40,104},{48,112},{56,120},{... | collective-permute-start | bytes 786440 | tf_op jit(solution)/shard_map/ppermute | solution.py:20
  37.5 14.2 %collective-permute-start.13 = (bf16[128,1024]{1,0:T(8,128)(2,1)}, bf16[128,1024]{1,0:T(8,128)(2,1)}, u32[]{:S(2)}, u32[]{:S(2)}) collective-permute-start(bf16[128,1024]{1,0:T(8,128)(2,1)} %constant_dynamic-update-slice_fusion.p0), channel_id=1, source_target_pairs={{0,128},{8,136},{16,144},{24,152},{32,160},{40,168},{48,176},{56,1... | collective-permute-start | bytes 786440 | tf_op jit(solution)/shard_map/ppermute | solution.py:20
  39.6 12.1 %collective-permute-start.12 = (bf16[128,1024]{1,0:T(8,128)(2,1)}, bf16[128,1024]{1,0:T(8,128)(2,1)}, u32[]{:S(2)}, u32[]{:S(2)}) collective-permute-start(bf16[128,1024]{1,0:T(8,128)(2,1)} %constant_dynamic-update-slice_fusion.p0), channel_id=1, source_target_pairs={{0,192},{8,200},{16,208},{24,216},{32,224},{40,232},{48,240},{56,2... | collective-permute-start | bytes 786440 | tf_op jit(solution)/shard_map/ppermute | solution.py:20
  56.5 10.1 %all-to-all-start = ((f32[4,64,128]{2,1,0:T(8,128)}), f32[4,64,128]{2,1,0:T(8,128)S(1)}, u32[]{:S(2)}, u32[]{:S(2)}) async-start(f32[4,64,128]{2,1,0:T(8,128)} %get-tuple-element.99), calls=%async_computation | async-start | bytes 262144 | tf_op jit(solution)/shard_map/all_to_all | solution.py:224
  66.6 5.4 %collective-permute-start.17 = (bf16[64,128]{1,0:T(8,128)(2,1)S(1)}, bf16[64,128]{1,0:T(8,128)(2,1)S(1)}, u32[]{:S(2)}, u32[]{:S(2)}) collective-permute-start(bf16[64,128]{1,0:T(8,128)(2,1)S(1)} %reduce_sum.9), channel_id=1, source_target_pairs={{0,0},{1,1},{2,64},{3,65},{4,128},{5,129},{6,192},{7,193},{8,8},{9... | collective-permute-start | bytes 49160 | tf_op jit(solution)/shard_map/ppermute | solution.py:38
  72.9 24.8 %all-to-all-start.1 = ((bf16[32,64,128]{2,1,0:T(8,128)(2,1)}), bf16[32,64,128]{2,1,0:T(8,128)(2,1)S(1)}, u32[]{:S(2)}, u32[]{:S(2)}) async-start(bf16[32,64,128]{2,1,0:T(8,128)(2,1)} %broadcast_in_dim.3), calls=%async_computation.1 | async-start | bytes 1048576 | tf_op jit(solution)/shard_map/all_to_all | solution.py:227
  85.2 23.3 %collective-permute-start.18 = (bf16[128,896]{1,0:T(8,128)(2,1)}, bf16[128,896]{1,0:T(8,128)(2,1)S(1)}, u32[]{:S(2)}, u32[]{:S(2)}) collective-permute-start(bf16[128,896]{1,0:T(8,128)(2,1)} %get-tuple-element.112), channel_id=1, source_target_pairs={{0,2},{1,3},{2,4},{3,5},{4,6},{5,7},{6,0},{7,1},{8,10},{9,11},{10,... | collective-permute-start | bytes 688136 | tf_op jit(solution)/shard_map/ppermute | solution.py:28
  85.3 24.8 %collective-permute-start.19 = (bf16[128,896]{1,0:T(8,128)(2,1)}, bf16[128,896]{1,0:T(8,128)(2,1)S(1)}, u32[]{:S(2)}, u32[]{:S(2)}) collective-permute-start(bf16[128,896]{1,0:T(8,128)(2,1)} %get-tuple-element.113), channel_id=1, source_target_pairs={{0,4},{1,5},{2,6},{3,7},{4,0},{5,1},{6,2},{7,3},{8,12},{9,13},{10,... | collective-permute-start | bytes 688136 | tf_op jit(solution)/shard_map/ppermute | solution.py:28
  86.3 23.7 %collective-permute-start.20 = (bf16[128,896]{1,0:T(8,128)(2,1)}, bf16[128,896]{1,0:T(8,128)(2,1)S(1)}, u32[]{:S(2)}, u32[]{:S(2)}) collective-permute-start(bf16[128,896]{1,0:T(8,128)(2,1)} %get-tuple-element.114), channel_id=1, source_target_pairs={{0,6},{1,7},{2,0},{3,1},{4,2},{5,3},{6,4},{7,5},{8,14},{9,15},{10,... | collective-permute-start | bytes 688136 | tf_op jit(solution)/shard_map/ppermute | solution.py:28
  94.0 22.7 %copy-start.7 = (f32[128,896]{1,0:T(8,128)S(1)}, f32[128,896]{1,0:T(8,128)}, u32[]{:S(2)}) copy-start(f32[128,896]{1,0:T(8,128)} %get-tuple-element.111) | copy-start | bytes 1376260
  107.7 5.1 %collective-permute-start.21 = (bf16[128,896]{1,0:T(8,128)(2,1)}, bf16[128,896]{1,0:T(8,128)(2,1)S(1)}, u32[]{:S(2)}, u32[]{:S(2)}) collective-permute-start(bf16[128,896]{1,0:T(8,128)(2,1)} %get-tuple-element.120), channel_id=1, source_target_pairs={{0,2},{1,3},{2,4},{3,5},{4,6},{5,7},{6,0},{7,1},{8,10},{9,11},{10,... | collective-permute-start | bytes 688136 | tf_op jit(solution)/shard_map/ppermute | solution.py:28
  107.7 6.8 %collective-permute-start.22 = (bf16[128,896]{1,0:T(8,128)(2,1)}, bf16[128,896]{1,0:T(8,128)(2,1)S(1)}, u32[]{:S(2)}, u32[]{:S(2)}) collective-permute-start(bf16[128,896]{1,0:T(8,128)(2,1)} %get-tuple-element.121), channel_id=1, source_target_pairs={{0,4},{1,5},{2,6},{3,7},{4,0},{5,1},{6,2},{7,3},{8,12},{9,13},{10,... | collective-permute-start | bytes 688136 | tf_op jit(solution)/shard_map/ppermute | solution.py:28
  108.4 8.3 %collective-permute-start.23 = (bf16[128,896]{1,0:T(8,128)(2,1)}, bf16[128,896]{1,0:T(8,128)(2,1)S(1)}, u32[]{:S(2)}, u32[]{:S(2)}) collective-permute-start(bf16[128,896]{1,0:T(8,128)(2,1)} %get-tuple-element.122), channel_id=1, source_target_pairs={{0,6},{1,7},{2,0},{3,1},{4,2},{5,3},{6,4},{7,5},{8,14},{9,15},{10,... | collective-permute-start | bytes 688136 | tf_op jit(solution)/shard_map/ppermute | solution.py:28
  118.1 9.4 %copy-start.5 = (bf16[128,896]{1,0:T(8,128)(2,1)}, bf16[128,896]{1,0:T(8,128)(2,1)S(1)}, u32[]{:S(2)}) copy-start(bf16[128,896]{1,0:T(8,128)(2,1)S(1)} %multiply_convert_fusion.h0) | copy-start | bytes 688132
  118.1 5.4 %collective-permute-start.26 = (bf16[128,896]{1,0:T(8,128)(2,1)S(1)}, bf16[128,896]{1,0:T(8,128)(2,1)S(1)}, u32[]{:S(2)}, u32[]{:S(2)}) collective-permute-start(bf16[128,896]{1,0:T(8,128)(2,1)S(1)} %multiply_convert_fusion.h0), channel_id=1, source_target_pairs={{0,2},{1,3},{2,4},{3,5},{4,6},{5,7},{6,0},{7,1},{8,10},{9,11},{10,... | collective-permute-start | bytes 688136 | tf_op jit(solution)/shard_map/ppermute | solution.py:28
  119.1 6.5 %collective-permute-start.25 = (bf16[128,896]{1,0:T(8,128)(2,1)S(1)}, bf16[128,896]{1,0:T(8,128)(2,1)S(1)}, u32[]{:S(2)}, u32[]{:S(2)}) collective-permute-start(bf16[128,896]{1,0:T(8,128)(2,1)S(1)} %multiply_convert_fusion.h0), channel_id=1, source_target_pairs={{0,4},{1,5},{2,6},{3,7},{4,0},{5,1},{6,2},{7,3},{8,12},{9,13},{10,... | collective-permute-start | bytes 688136 | tf_op jit(solution)/shard_map/ppermute | solution.py:28
  119.5 7.9 %collective-permute-start.24 = (bf16[128,896]{1,0:T(8,128)(2,1)S(1)}, bf16[128,896]{1,0:T(8,128)(2,1)S(1)}, u32[]{:S(2)}, u32[]{:S(2)}) collective-permute-start(bf16[128,896]{1,0:T(8,128)(2,1)S(1)} %multiply_convert_fusion.h0), channel_id=1, source_target_pairs={{0,6},{1,7},{2,0},{3,1},{4,2},{5,3},{6,4},{7,5},{8,14},{9,15},{10,... | collective-permute-start | bytes 688136 | tf_op jit(solution)/shard_map/ppermute | solution.py:28
  134.2 25.6 %copy-start.4 = (f32[256,1024]{1,0:T(8,128)S(1)}, f32[256,1024]{1,0:T(8,128)}, u32[]{:S(2)}) copy-start(f32[256,1024]{1,0:T(8,128)} %get-tuple-element.132) | copy-start | bytes 3145732
  134.2 23.9 %collective-permute-start.30 = (bf16[256,1024]{1,0:T(8,128)(2,1)}, bf16[256,1024]{1,0:T(8,128)(2,1)S(1)}, u32[]{:S(2)}, u32[]{:S(2)}) collective-permute-start(bf16[256,1024]{1,0:T(8,128)(2,1)} %get-tuple-element.128), channel_id=1, source_target_pairs={{0,8},{8,0},{16,24},{24,16},{32,40},{40,32},{48,56},{56,48},{64,72... | collective-permute-start | bytes 1572872 | tf_op jit(solution)/shard_map/ppermute | solution.py:32
  139.1 12.4 %collective-permute-start.27 = (bf16[128,1024]{1,0:T(8,128)(2,1)}, bf16[128,1024]{1,0:T(8,128)(2,1)S(1)}, u32[]{:S(2)}, u32[]{:S(2)}) collective-permute-start(bf16[128,1024]{1,0:T(8,128)(2,1)} %get-tuple-element.125), channel_id=1, source_target_pairs={{0,64},{8,72},{16,80},{24,88},{32,96},{40,104},{48,112},{56,120},{... | collective-permute-start | bytes 786440 | tf_op jit(solution)/shard_map/ppermute | solution.py:20
  145.7 12.5 %collective-permute-start.28 = (bf16[128,1024]{1,0:T(8,128)(2,1)}, bf16[128,1024]{1,0:T(8,128)(2,1)S(1)}, u32[]{:S(2)}, u32[]{:S(2)}) collective-permute-start(bf16[128,1024]{1,0:T(8,128)(2,1)} %get-tuple-element.126), channel_id=1, source_target_pairs={{0,128},{8,136},{16,144},{24,152},{32,160},{40,168},{48,176},{56,1... | collective-permute-start | bytes 786440 | tf_op jit(solution)/shard_map/ppermute | solution.py:20
  147.5 10.7 %collective-permute-start.29 = (bf16[128,1024]{1,0:T(8,128)(2,1)}, bf16[128,1024]{1,0:T(8,128)(2,1)S(1)}, u32[]{:S(2)}, u32[]{:S(2)}) collective-permute-start(bf16[128,1024]{1,0:T(8,128)(2,1)} %get-tuple-element.127), channel_id=1, source_target_pairs={{0,192},{8,200},{16,208},{24,216},{32,224},{40,232},{48,240},{56,2... | collective-permute-start | bytes 786440 | tf_op jit(solution)/shard_map/ppermute | solution.py:20
  159.3 4.9 %collective-permute-start.31 = (bf16[64,1024]{1,0:T(8,128)(2,1)S(1)}, bf16[64,1024]{1,0:T(8,128)(2,1)S(1)}, u32[]{:S(2)}, u32[]{:S(2)}) collective-permute-start(bf16[64,1024]{1,0:T(8,128)(2,1)S(1)} %slice.97), channel_id=1, source_target_pairs={{0,8},{8,0},{16,24},{24,16},{32,40},{40,32},{48,56},{56,48},{64,72... | collective-permute-start | bytes 393224 | tf_op jit(solution)/shard_map/ppermute | solution.py:32
  160.1 6.8 %collective-permute-start.34 = (bf16[64,1024]{1,0:T(8,128)(2,1)S(1)}, bf16[64,1024]{1,0:T(8,128)(2,1)S(1)}, u32[]{:S(2)}, u32[]{:S(2)}) collective-permute-start(bf16[64,1024]{1,0:T(8,128)(2,1)S(1)} %get-tuple-element.143), channel_id=1, source_target_pairs={{0,192},{8,200},{16,208},{24,216},{32,224},{40,232},{48,240},{56,2... | collective-permute-start | bytes 393224 | tf_op jit(solution)/shard_map/ppermute | solution.py:20
  163.4 5.4 %collective-permute-start.33 = (bf16[64,1024]{1,0:T(8,128)(2,1)S(1)}, bf16[64,1024]{1,0:T(8,128)(2,1)S(1)}, u32[]{:S(2)}, u32[]{:S(2)}) collective-permute-start(bf16[64,1024]{1,0:T(8,128)(2,1)S(1)} %get-tuple-element.144), channel_id=1, source_target_pairs={{0,128},{8,136},{16,144},{24,152},{32,160},{40,168},{48,176},{56,1... | collective-permute-start | bytes 393224 | tf_op jit(solution)/shard_map/ppermute | solution.py:20
  163.4 7.5 %collective-permute-start.32 = (bf16[64,1024]{1,0:T(8,128)(2,1)S(1)}, bf16[64,1024]{1,0:T(8,128)(2,1)S(1)}, u32[]{:S(2)}, u32[]{:S(2)}) collective-permute-start(bf16[64,1024]{1,0:T(8,128)(2,1)S(1)} %get-tuple-element.145), channel_id=1, source_target_pairs={{0,64},{8,72},{16,80},{24,88},{32,96},{40,104},{48,112},{56,120},{... | collective-permute-start | bytes 393224 | tf_op jit(solution)/shard_map/ppermute | solution.py:20
  171.1 9.7 %collective-permute-start.37 = (bf16[16,2048]{1,0:T(8,128)(2,1)S(1)}, bf16[16,2048]{1,0:T(8,128)(2,1)S(1)}, u32[]{:S(2)}, u32[]{:S(2)}) collective-permute-start(bf16[16,2048]{1,0:T(8,128)(2,1)S(1)} %get-tuple-element.146), channel_id=1, source_target_pairs={{0,48},{8,56},{16,0},{24,8},{32,16},{40,24},{48,32},{56,40},{64,11... | collective-permute-start | bytes 196616 | tf_op jit(solution)/shard_map/ppermute | solution.py:24
  174.3 7.9 %collective-permute-start.36 = (bf16[16,2048]{1,0:T(8,128)(2,1)S(1)}, bf16[16,2048]{1,0:T(8,128)(2,1)S(1)}, u32[]{:S(2)}, u32[]{:S(2)}) collective-permute-start(bf16[16,2048]{1,0:T(8,128)(2,1)S(1)} %get-tuple-element.147), channel_id=1, source_target_pairs={{0,32},{8,40},{16,48},{24,56},{32,0},{40,8},{48,16},{56,24},{64,96... | collective-permute-start | bytes 196616 | tf_op jit(solution)/shard_map/ppermute | solution.py:24
  179.9 6.3 %collective-permute-start.35 = (bf16[16,2048]{1,0:T(8,128)(2,1)S(1)}, bf16[16,2048]{1,0:T(8,128)(2,1)S(1)}, u32[]{:S(2)}, u32[]{:S(2)}) collective-permute-start(bf16[16,2048]{1,0:T(8,128)(2,1)S(1)} %get-tuple-element.148), channel_id=1, source_target_pairs={{0,16},{8,24},{16,32},{24,40},{32,48},{40,56},{48,0},{56,8},{64,80... | collective-permute-start | bytes 196616 | tf_op jit(solution)/shard_map/ppermute | solution.py:24
  186.3 2.6 %collective-permute-start.38 = (bf16[16,1024]{1,0:T(8,128)(2,1)S(1)}, bf16[16,1024]{1,0:T(8,128)(2,1)S(1)}, u32[]{:S(2)}, u32[]{:S(2)}) collective-permute-start(bf16[16,1024]{1,0:T(8,128)(2,1)S(1)} %get-tuple-element.150), channel_id=1, source_target_pairs={{0,1},{1,0},{2,3},{3,2},{4,5},{5,4},{6,7},{7,6},{8,9},{9,8},{10,11... | collective-permute-start | bytes 98312 | tf_op jit(solution)/shard_map/ppermute | solution.py:42
  (9 other events, 19.4 us)

commit v3 on v2

--- a/solution.py
+++ b/solution.py
@@ -9,7 +9,7 @@
 
 NX, NZ, NY, NC = 4, 8, 4, 2
 F32, BF16 = jnp.float32, jnp.bfloat16
-VMEM_LIMIT = 60 * 1024 * 1024
+MIB = 1024 * 1024
 
 
 def device(x, z, y, c):
@@ -32,17 +32,15 @@
     return lax.ppermute(v, "wide", [(i, i ^ 1) for i in range(NX * NZ)])
 
 
-def send_home(v):
-    cells = [(x, z, y, c) for x in range(NX) for z in range(NZ) for y in range(NY) for c in range(NC)]
-    moves = [(device(x, z, y, c), device(y, z, x, c)) for x, z, y, c in cells]
-    return lax.ppermute(v, ("wide", "narrow"), moves)
-
-
 def core(v):
     return lax.ppermute(v, "narrow", [(i, i ^ 1) for i in range(NY * NC)])
 
 
-Y_GROUPS = [[y * NC + c for y in range(NY)] for c in range(NC)]
+HOME_GROUPS = [
+    [device(x, z + p, y, c) for x in range(NX) for y in range(NY) for p in range(2)]
+    for z in range(0, NZ, 2)
+    for c in range(NC)
+]
 
 
 def dot(a, b):
@@ -53,8 +51,8 @@
 VMEM = pl.BlockSpec(memory_space=pltpu.VMEM)
 
 
-def params():
-    return pltpu.CompilerParams(vmem_limit_bytes=VMEM_LIMIT)
+def params(limit=60 * MIB):
+    return pltpu.CompilerParams(vmem_limit_bytes=limit)
 
 
 def together(*v):
@@ -68,6 +66,14 @@
         at = slice(k * half, (k + 1) * half)
         keep[at, :] = ref[pl.ds(pl.multiple_of(c * half, half), half), :]
         give[at, :] = ref[pl.ds(pl.multiple_of((1 - c) * half, half), half), :]
+
+
+def join_kernel(n0, n1, f0, f1, f2, f3, near, far):
+    some = n0.shape[0]
+    for k, ref in enumerate((n0, n1)):
+        near[k * some : (k + 1) * some, :] = ref[...]
+    for k, ref in enumerate((f0, f1, f2, f3)):
+        far[k * some : (k + 1) * some, :] = ref[...]
 
 
 def shrink_kernel(own, rank, place, index, p0, p1, p2, p3, q0, q1, a_n, a_f, t, low):
@@ -93,9 +99,13 @@
     total = jnp.zeros((t.shape[0], rank), F32)
     for k in range(own):
         total = jnp.where(index[...] == first + k, s[:, k * rank : (k + 1) * rank], total)
-    total = total.reshape(NX, NZ * half, rank)
-    some = NZ * half // 2
-    low[...] = jnp.concatenate([total[:, :some], total[:, some:]], 2)
+    some = NZ * half // 4
+    total = total.reshape(NX, 2, 2 * some, rank)
+    total = jnp.concatenate([total[:, :, :some], total[:, :, some:]], 3)
+    for b in range(NX):
+        for y in range(NY):
+            for p in range(2):
+                low[(b * NY + y) * 2 + p] = total[b, p]
 
 
 def gate_kernel(place, t, w_n, w_f, mine, o1, o2, o3):
@@ -120,8 +130,8 @@
 
     @pl.when(k == 0)
     def _():
-        v = jnp.sum(low[...].astype(F32).reshape(NX, NZ, rows // 2, 2 * rank), 1)
-        v = jnp.concatenate([v[:, :, :rank], v[:, :, rank:]], 1).reshape(NX * rows, rank)
+        v = jnp.sum(low[...].astype(F32).reshape(NX, NZ // 2, 2, rows // 4, 2 * rank), 1)
+        v = jnp.concatenate([v[:, :, :, :rank], v[:, :, :, rank:]], 2).reshape(NX * rows, rank)
         wide_low[...] = jnp.concatenate([v] * count, 1)
         total[...] = up[...]
 
@@ -172,7 +182,6 @@
     everyone = NX * rows
     shape = jax.ShapeDtypeStruct
 
-    a_n = a.reshape(width, own_a * rank)
     b_n = b.reshape(own_b * rank, hid)
     place = jnp.stack([x, z, y, c, w * own_a, n * own_b, (n ^ 1) * own_b]).astype(jnp.int32)
     column = lax.dynamic_index_in_dim(index.reshape(NX * NZ, 2, half), c, 1, keepdims=False).reshape(everyone, 1)
@@ -185,19 +194,26 @@
         out_shape=(shape((rows // 2, width), BF16),) * 2,
         in_specs=[SMEM] + [VMEM] * 4,
         out_specs=(VMEM,) * 2,
-        compiler_params=params(),
+        compiler_params=params(4 * MIB),
         name="pick",
     )(place, tokens, *quad)
-    a_n, far, near = together(a_n, far, near)
-    far, a_f, up = together(core(far), core(a_n), up)
-    pair, *fars, up_f = together(send_pair(near), *[send_x(far, -d) for d in (1, 2, 3)], core(up))
-    down, near, pair = together(down, near, pair)
-    near = jnp.concatenate([near, pair], 0)
-    far = jnp.concatenate([far] + fars, 0)
-    *pieces, down_f = together(near, *[send_x(near, -d) for d in (1, 2, 3)], far, send_pair(far), core(down))
+    far, up = together(core(far), up)
+    a_n = a.reshape(width, own_a * rank)
+    pair, *fars, a_f = together(send_pair(near), *[send_x(far, -d) for d in (1, 2, 3)], core(a_n))
+    near, far = pl.pallas_call(
+        join_kernel,
+        out_shape=(shape((rows, width), BF16), shape((everyone // 2, width), BF16)),
+        in_specs=[VMEM] * 6,
+        out_specs=(VMEM,) * 2,
+        compiler_params=params(4 * MIB),
+        name="join",
+    )(near, pair, far, *fars)
+    *pieces, up_f = together(near, *[send_x(near, -d) for d in (1, 2, 3)], far, send_pair(far), core(up))
+    down, gate = together(down, gate, up_f)[:2]
+    down_f = core(down)
     t, low = pl.pallas_call(
         functools.partial(shrink_kernel, own_a, rank),
-        out_shape=(shape((everyone, 2 * width), BF16),) + (shape((NX, rows // 2, 2 * rank), F32),),
+        out_shape=(shape((everyone, 2 * width), BF16),) + (shape((2 * NX * NY, rows // 4, 2 * rank), F32),),
         in_specs=[SMEM] + [VMEM] * 9,
         out_specs=(VMEM,) * 2,
         compiler_params=params(),
@@ -220,10 +236,11 @@
         name="gate",
     )(place, t, gate, gate_f)
 
-    low, *gates = together(
-        lax.all_to_all(low, "narrow", 0, 0, tiled=True, axis_index_groups=Y_GROUPS), *gates
-    )
-    low, t, *gates = together(send_home(jnp.sum(low, 0).astype(BF16)), t, *gates)
+    low, t, *gates = together(
+        lax.all_to_all(low, ("wide", "narrow"), 0, 0, tiled=True, axis_index_groups=HOME_GROUPS), t, *gates
+    )
+    low = lax.dynamic_slice_in_dim(low, y * 2 * NY, 2 * NY, 0)
+    low = jnp.sum(low, 0).astype(BF16)
     low = lax.all_to_all(jnp.broadcast_to(low, (NX * NZ,) + low.shape), "wide", 0, 0, tiled=True)
 
     up_part = pl.pallas_call(
@@ -261,7 +278,7 @@
         in_specs=[SMEM] + [VMEM] * 6,
         out_specs=(VMEM,) * 6,
         scratch_shapes=[pltpu.VMEM((everyone, hid), BF16)],
-        compiler_params=params(),
+        compiler_params=params(24 * MIB),
         name="mix",
     )(place, hidden, *[send_y(hidden, -e) for e in (1, 2, 3)], down, down_f)
     n1, n2, n3, f1 = together(send_x(n1, 1), send_x(n2, 2), send_x(n3, 3), send_pair(f1))

time: 190 us -> 172 us (0.905)
  waiting for transfers between devices: 61.7 us -> 51.2 us
  starting transfers between devices: 81.7 us -> 78.6 us
  Pallas kernels: 33.9 us -> 30.8 us
    all_to_all x1, starting transfers between devices: 12.2 us -> 6.49 us  [body(): lax.all_to_all(jnp.broadcast_to(low, (NX * NZ,) + low.shape), 'wide', 0,...]
    ppermute x12, waiting for transfers between devices: 30.2 us -> 25.2 us  [send_x(): lax.ppermute(v, 'wide', [(x * NZ + z, (x + d) % NX * NZ + z) for x in ran...]
    ppermute x7, starting transfers between devices: 4.91 us -> 9.57 us  [core(): return lax.ppermute(v, 'narrow', [(i, i ^ 1) for i in range(NY * NC)])]
    all_to_all x1, waiting for transfers between devices: 3.64 us -> 0.01 us  [body(): lax.all_to_all(jnp.broadcast_to(low, (NX * NZ,) + low.shape), 'wide', 0,...]
    all_to_all x1, starting transfers between devices: 4.36 us -> 7.89 us  [body(): lax.all_to_all(low, ('wide', 'narrow'), 0, 0, tiled=True, axis_index_grou...]
    ppermute x12, starting transfers between devices: 23.8 us -> 20.2 us  [send_x(): lax.ppermute(v, 'wide', [(x * NZ + z, (x + d) % NX * NZ + z) for x in ran...]
    ppermute x1 -> x0, starting transfers between devices: 3.46 us -> none  [send_home(): return lax.ppermute(v, ('wide', 'narrow'), moves)]
    ppermute x9, starting transfers between devices: 8 us -> 10.7 us  [send_y(): lax.ppermute(v, 'narrow', [(y * NC + c, (y + d) % NY * NC + c) for y in r...]
  transfers between devices with their start and end apart: 41 -> 40, of which waited for: 23 -> 21; matrix products, arithmetic and copies ran while one was open for 2% -> 3% of each run, Pallas kernels for 11% -> 12%
where the time goes in v3:
time: 172 us; the launch traced here: 171 us
  starting transfers between devices  78.6 us (46%)
  waiting for transfers between devices  51.2 us (30%)
  Pallas kernels  30.8 us (18%)
  local copies, waits for them, and re-layouts  7.76 us (5%)
  other arithmetic  2.45 us (1%)
    ppermute x12, waiting for transfers between devices, send_x(): lax.ppermute(v, 'wide', [(x * NZ + z, (x + d) % NX * NZ + z) for x in ran...  25.2 us
    ppermute x12, starting transfers between devices, send_x(): lax.ppermute(v, 'wide', [(x * NZ + z, (x + d) % NX * NZ + z) for x in ran...  20.2 us
    ppermute x6, starting transfers between devices, send_z(): lax.ppermute(v, 'wide', [(x * NZ + z, x * NZ + (z + d) % NZ) for x in ran...  18.7 us
    ppermute x9, waiting for transfers between devices, send_y(): lax.ppermute(v, 'narrow', [(y * NC + c, (y + d) % NY * NC + c) for y in r...  13.5 us
    ppermute x9, starting transfers between devices, send_y(): lax.ppermute(v, 'narrow', [(y * NC + c, (y + d) % NY * NC + c) for y in r...  10.7 us
    ppermute x7, starting transfers between devices, core(): return lax.ppermute(v, 'narrow', [(i, i ^ 1) for i in range(NY * NC)])  9.57 us
    pallas_call x1, Pallas kernels, body(): pl.pallas_call(functools.partial(up_kernel, rank), out_shape=blocks, grid...  9.18 us
    ppermute x6, waiting for transfers between devices, send_z(): lax.ppermute(v, 'wide', [(x * NZ + z, x * NZ + (z + d) % NZ) for x in ran...  8.56 us
  transfers between devices with their start and end apart: 40, of which 21 were waited for; matrix products, arithmetic and copies ran while one was open for 3% of the time, Pallas kernels for 12%

profile of v3, /device:TPU:9, one launch (start us, length us, event | category | flops | bytes accessed | tf_op | source)
XLA Modules:
  0.0 171.0 jit_solution(16630043573976955398)
XLA Ops:
  0.7 6.9 %collective-permute-start.1 = (bf16[32,1024]{1,0:T(8,128)(2,1)}, bf16[32,1024]{1,0:T(8,128)(2,1)S(1)}, u32[]{:S(2)}, u32[]{:S(2)}) collective-permute-start(bf16[32,1024]{1,0:T(8,128)(2,1)} %q0.1), channel_id=1, source_target_pairs={{0,32},{8,40},{16,48},{24,56},{32,0},{40,8},{48,16},{56,24},{64,96... | collective-permute-start | bytes 196616 | tf_op jit(solution)/shard_map/ppermute | solution.py:24
  7.6 2.4 %collective-permute-start.2 = (bf16[32,1024]{1,0:T(8,128)(2,1)}, bf16[32,1024]{1,0:T(8,128)(2,1)S(1)}, u32[]{:S(2)}, u32[]{:S(2)}) collective-permute-start(bf16[32,1024]{1,0:T(8,128)(2,1)} %q0.1), channel_id=1, source_target_pairs={{0,16},{8,24},{16,32},{24,40},{32,48},{40,56},{48,0},{56,8},{64,80... | collective-permute-start | bytes 196616 | tf_op jit(solution)/shard_map/ppermute | solution.py:24
  11.0 4.0 %collective-permute-done.q1 = bf16[32,1024]{1,0:T(8,128)(2,1)S(1)} collective-permute-done((bf16[32,1024]{1,0:T(8,128)(2,1)}, bf16[32,1024]{1,0:T(8,128)(2,1)S(1)}, u32[]{:S(2)}, u32[]{:S(2)}) %collective-permute-start) | collective-permute-done | bytes 65568 | tf_op jit(solution)/shard_map/ppermute | solution.py:24
  15.0 1.2 copy-done.7
  19.7 1.5 copy.9.a_n
  21.4 1.3 collective-permute-start.5
  22.7 1.2 collective-permute-start.9
  23.9 2.5 %collective-permute-start.8 = (bf16[64,1024]{1,0:T(8,128)(2,1)S(1)}, bf16[64,1024]{1,0:T(8,128)(2,1)S(1)}, u32[]{:S(2)}, u32[]{:S(2)}) collective-permute-start(bf16[64,1024]{1,0:T(8,128)(2,1)S(1)} %collective-permute-done.6.f0), channel_id=1, source_target_pairs={{0,128},{8,136},{16,144},{24,152},{32,160},{40,168},{48,176},{56,1... | collective-permute-start | bytes 393224 | tf_op jit(solution)/shard_map/ppermute | solution.py:20
  26.4 1.2 collective-permute-start.7
  28.3 3.8 %collective-permute-done.8.f2 = bf16[64,1024]{1,0:T(8,128)(2,1)S(1)} collective-permute-done((bf16[64,1024]{1,0:T(8,128)(2,1)S(1)}, bf16[64,1024]{1,0:T(8,128)(2,1)S(1)}, u32[]{:S(2)}, u32[]{:S(2)}) %collective-permute-start.8) | collective-permute-done | bytes 131104 | tf_op jit(solution)/shard_map/ppermute | solution.py:20
  32.5 2.8 %collective-permute-start.13 = (bf16[128,1024]{1,0:T(8,128)(2,1)S(1)}, bf16[128,1024]{1,0:T(8,128)(2,1)}, u32[]{:S(2)}, u32[]{:S(2)}) collective-permute-start(bf16[128,1024]{1,0:T(8,128)(2,1)S(1)} %get-tuple-element.80.p0), channel_id=1, source_target_pairs={{0,64},{8,72},{16,80},{24,88},{32,96},{40,104},{48,112},{56,120},{... | collective-permute-start | bytes 786440 | tf_op jit(solution)/shard_map/ppermute | solution.py:20
  35.2 1.3 collective-permute-start.12
  38.5 1.6 collective-permute-done.13.p3
  40.1 7.2 %collective-permute-done.12.p2 = bf16[128,1024]{1,0:T(8,128)(2,1)} collective-permute-done((bf16[128,1024]{1,0:T(8,128)(2,1)S(1)}, bf16[128,1024]{1,0:T(8,128)(2,1)}, u32[]{:S(2)}, u32[]{:S(2)}) %collective-permute-start.12) | collective-permute-done | bytes 262176 | tf_op jit(solution)/shard_map/ppermute | solution.py:20
  48.1 5.0 %shrink.1 = (bf16[512,2048]{1,0:T(8,128)(2,1)}, f32[32,32,128]{2,1,0:T(8,128)}) custom-call(s32[7]{0:T(128)} %copy-done.4, s32[512,1]{1,0:T(8,128)} %copy.10.index, bf16[128,1024]{1,0:T(8,128)(2,1)} %copy-done.2, bf16[128,1024]{1,0:T(8,128)(2,1)} %collective-permute-done.11.p1, bf16[128,1024]{1,0:T(8,128)(2,1)} %collective-permute-done.12.p2, ...), custom_call_target="tpu_custom_call" | custom-call | tf_op jit(solution)/shard_map/shrink/pallas_call | solution.py:214
  53.1 7.9 %all-to-all-start = ((f32[32,32,128]{2,1,0:T(8,128)}), f32[32,32,128]{2,1,0:T(8,128)S(1)}, u32[]{:S(2)}, u32[]{:S(2)}) async-start(f32[32,32,128]{2,1,0:T(8,128)} %get-tuple-element.87), calls=%async_computation | async-start | bytes 1048576 | tf_op jit(solution)/shard_map/all_to_all | solution.py:240
  61.1 1.8 %collective-permute-start.25 = (bf16[896,1024]{1,0:T(8,128)(2,1)S(1)}, bf16[896,1024]{1,0:T(8,128)(2,1)}, u32[]{:S(2)}, u32[]{:S(2)}) collective-permute-start(bf16[896,1024]{1,0:T(8,128)(2,1)S(1)} %copy-done), channel_id=1, source_target_pairs={{0,1},{1,0},{2,3},{3,2},{4,5},{5,4},{6,7},{7,6},{8,9},{9,8},{10,11... | collective-permute-start | bytes 5505032 | tf_op jit(solution)/shard_map/ppermute | solution.py:36
  62.8 5.8 %gate.1 = (f32[128,896]{1,0:T(8,128)}, bf16[128,896]{1,0:T(8,128)(2,1)}, bf16[128,896]{1,0:T(8,128)(2,1)}, bf16[128,896]{1,0:T(8,128)(2,1)}) custom-call(s32[7]{0:T(128)} %copy-done.4, bf16[512,2048]{1,0:T(8,128)(2,1)} %get-tuple-element.101.t, bf16[1024,896]{1,0:T(8,128)(2,1)} %w_n, bf16[1024,896]{1,0:T(8,128)(2,1)} %copy-done.7), custom_call_target="tpu_custom_call" | custom-call | tf_op jit(solution)/shard_map/gate/pallas_call | solution.py:230
  68.6 2.1 %all-to-all-done = f32[32,32,128]{2,1,0:T(8,128)S(1)} async-done(((f32[32,32,128]{2,1,0:T(8,128)}), f32[32,32,128]{2,1,0:T(8,128)S(1)}, u32[]{:S(2)}, u32[]{:S(2)}) %all-to-all-start) | async-done | bytes 524320 | tf_op jit(solution)/shard_map/all_to_all | solution.py:240
  71.5 6.5 %all-to-all-start.1 = ((bf16[32,32,128]{2,1,0:T(8,128)(2,1)}), bf16[32,32,128]{2,1,0:T(8,128)(2,1)S(1)}, u32[]{:S(2)}, u32[]{:S(2)}) async-start(bf16[32,32,128]{2,1,0:T(8,128)(2,1)} %broadcast_in_dim.3), calls=%async_computation.1 | async-start | bytes 524288 | tf_op jit(solution)/shard_map/all_to_all | solution.py:244
  79.0 2.3 %collective-permute-start.17 = (bf16[128,896]{1,0:T(8,128)(2,1)}, bf16[128,896]{1,0:T(8,128)(2,1)S(1)}, u32[]{:S(2)}, u32[]{:S(2)}) collective-permute-start(bf16[128,896]{1,0:T(8,128)(2,1)} %get-tuple-element.98), channel_id=1, source_target_pairs={{0,4},{1,5},{2,6},{3,7},{4,0},{5,1},{6,2},{7,3},{8,12},{9,13},{10,... | collective-permute-start | bytes 688136 | tf_op jit(solution)/shard_map/ppermute | solution.py:28
  81.3 6.2 %base.1.up = f32[512,896]{1,0:T(8,128)} custom-call(bf16[512,2048]{1,0:T(8,128)(2,1)} %get-tuple-element.101.t, bf16[1024,896]{1,0:T(8,128)(2,1)} %w_n.1, bf16[1024,896]{1,0:T(8,128)(2,1)} %collective-permute-done.15.w_f), custom_call_target="tpu_custom_call" | custom-call | tf_op jit(solution)/shard_map/base/pallas_call | solution.py:246
  88.7 9.2 %up.1 = (f32[128,896]{1,0:T(8,128)}, bf16[128,896]{1,0:T(8,128)(2,1)}, bf16[128,896]{1,0:T(8,128)(2,1)}, bf16[128,896]{1,0:T(8,128)(2,1)}) custom-call(s32[7]{0:T(128)} %copy-done.4, s32[512,1]{1,0:T(8,128)} %copy.10.index, bf16[32,32,128]{2,1,0:T(8,128)(2,1)} %copy-done.9, f32[512,896]{1,0:T(8,128)} %base.1.up, bf16[2048,896]{1,0:T(8,128)(2,1)} %bitcast.10, ...), custom_call_target="tpu_custom_call" | custom-call | tf_op jit(solution)/shard_map/up/pallas_call | solution.py:259
  99.0 1.8 %collective-permute-start.20 = (bf16[128,896]{1,0:T(8,128)(2,1)}, bf16[128,896]{1,0:T(8,128)(2,1)S(1)}, u32[]{:S(2)}, u32[]{:S(2)}) collective-permute-start(bf16[128,896]{1,0:T(8,128)(2,1)} %get-tuple-element.105), channel_id=1, source_target_pairs={{0,4},{1,5},{2,6},{3,7},{4,0},{5,1},{6,2},{7,3},{8,12},{9,13},{10,... | collective-permute-start | bytes 688136 | tf_op jit(solution)/shard_map/ppermute | solution.py:28
  101.3 1.7 %collective-permute-done.19 = bf16[128,896]{1,0:T(8,128)(2,1)S(1)} collective-permute-done((bf16[128,896]{1,0:T(8,128)(2,1)}, bf16[128,896]{1,0:T(8,128)(2,1)S(1)}, u32[]{:S(2)}, u32[]{:S(2)}) %collective-permute-start.19) | collective-permute-done | bytes 229408 | tf_op jit(solution)/shard_map/ppermute | solution.py:28
  103.0 2.7 %collective-permute-done.20 = bf16[128,896]{1,0:T(8,128)(2,1)S(1)} collective-permute-done((bf16[128,896]{1,0:T(8,128)(2,1)}, bf16[128,896]{1,0:T(8,128)(2,1)S(1)}, u32[]{:S(2)}, u32[]{:S(2)}) %collective-permute-start.20) | collective-permute-done | bytes 229408 | tf_op jit(solution)/shard_map/ppermute | solution.py:28
  105.7 3.2 %collective-permute-done.21 = bf16[128,896]{1,0:T(8,128)(2,1)S(1)} collective-permute-done((bf16[128,896]{1,0:T(8,128)(2,1)}, bf16[128,896]{1,0:T(8,128)(2,1)S(1)}, u32[]{:S(2)}, u32[]{:S(2)}) %collective-permute-start.21) | collective-permute-done | bytes 229408 | tf_op jit(solution)/shard_map/ppermute | solution.py:28
  108.9 1.3 multiply_convert_fusion.h0
  110.6 1.4 collective-permute-start.23
  112.0 1.8 %collective-permute-start.22 = (bf16[128,896]{1,0:T(8,128)(2,1)S(1)}, bf16[128,896]{1,0:T(8,128)(2,1)S(1)}, u32[]{:S(2)}, u32[]{:S(2)}) collective-permute-start(bf16[128,896]{1,0:T(8,128)(2,1)S(1)} %multiply_convert_fusion.h0), channel_id=1, source_target_pairs={{0,6},{1,7},{2,0},{3,1},{4,2},{5,3},{6,4},{7,5},{8,14},{9,15},{10,... | collective-permute-start | bytes 688136 | tf_op jit(solution)/shard_map/ppermute | solution.py:28
  113.8 1.3 collective-permute-done.24.h3
  115.1 2.0 %collective-permute-done.23.h2 = bf16[128,896]{1,0:T(8,128)(2,1)S(1)} collective-permute-done((bf16[128,896]{1,0:T(8,128)(2,1)S(1)}, bf16[128,896]{1,0:T(8,128)(2,1)S(1)}, u32[]{:S(2)}, u32[]{:S(2)}) %collective-permute-start.23) | collective-permute-done | bytes 229408 | tf_op jit(solution)/shard_map/ppermute | solution.py:28
  117.1 2.5 %collective-permute-done.22.h1 = bf16[128,896]{1,0:T(8,128)(2,1)S(1)} collective-permute-done((bf16[128,896]{1,0:T(8,128)(2,1)S(1)}, bf16[128,896]{1,0:T(8,128)(2,1)S(1)}, u32[]{:S(2)}, u32[]{:S(2)}) %collective-permute-start.22) | collective-permute-done | bytes 229408 | tf_op jit(solution)/shard_map/ppermute | solution.py:28
  119.7 3.9 %mix.1 = (f32[128,1024]{1,0:T(8,128)S(1)}, bf16[128,1024]{1,0:T(8,128)(2,1)S(1)}, bf16[128,1024]{1,0:T(8,128)(2,1)S(1)}, bf16[128,1024]{1,0:T(8,128)(2,1)S(1)}, ...) custom-call(s32[7]{0:T(128)S(1)} %copy-done.5, bf16[128,896]{1,0:T(8,128)(2,1)S(1)} %multiply_convert_fusion.h0, ...), custom_call_target="tpu_custom_call" | custom-call | tf_op jit(solution)/shard_map/mix/pallas_call | solution.py:273
  123.6 3.2 %collective-permute-start.29 = (bf16[256,1024]{1,0:T(8,128)(2,1)S(1)}, bf16[256,1024]{1,0:T(8,128)(2,1)S(1)}, u32[]{:S(2)}, u32[]{:S(2)}) collective-permute-start(bf16[256,1024]{1,0:T(8,128)(2,1)S(1)} %get-tuple-element.112), channel_id=1, source_target_pairs={{0,8},{8,0},{16,24},{24,16},{32,40},{40,32},{48,56},{56,48},{64,72... | collective-permute-start | bytes 1572872 | tf_op jit(solution)/shard_map/ppermute | solution.py:32
  126.7 2.8 %collective-permute-start.26 = (bf16[128,1024]{1,0:T(8,128)(2,1)S(1)}, bf16[128,1024]{1,0:T(8,128)(2,1)S(1)}, u32[]{:S(2)}, u32[]{:S(2)}) collective-permute-start(bf16[128,1024]{1,0:T(8,128)(2,1)S(1)} %get-tuple-element.109), channel_id=1, source_target_pairs={{0,64},{8,72},{16,80},{24,88},{32,96},{40,104},{48,112},{56,120},{... | collective-permute-start | bytes 786440 | tf_op jit(solution)/shard_map/ppermute | solution.py:20
  129.6 2.4 %collective-permute-start.27 = (bf16[128,1024]{1,0:T(8,128)(2,1)S(1)}, bf16[128,1024]{1,0:T(8,128)(2,1)S(1)}, u32[]{:S(2)}, u32[]{:S(2)}) collective-permute-start(bf16[128,1024]{1,0:T(8,128)(2,1)S(1)} %get-tuple-element.110), channel_id=1, source_target_pairs={{0,128},{8,136},{16,144},{24,152},{32,160},{40,168},{48,176},{56,1... | collective-permute-start | bytes 786440 | tf_op jit(solution)/shard_map/ppermute | solution.py:20
  133.1 1.5 collective-permute-done.26
  134.6 5.4 %collective-permute-done.27 = bf16[128,1024]{1,0:T(8,128)(2,1)S(1)} collective-permute-done((bf16[128,1024]{1,0:T(8,128)(2,1)S(1)}, bf16[128,1024]{1,0:T(8,128)(2,1)S(1)}, u32[]{:S(2)}, u32[]{:S(2)}) %collective-permute-start.27) | collective-permute-done | bytes 262176 | tf_op jit(solution)/shard_map/ppermute | solution.py:20
  140.6 2.1 %collective-permute-start.33 = (bf16[64,1024]{1,0:T(8,128)(2,1)S(1)}, bf16[64,1024]{1,0:T(8,128)(2,1)S(1)}, u32[]{:S(2)}, u32[]{:S(2)}) collective-permute-start(bf16[64,1024]{1,0:T(8,128)(2,1)S(1)} %get-tuple-element.127), channel_id=1, source_target_pairs={{0,192},{8,200},{16,208},{24,216},{32,224},{40,232},{48,240},{56,2... | collective-permute-start | bytes 393224 | tf_op jit(solution)/shard_map/ppermute | solution.py:20
  142.7 1.7 %collective-permute-start.32 = (bf16[64,1024]{1,0:T(8,128)(2,1)S(1)}, bf16[64,1024]{1,0:T(8,128)(2,1)S(1)}, u32[]{:S(2)}, u32[]{:S(2)}) collective-permute-start(bf16[64,1024]{1,0:T(8,128)(2,1)S(1)} %get-tuple-element.128), channel_id=1, source_target_pairs={{0,128},{8,136},{16,144},{24,152},{32,160},{40,168},{48,176},{56,1... | collective-permute-start | bytes 393224 | tf_op jit(solution)/shard_map/ppermute | solution.py:20
  145.0 3.0 %collective-permute-done.32 = bf16[64,1024]{1,0:T(8,128)(2,1)S(1)} collective-permute-done((bf16[64,1024]{1,0:T(8,128)(2,1)S(1)}, bf16[64,1024]{1,0:T(8,128)(2,1)S(1)}, u32[]{:S(2)}, u32[]{:S(2)}) %collective-permute-start.32) | collective-permute-done | bytes 131104 | tf_op jit(solution)/shard_map/ppermute | solution.py:20
  148.1 1.4 collective-permute-done.31
  149.7 6.4 %collective-permute-start.36 = (bf16[16,2048]{1,0:T(8,128)(2,1)S(1)}, bf16[16,2048]{1,0:T(8,128)(2,1)S(1)}, u32[]{:S(2)}, u32[]{:S(2)}) collective-permute-start(bf16[16,2048]{1,0:T(8,128)(2,1)S(1)} %get-tuple-element.130), channel_id=1, source_target_pairs={{0,48},{8,56},{16,0},{24,8},{32,16},{40,24},{48,32},{56,40},{64,11... | collective-permute-start | bytes 196616 | tf_op jit(solution)/shard_map/ppermute | solution.py:24
  156.1 1.5 collective-permute-start.35
  157.6 1.5 collective-permute-start.34
  159.1 4.2 %collective-permute-done.35 = bf16[16,2048]{1,0:T(8,128)(2,1)S(1)} collective-permute-done((bf16[16,2048]{1,0:T(8,128)(2,1)S(1)}, bf16[16,2048]{1,0:T(8,128)(2,1)S(1)}, u32[]{:S(2)}, u32[]{:S(2)}) %collective-permute-start.35) | collective-permute-done | bytes 65568 | tf_op jit(solution)/shard_map/ppermute | solution.py:24
  163.6 5.9 %collective-permute-start.37 = (bf16[16,1024]{1,0:T(8,128)(2,1)S(1)}, bf16[16,1024]{1,0:T(8,128)(2,1)S(1)}, u32[]{:S(2)}, u32[]{:S(2)}) collective-permute-start(bf16[16,1024]{1,0:T(8,128)(2,1)S(1)} %get-tuple-element.134), channel_id=1, source_target_pairs={{0,1},{1,0},{2,3},{3,2},{4,5},{5,4},{6,7},{7,6},{8,9},{9,8},{10,11... | collective-permute-start | bytes 98312 | tf_op jit(solution)/shard_map/ppermute | solution.py:36
  (84 shorter events, 18.4 us)
Async XLA Ops:
  0.0 16.3 %collective-permute-start.3 = (bf16[2048,896]{1,0:T(8,128)(2,1)}, bf16[2048,896]{1,0:T(8,128)(2,1)}, u32[]{:S(2)}, u32[]{:S(2)}) collective-permute-start(bf16[2048,896]{1,0:T(8,128)(2,1)} %bitcast.9), channel_id=1, source_target_pairs={{0,1},{1,0},{2,3},{3,2},{4,5},{5,4},{6,7},{7,6},{8,9},{9,8},{10,11... | collective-permute-start | bytes 11010056 | tf_op jit(solution)/shard_map/ppermute | solution.py:36
  0.7 14.4 %collective-permute-start.4 = (bf16[1024,896]{1,0:T(8,128)(2,1)}, bf16[1024,896]{1,0:T(8,128)(2,1)S(1)}, u32[]{:S(2)}, u32[]{:S(2)}) collective-permute-start(bf16[1024,896]{1,0:T(8,128)(2,1)} %w_n), channel_id=1, source_target_pairs={{0,1},{1,0},{2,3},{3,2},{4,5},{5,4},{6,7},{7,6},{8,9},{9,8},{10,11... | collective-permute-start | bytes 5505032 | tf_op jit(solution)/shard_map/ppermute | solution.py:36
  0.7 10.3 %collective-permute-start.1 = (bf16[32,1024]{1,0:T(8,128)(2,1)}, bf16[32,1024]{1,0:T(8,128)(2,1)S(1)}, u32[]{:S(2)}, u32[]{:S(2)}) collective-permute-start(bf16[32,1024]{1,0:T(8,128)(2,1)} %q0.1), channel_id=1, source_target_pairs={{0,32},{8,40},{16,48},{24,56},{32,0},{40,8},{48,16},{56,24},{64,96... | collective-permute-start | bytes 196616 | tf_op jit(solution)/shard_map/ppermute | solution.py:24
  7.6 7.4 %collective-permute-start = (bf16[32,1024]{1,0:T(8,128)(2,1)}, bf16[32,1024]{1,0:T(8,128)(2,1)S(1)}, u32[]{:S(2)}, u32[]{:S(2)}) collective-permute-start(bf16[32,1024]{1,0:T(8,128)(2,1)} %q0.1), channel_id=1, source_target_pairs={{0,48},{8,56},{16,0},{24,8},{32,16},{40,24},{48,32},{56,40},{64,11... | collective-permute-start | bytes 196616 | tf_op jit(solution)/shard_map/ppermute | solution.py:24
  7.6 7.4 %collective-permute-start.2 = (bf16[32,1024]{1,0:T(8,128)(2,1)}, bf16[32,1024]{1,0:T(8,128)(2,1)S(1)}, u32[]{:S(2)}, u32[]{:S(2)}) collective-permute-start(bf16[32,1024]{1,0:T(8,128)(2,1)} %q0.1), channel_id=1, source_target_pairs={{0,16},{8,24},{16,32},{24,40},{32,48},{40,56},{48,0},{56,8},{64,80... | collective-permute-start | bytes 196616 | tf_op jit(solution)/shard_map/ppermute | solution.py:24
  11.0 36.4 %copy-start.4 = (s32[7]{0:T(128)}, s32[7]{0:T(128)S(1)}, u32[]{:S(2)}) copy-start(s32[7]{0:T(128)S(1)} %stack.31.place) | copy-start | bytes 88
  17.7 1.6 collective-permute-start.6
  19.3 28.0 %collective-permute-start.15 = (bf16[1024,896]{1,0:T(8,128)(2,1)}, bf16[1024,896]{1,0:T(8,128)(2,1)}, u32[]{:S(2)}, u32[]{:S(2)}) collective-permute-start(bf16[1024,896]{1,0:T(8,128)(2,1)} %w_n.1), channel_id=1, source_target_pairs={{0,1},{1,0},{2,3},{3,2},{4,5},{5,4},{6,7},{7,6},{8,9},{9,8},{10,11... | collective-permute-start | bytes 5505032 | tf_op jit(solution)/shard_map/ppermute | solution.py:36
  21.2 5.2 %collective-permute-start.10 = (bf16[1024,512]{1,0:T(8,128)(2,1)S(1)}, bf16[1024,512]{1,0:T(8,128)(2,1)S(1)}, u32[]{:S(2)}, u32[]{:S(2)}) collective-permute-start(bf16[1024,512]{1,0:T(8,128)(2,1)S(1)} %copy.9.a_n), channel_id=1, source_target_pairs={{0,1},{1,0},{2,3},{3,2},{4,5},{5,4},{6,7},{7,6},{8,9},{9,8},{10,11... | collective-permute-start | bytes 3145736 | tf_op jit(solution)/shard_map/ppermute | solution.py:36
  21.4 6.2 %collective-permute-start.5 = (bf16[64,1024]{1,0:T(8,128)(2,1)S(1)}, bf16[64,1024]{1,0:T(8,128)(2,1)S(1)}, u32[]{:S(2)}, u32[]{:S(2)}) collective-permute-start(bf16[64,1024]{1,0:T(8,128)(2,1)S(1)} %get-tuple-element.70.n0), channel_id=1, source_target_pairs={{0,8},{8,0},{16,24},{24,16},{32,40},{40,32},{48,56},{56,48},{64,72... | collective-permute-start | bytes 393224 | tf_op jit(solution)/shard_map/ppermute | solution.py:32
  22.7 5.6 %collective-permute-start.9 = (bf16[64,1024]{1,0:T(8,128)(2,1)S(1)}, bf16[64,1024]{1,0:T(8,128)(2,1)S(1)}, u32[]{:S(2)}, u32[]{:S(2)}) collective-permute-start(bf16[64,1024]{1,0:T(8,128)(2,1)S(1)} %collective-permute-done.6.f0), channel_id=1, source_target_pairs={{0,64},{8,72},{16,80},{24,88},{32,96},{40,104},{48,112},{56,120},{... | collective-permute-start | bytes 393224 | tf_op jit(solution)/shard_map/ppermute | solution.py:20
  23.9 8.2 %collective-permute-start.8 = (bf16[64,1024]{1,0:T(8,128)(2,1)S(1)}, bf16[64,1024]{1,0:T(8,128)(2,1)S(1)}, u32[]{:S(2)}, u32[]{:S(2)}) collective-permute-start(bf16[64,1024]{1,0:T(8,128)(2,1)S(1)} %collective-permute-done.6.f0), channel_id=1, source_target_pairs={{0,128},{8,136},{16,144},{24,152},{32,160},{40,168},{48,176},{56,1... | collective-permute-start | bytes 393224 | tf_op jit(solution)/shard_map/ppermute | solution.py:20
  26.4 5.7 %copy-start.8 = (bf16[1024,512]{1,0:T(8,128)(2,1)}, bf16[1024,512]{1,0:T(8,128)(2,1)S(1)}, u32[]{:S(2)}) copy-start(bf16[1024,512]{1,0:T(8,128)(2,1)S(1)} %collective-permute-done.10.a_f) | copy-start | bytes 3145732
  26.4 5.7 %collective-permute-start.7 = (bf16[64,1024]{1,0:T(8,128)(2,1)S(1)}, bf16[64,1024]{1,0:T(8,128)(2,1)S(1)}, u32[]{:S(2)}, u32[]{:S(2)}) collective-permute-start(bf16[64,1024]{1,0:T(8,128)(2,1)S(1)} %collective-permute-done.6.f0), channel_id=1, source_target_pairs={{0,192},{8,200},{16,208},{24,216},{32,224},{40,232},{48,240},{56,2... | collective-permute-start | bytes 393224 | tf_op jit(solution)/shard_map/ppermute | solution.py:20
  32.2 15.2 %copy-start.1 = (bf16[256,1024]{1,0:T(8,128)(2,1)}, bf16[256,1024]{1,0:T(8,128)(2,1)S(1)}, u32[]{:S(2)}) copy-start(bf16[256,1024]{1,0:T(8,128)(2,1)S(1)} %get-tuple-element.84.q0) | copy-start | bytes 1572868
  32.2 15.2 %copy-start.2 = (bf16[128,1024]{1,0:T(8,128)(2,1)}, bf16[128,1024]{1,0:T(8,128)(2,1)S(1)}, u32[]{:S(2)}) copy-start(bf16[128,1024]{1,0:T(8,128)(2,1)S(1)} %get-tuple-element.80.p0) | copy-start | bytes 786436
  32.2 15.1 %collective-permute-start.14 = (bf16[256,1024]{1,0:T(8,128)(2,1)S(1)}, bf16[256,1024]{1,0:T(8,128)(2,1)S(1)}, u32[]{:S(2)}, u32[]{:S(2)}) collective-permute-start(bf16[256,1024]{1,0:T(8,128)(2,1)S(1)} %get-tuple-element.84.q0), channel_id=1, source_target_pairs={{0,8},{8,0},{16,24},{24,16},{32,40},{40,32},{48,56},{56,48},{64,72... | collective-permute-start | bytes 1572872 | tf_op jit(solution)/shard_map/ppermute | solution.py:32
  32.5 7.6 %collective-permute-start.13 = (bf16[128,1024]{1,0:T(8,128)(2,1)S(1)}, bf16[128,1024]{1,0:T(8,128)(2,1)}, u32[]{:S(2)}, u32[]{:S(2)}) collective-permute-start(bf16[128,1024]{1,0:T(8,128)(2,1)S(1)} %get-tuple-element.80.p0), channel_id=1, source_target_pairs={{0,64},{8,72},{16,80},{24,88},{32,96},{40,104},{48,112},{56,120},{... | collective-permute-start | bytes 786440 | tf_op jit(solution)/shard_map/ppermute | solution.py:20
  35.2 12.1 %collective-permute-start.12 = (bf16[128,1024]{1,0:T(8,128)(2,1)S(1)}, bf16[128,1024]{1,0:T(8,128)(2,1)}, u32[]{:S(2)}, u32[]{:S(2)}) collective-permute-start(bf16[128,1024]{1,0:T(8,128)(2,1)S(1)} %get-tuple-element.80.p0), channel_id=1, source_target_pairs={{0,128},{8,136},{16,144},{24,152},{32,160},{40,168},{48,176},{56,1... | collective-permute-start | bytes 786440 | tf_op jit(solution)/shard_map/ppermute | solution.py:20
  36.5 10.8 %collective-permute-start.11 = (bf16[128,1024]{1,0:T(8,128)(2,1)S(1)}, bf16[128,1024]{1,0:T(8,128)(2,1)}, u32[]{:S(2)}, u32[]{:S(2)}) collective-permute-start(bf16[128,1024]{1,0:T(8,128)(2,1)S(1)} %get-tuple-element.80.p0), channel_id=1, source_target_pairs={{0,192},{8,200},{16,208},{24,216},{32,224},{40,232},{48,240},{56,2... | collective-permute-start | bytes 786440 | tf_op jit(solution)/shard_map/ppermute | solution.py:20
  38.5 22.6 %copy-start = (bf16[896,1024]{1,0:T(8,128)(2,1)S(1)}, bf16[896,1024]{1,0:T(8,128)(2,1)}, u32[]{:S(2)}) copy-start(bf16[896,1024]{1,0:T(8,128)(2,1)} %d_n) | copy-start | bytes 5505028
  53.1 17.6 %all-to-all-start = ((f32[32,32,128]{2,1,0:T(8,128)}), f32[32,32,128]{2,1,0:T(8,128)S(1)}, u32[]{:S(2)}, u32[]{:S(2)}) async-start(f32[32,32,128]{2,1,0:T(8,128)} %get-tuple-element.87), calls=%async_computation | async-start | bytes 1048576 | tf_op jit(solution)/shard_map/all_to_all | solution.py:240
  61.1 52.7 %collective-permute-start.25 = (bf16[896,1024]{1,0:T(8,128)(2,1)S(1)}, bf16[896,1024]{1,0:T(8,128)(2,1)}, u32[]{:S(2)}, u32[]{:S(2)}) collective-permute-start(bf16[896,1024]{1,0:T(8,128)(2,1)S(1)} %copy-done), channel_id=1, source_target_pairs={{0,1},{1,0},{2,3},{3,2},{4,5},{5,4},{6,7},{7,6},{8,9},{9,8},{10,11... | collective-permute-start | bytes 5505032 | tf_op jit(solution)/shard_map/ppermute | solution.py:36
  71.5 16.5 %all-to-all-start.1 = ((bf16[32,32,128]{2,1,0:T(8,128)(2,1)}), bf16[32,32,128]{2,1,0:T(8,128)(2,1)S(1)}, u32[]{:S(2)}, u32[]{:S(2)}) async-start(bf16[32,32,128]{2,1,0:T(8,128)(2,1)} %broadcast_in_dim.3), calls=%async_computation.1 | async-start | bytes 524288 | tf_op jit(solution)/shard_map/all_to_all | solution.py:244
  78.0 9.6 %copy-start.12 = (bf16[128,896]{1,0:T(8,128)(2,1)S(1)}, bf16[128,896]{1,0:T(8,128)(2,1)}, u32[]{:S(2)}) copy-start(bf16[128,896]{1,0:T(8,128)(2,1)} %get-tuple-element.99) | copy-start | bytes 688132
  78.0 21.0 %collective-permute-start.16 = (bf16[128,896]{1,0:T(8,128)(2,1)}, bf16[128,896]{1,0:T(8,128)(2,1)S(1)}, u32[]{:S(2)}, u32[]{:S(2)}) collective-permute-start(bf16[128,896]{1,0:T(8,128)(2,1)} %get-tuple-element.97), channel_id=1, source_target_pairs={{0,2},{1,3},{2,4},{3,5},{4,6},{5,7},{6,0},{7,1},{8,10},{9,11},{10,... | collective-permute-start | bytes 688136 | tf_op jit(solution)/shard_map/ppermute | solution.py:28
  79.0 21.8 %collective-permute-start.17 = (bf16[128,896]{1,0:T(8,128)(2,1)}, bf16[128,896]{1,0:T(8,128)(2,1)S(1)}, u32[]{:S(2)}, u32[]{:S(2)}) collective-permute-start(bf16[128,896]{1,0:T(8,128)(2,1)} %get-tuple-element.98), channel_id=1, source_target_pairs={{0,4},{1,5},{2,6},{3,7},{4,0},{5,1},{6,2},{7,3},{8,12},{9,13},{10,... | collective-permute-start | bytes 688136 | tf_op jit(solution)/shard_map/ppermute | solution.py:28
  87.6 21.3 %copy-start.11 = (f32[128,896]{1,0:T(8,128)S(1)}, f32[128,896]{1,0:T(8,128)}, u32[]{:S(2)}) copy-start(f32[128,896]{1,0:T(8,128)} %get-tuple-element.96) | copy-start | bytes 1376260
  87.6 13.7 %collective-permute-start.18 = (bf16[128,896]{1,0:T(8,128)(2,1)S(1)}, bf16[128,896]{1,0:T(8,128)(2,1)S(1)}, u32[]{:S(2)}, u32[]{:S(2)}) collective-permute-start(bf16[128,896]{1,0:T(8,128)(2,1)S(1)} %copy-done.12), channel_id=1, source_target_pairs={{0,6},{1,7},{2,0},{3,1},{4,2},{5,3},{6,4},{7,5},{8,14},{9,15},{10,... | collective-permute-start | bytes 688136 | tf_op jit(solution)/shard_map/ppermute | solution.py:28
  97.9 21.8 %copy-start.5 = (s32[7]{0:T(128)S(1)}, s32[7]{0:T(128)}, u32[]{:S(2)}) copy-start(s32[7]{0:T(128)} %copy-done.4) | copy-start | bytes 88
  97.9 5.1 %collective-permute-start.19 = (bf16[128,896]{1,0:T(8,128)(2,1)}, bf16[128,896]{1,0:T(8,128)(2,1)S(1)}, u32[]{:S(2)}, u32[]{:S(2)}) collective-permute-start(bf16[128,896]{1,0:T(8,128)(2,1)} %get-tuple-element.104), channel_id=1, source_target_pairs={{0,2},{1,3},{2,4},{3,5},{4,6},{5,7},{6,0},{7,1},{8,10},{9,11},{10,... | collective-permute-start | bytes 688136 | tf_op jit(solution)/shard_map/ppermute | solution.py:28
  99.0 6.7 %collective-permute-start.20 = (bf16[128,896]{1,0:T(8,128)(2,1)}, bf16[128,896]{1,0:T(8,128)(2,1)S(1)}, u32[]{:S(2)}, u32[]{:S(2)}) collective-permute-start(bf16[128,896]{1,0:T(8,128)(2,1)} %get-tuple-element.105), channel_id=1, source_target_pairs={{0,4},{1,5},{2,6},{3,7},{4,0},{5,1},{6,2},{7,3},{8,12},{9,13},{10,... | collective-permute-start | bytes 688136 | tf_op jit(solution)/shard_map/ppermute | solution.py:28
  100.8 8.0 %collective-permute-start.21 = (bf16[128,896]{1,0:T(8,128)(2,1)}, bf16[128,896]{1,0:T(8,128)(2,1)S(1)}, u32[]{:S(2)}, u32[]{:S(2)}) collective-permute-start(bf16[128,896]{1,0:T(8,128)(2,1)} %get-tuple-element.106), channel_id=1, source_target_pairs={{0,6},{1,7},{2,0},{3,1},{4,2},{5,3},{6,4},{7,5},{8,14},{9,15},{10,... | collective-permute-start | bytes 688136 | tf_op jit(solution)/shard_map/ppermute | solution.py:28
  110.2 4.9 %collective-permute-start.24 = (bf16[128,896]{1,0:T(8,128)(2,1)S(1)}, bf16[128,896]{1,0:T(8,128)(2,1)S(1)}, u32[]{:S(2)}, u32[]{:S(2)}) collective-permute-start(bf16[128,896]{1,0:T(8,128)(2,1)S(1)} %multiply_convert_fusion.h0), channel_id=1, source_target_pairs={{0,2},{1,3},{2,4},{3,5},{4,6},{5,7},{6,0},{7,1},{8,10},{9,11},{10,... | collective-permute-start | bytes 688136 | tf_op jit(solution)/shard_map/ppermute | solution.py:28
  110.6 6.5 %collective-permute-start.23 = (bf16[128,896]{1,0:T(8,128)(2,1)S(1)}, bf16[128,896]{1,0:T(8,128)(2,1)S(1)}, u32[]{:S(2)}, u32[]{:S(2)}) collective-permute-start(bf16[128,896]{1,0:T(8,128)(2,1)S(1)} %multiply_convert_fusion.h0), channel_id=1, source_target_pairs={{0,4},{1,5},{2,6},{3,7},{4,0},{5,1},{6,2},{7,3},{8,12},{9,13},{10,... | collective-permute-start | bytes 688136 | tf_op jit(solution)/shard_map/ppermute | solution.py:28
  112.0 7.6 %collective-permute-start.22 = (bf16[128,896]{1,0:T(8,128)(2,1)S(1)}, bf16[128,896]{1,0:T(8,128)(2,1)S(1)}, u32[]{:S(2)}, u32[]{:S(2)}) collective-permute-start(bf16[128,896]{1,0:T(8,128)(2,1)S(1)} %multiply_convert_fusion.h0), channel_id=1, source_target_pairs={{0,6},{1,7},{2,0},{3,1},{4,2},{5,3},{6,4},{7,5},{8,14},{9,15},{10,... | collective-permute-start | bytes 688136 | tf_op jit(solution)/shard_map/ppermute | solution.py:28
  123.6 16.4 %collective-permute-start.29 = (bf16[256,1024]{1,0:T(8,128)(2,1)S(1)}, bf16[256,1024]{1,0:T(8,128)(2,1)S(1)}, u32[]{:S(2)}, u32[]{:S(2)}) collective-permute-start(bf16[256,1024]{1,0:T(8,128)(2,1)S(1)} %get-tuple-element.112), channel_id=1, source_target_pairs={{0,8},{8,0},{16,24},{24,16},{32,40},{40,32},{48,56},{56,48},{64,72... | collective-permute-start | bytes 1572872 | tf_op jit(solution)/shard_map/ppermute | solution.py:32
  126.7 7.9 %collective-permute-start.26 = (bf16[128,1024]{1,0:T(8,128)(2,1)S(1)}, bf16[128,1024]{1,0:T(8,128)(2,1)S(1)}, u32[]{:S(2)}, u32[]{:S(2)}) collective-permute-start(bf16[128,1024]{1,0:T(8,128)(2,1)S(1)} %get-tuple-element.109), channel_id=1, source_target_pairs={{0,64},{8,72},{16,80},{24,88},{32,96},{40,104},{48,112},{56,120},{... | collective-permute-start | bytes 786440 | tf_op jit(solution)/shard_map/ppermute | solution.py:20
  129.6 10.4 %collective-permute-start.27 = (bf16[128,1024]{1,0:T(8,128)(2,1)S(1)}, bf16[128,1024]{1,0:T(8,128)(2,1)S(1)}, u32[]{:S(2)}, u32[]{:S(2)}) collective-permute-start(bf16[128,1024]{1,0:T(8,128)(2,1)S(1)} %get-tuple-element.110), channel_id=1, source_target_pairs={{0,128},{8,136},{16,144},{24,152},{32,160},{40,168},{48,176},{56,1... | collective-permute-start | bytes 786440 | tf_op jit(solution)/shard_map/ppermute | solution.py:20
  132.0 7.9 %collective-permute-start.28 = (bf16[128,1024]{1,0:T(8,128)(2,1)S(1)}, bf16[128,1024]{1,0:T(8,128)(2,1)S(1)}, u32[]{:S(2)}, u32[]{:S(2)}) collective-permute-start(bf16[128,1024]{1,0:T(8,128)(2,1)S(1)} %get-tuple-element.111), channel_id=1, source_target_pairs={{0,192},{8,200},{16,208},{24,216},{32,224},{40,232},{48,240},{56,2... | collective-permute-start | bytes 786440 | tf_op jit(solution)/shard_map/ppermute | solution.py:20
  140.1 4.3 %collective-permute-start.30 = (bf16[64,1024]{1,0:T(8,128)(2,1)S(1)}, bf16[64,1024]{1,0:T(8,128)(2,1)S(1)}, u32[]{:S(2)}, u32[]{:S(2)}) collective-permute-start(bf16[64,1024]{1,0:T(8,128)(2,1)S(1)} %slice.97), channel_id=1, source_target_pairs={{0,8},{8,0},{16,24},{24,16},{32,40},{40,32},{48,56},{56,48},{64,72... | collective-permute-start | bytes 393224 | tf_op jit(solution)/shard_map/ppermute | solution.py:32
  140.6 4.4 %collective-permute-start.33 = (bf16[64,1024]{1,0:T(8,128)(2,1)S(1)}, bf16[64,1024]{1,0:T(8,128)(2,1)S(1)}, u32[]{:S(2)}, u32[]{:S(2)}) collective-permute-start(bf16[64,1024]{1,0:T(8,128)(2,1)S(1)} %get-tuple-element.127), channel_id=1, source_target_pairs={{0,192},{8,200},{16,208},{24,216},{32,224},{40,232},{48,240},{56,2... | collective-permute-start | bytes 393224 | tf_op jit(solution)/shard_map/ppermute | solution.py:20
  142.7 5.3 %collective-permute-start.32 = (bf16[64,1024]{1,0:T(8,128)(2,1)S(1)}, bf16[64,1024]{1,0:T(8,128)(2,1)S(1)}, u32[]{:S(2)}, u32[]{:S(2)}) collective-permute-start(bf16[64,1024]{1,0:T(8,128)(2,1)S(1)} %get-tuple-element.128), channel_id=1, source_target_pairs={{0,128},{8,136},{16,144},{24,152},{32,160},{40,168},{48,176},{56,1... | collective-permute-start | bytes 393224 | tf_op jit(solution)/shard_map/ppermute | solution.py:20
  144.5 5.0 %collective-permute-start.31 = (bf16[64,1024]{1,0:T(8,128)(2,1)S(1)}, bf16[64,1024]{1,0:T(8,128)(2,1)S(1)}, u32[]{:S(2)}, u32[]{:S(2)}) collective-permute-start(bf16[64,1024]{1,0:T(8,128)(2,1)S(1)} %get-tuple-element.129), channel_id=1, source_target_pairs={{0,64},{8,72},{16,80},{24,88},{32,96},{40,104},{48,112},{56,120},{... | collective-permute-start | bytes 393224 | tf_op jit(solution)/shard_map/ppermute | solution.py:20
  149.7 9.4 %collective-permute-start.36 = (bf16[16,2048]{1,0:T(8,128)(2,1)S(1)}, bf16[16,2048]{1,0:T(8,128)(2,1)S(1)}, u32[]{:S(2)}, u32[]{:S(2)}) collective-permute-start(bf16[16,2048]{1,0:T(8,128)(2,1)S(1)} %get-tuple-element.130), channel_id=1, source_target_pairs={{0,48},{8,56},{16,0},{24,8},{32,16},{40,24},{48,32},{56,40},{64,11... | collective-permute-start | bytes 196616 | tf_op jit(solution)/shard_map/ppermute | solution.py:24
  156.1 7.2 %collective-permute-start.35 = (bf16[16,2048]{1,0:T(8,128)(2,1)S(1)}, bf16[16,2048]{1,0:T(8,128)(2,1)S(1)}, u32[]{:S(2)}, u32[]{:S(2)}) collective-permute-start(bf16[16,2048]{1,0:T(8,128)(2,1)S(1)} %get-tuple-element.131), channel_id=1, source_target_pairs={{0,32},{8,40},{16,48},{24,56},{32,0},{40,8},{48,16},{56,24},{64,96... | collective-permute-start | bytes 196616 | tf_op jit(solution)/shard_map/ppermute | solution.py:24
  157.6 6.0 %collective-permute-start.34 = (bf16[16,2048]{1,0:T(8,128)(2,1)S(1)}, bf16[16,2048]{1,0:T(8,128)(2,1)S(1)}, u32[]{:S(2)}, u32[]{:S(2)}) collective-permute-start(bf16[16,2048]{1,0:T(8,128)(2,1)S(1)} %get-tuple-element.132), channel_id=1, source_target_pairs={{0,16},{8,24},{16,32},{24,40},{32,48},{40,56},{48,0},{56,8},{64,80... | collective-permute-start | bytes 196616 | tf_op jit(solution)/shard_map/ppermute | solution.py:24
  163.6 6.8 %collective-permute-start.37 = (bf16[16,1024]{1,0:T(8,128)(2,1)S(1)}, bf16[16,1024]{1,0:T(8,128)(2,1)S(1)}, u32[]{:S(2)}, u32[]{:S(2)}) collective-permute-start(bf16[16,1024]{1,0:T(8,128)(2,1)S(1)} %get-tuple-element.134), channel_id=1, source_target_pairs={{0,1},{1,0},{2,3},{3,2},{4,5},{5,4},{6,7},{7,6},{8,9},{9,8},{10,11... | collective-permute-start | bytes 98312 | tf_op jit(solution)/shard_map/ppermute | solution.py:36
  (5 other events, 8.8 us)

commit v4 on v3

--- a/solution.py
+++ b/solution.py
@@ -57,6 +57,10 @@
 
 def together(*v):
     return lax.optimization_barrier(v)
+
+
+def in_hbm(*arrays):
+    return [pltpu.with_memory_space_constraint(v, pltpu.HBM) for v in arrays]
 
 
 def pick_kernel(place, q0, q1, q2, q3, keep, give):
@@ -196,7 +200,7 @@
         out_specs=(VMEM,) * 2,
         compiler_params=params(4 * MIB),
         name="pick",
-    )(place, tokens, *quad)
+    )(place, *in_hbm(tokens), *quad)
     far, up = together(core(far), up)
     a_n = a.reshape(width, own_a * rank)
     pair, *fars, a_f = together(send_pair(near), *[send_x(far, -d) for d in (1, 2, 3)], core(a_n))
@@ -263,9 +267,9 @@
             in_specs=[SMEM, fixed(everyone, 1), fixed(*low.shape), fixed(everyone, hid), part, part],
             out_specs=(fixed(rows, hid),) * 4,
             scratch_shapes=[pltpu.VMEM((everyone, hid), F32), pltpu.VMEM((everyone, own_b * rank // steps), F32)],
-            compiler_params=params(),
+            compiler_params=params(32 * MIB),
             name="up",
-        )(place, column, low, up_part, b_n, b_f)
+        )(place, column, low, *in_hbm(up_part, b_n, b_f))
     )
     hidden = (jax.nn.silu(gate_sum) * up_sum).astype(BF16)
 

time: 172 us -> 168 us (0.977)
    unnamed x26 -> x22, local copies, waits for them, and re-layouts: 3.58 us -> 2.07 us
where the time goes in v4:
time: 168 us
  starting transfers between devices  78.6 us (47%)
  waiting for transfers between devices  51.4 us (31%)
  Pallas kernels  29.9 us (18%)
  local copies, waits for them, and re-layouts  6.26 us (4%)
    ppermute x12, waiting for transfers between devices, send_x(): lax.ppermute(v, 'wide', [(x * NZ + z, (x + d) % NX * NZ + z) for x in ran...  25.2 us
    ppermute x12, starting transfers between devices, send_x(): lax.ppermute(v, 'wide', [(x * NZ + z, (x + d) % NX * NZ + z) for x in ran...  21.8 us
    ppermute x6, starting transfers between devices, send_z(): lax.ppermute(v, 'wide', [(x * NZ + z, x * NZ + (z + d) % NZ) for x in ran...  17.5 us
    ppermute x9, waiting for transfers between devices, send_y(): lax.ppermute(v, 'narrow', [(y * NC + c, (y + d) % NY * NC + c) for y in r...  13.7 us
    ppermute x9, starting transfers between devices, send_y(): lax.ppermute(v, 'narrow', [(y * NC + c, (y + d) % NY * NC + c) for y in r...  10.5 us
    ppermute x7, starting transfers between devices, core(): return lax.ppermute(v, 'narrow', [(i, i ^ 1) for i in range(NY * NC)])  9.34 us
    ppermute x6, waiting for transfers between devices, send_z(): lax.ppermute(v, 'wide', [(x * NZ + z, x * NZ + (z + d) % NZ) for x in ran...  8.56 us
    pallas_call x1, Pallas kernels, body(): pl.pallas_call(functools.partial(up_kernel, rank), out_shape=blocks, grid...  8.01 us
  transfers between devices with their start and end apart: 40, of which 21 were waited for; matrix products, arithmetic and copies ran while one was open for 3% of the time, Pallas kernels for 12%

profile of v4, /device:TPU:9, one launch (start us, length us, event | category | flops | bytes accessed | tf_op | source)
XLA Modules:
  0.0 167.9 jit_solution(5273022057349917280)
XLA Ops:
  0.7 6.9 %collective-permute-start.1 = (bf16[32,1024]{1,0:T(8,128)(2,1)}, bf16[32,1024]{1,0:T(8,128)(2,1)S(1)}, u32[]{:S(2)}, u32[]{:S(2)}) collective-permute-start(bf16[32,1024]{1,0:T(8,128)(2,1)} %q0.1), channel_id=1, source_target_pairs={{0,32},{8,40},{16,48},{24,56},{32,0},{40,8},{48,16},{56,24},{64,96... | collective-permute-start | bytes 196616 | tf_op jit(solution)/shard_map/ppermute | solution.py:24
  7.6 2.4 %collective-permute-start.2 = (bf16[32,1024]{1,0:T(8,128)(2,1)}, bf16[32,1024]{1,0:T(8,128)(2,1)S(1)}, u32[]{:S(2)}, u32[]{:S(2)}) collective-permute-start(bf16[32,1024]{1,0:T(8,128)(2,1)} %q0.1), channel_id=1, source_target_pairs={{0,16},{8,24},{16,32},{24,40},{32,48},{40,56},{48,0},{56,8},{64,80... | collective-permute-start | bytes 196616 | tf_op jit(solution)/shard_map/ppermute | solution.py:24
  11.0 4.0 %collective-permute-done.q1 = bf16[32,1024]{1,0:T(8,128)(2,1)S(1)} collective-permute-done((bf16[32,1024]{1,0:T(8,128)(2,1)}, bf16[32,1024]{1,0:T(8,128)(2,1)S(1)}, u32[]{:S(2)}, u32[]{:S(2)}) %collective-permute-start) | collective-permute-done | bytes 65568 | tf_op jit(solution)/shard_map/ppermute | solution.py:24
  15.0 1.3 copy-done.7
  19.2 1.5 copy.9.a_n
  20.9 1.3 collective-permute-start.5
  22.2 1.2 collective-permute-start.9
  23.4 2.5 %collective-permute-start.8 = (bf16[64,1024]{1,0:T(8,128)(2,1)S(1)}, bf16[64,1024]{1,0:T(8,128)(2,1)S(1)}, u32[]{:S(2)}, u32[]{:S(2)}) collective-permute-start(bf16[64,1024]{1,0:T(8,128)(2,1)S(1)} %collective-permute-done.6.f0), channel_id=1, source_target_pairs={{0,128},{8,136},{16,144},{24,152},{32,160},{40,168},{48,176},{56,1... | collective-permute-start | bytes 393224 | tf_op jit(solution)/shard_map/ppermute | solution.py:20
  25.9 1.2 collective-permute-start.7
  27.8 3.8 %collective-permute-done.8.f2 = bf16[64,1024]{1,0:T(8,128)(2,1)S(1)} collective-permute-done((bf16[64,1024]{1,0:T(8,128)(2,1)S(1)}, bf16[64,1024]{1,0:T(8,128)(2,1)S(1)}, u32[]{:S(2)}, u32[]{:S(2)}) %collective-permute-start.8) | collective-permute-done | bytes 131104 | tf_op jit(solution)/shard_map/ppermute | solution.py:20
  32.0 2.8 %collective-permute-start.13 = (bf16[128,1024]{1,0:T(8,128)(2,1)S(1)}, bf16[128,1024]{1,0:T(8,128)(2,1)}, u32[]{:S(2)}, u32[]{:S(2)}) collective-permute-start(bf16[128,1024]{1,0:T(8,128)(2,1)S(1)} %get-tuple-element.80.p0), channel_id=1, source_target_pairs={{0,64},{8,72},{16,80},{24,88},{32,96},{40,104},{48,112},{56,120},{... | collective-permute-start | bytes 786440 | tf_op jit(solution)/shard_map/ppermute | solution.py:20
  34.7 1.3 collective-permute-start.12
  36.0 1.1 collective-permute-start.11
  38.0 1.6 collective-permute-done.13.p3
  39.6 7.2 %collective-permute-done.12.p2 = bf16[128,1024]{1,0:T(8,128)(2,1)} collective-permute-done((bf16[128,1024]{1,0:T(8,128)(2,1)S(1)}, bf16[128,1024]{1,0:T(8,128)(2,1)}, u32[]{:S(2)}, u32[]{:S(2)}) %collective-permute-start.12) | collective-permute-done | bytes 262176 | tf_op jit(solution)/shard_map/ppermute | solution.py:20
  47.6 5.0 %shrink.1 = (bf16[512,2048]{1,0:T(8,128)(2,1)}, f32[32,32,128]{2,1,0:T(8,128)}) custom-call(s32[7]{0:T(128)} %copy-done.4, s32[512,1]{1,0:T(8,128)} %copy.10.index, bf16[128,1024]{1,0:T(8,128)(2,1)} %copy-done.3, bf16[128,1024]{1,0:T(8,128)(2,1)} %collective-permute-done.11.p1, bf16[128,1024]{1,0:T(8,128)(2,1)} %collective-permute-done.12.p2, ...), custom_call_target="tpu_custom_call" | custom-call | tf_op jit(solution)/shard_map/shrink/pallas_call | solution.py:218
  52.6 7.9 %all-to-all-start = ((f32[32,32,128]{2,1,0:T(8,128)}), f32[32,32,128]{2,1,0:T(8,128)S(1)}, u32[]{:S(2)}, u32[]{:S(2)}) async-start(f32[32,32,128]{2,1,0:T(8,128)} %get-tuple-element.87), calls=%async_computation | async-start | bytes 1048576 | tf_op jit(solution)/shard_map/all_to_all | solution.py:244
  60.5 1.8 %collective-permute-start.25 = (bf16[896,1024]{1,0:T(8,128)(2,1)S(1)}, bf16[896,1024]{1,0:T(8,128)(2,1)}, u32[]{:S(2)}, u32[]{:S(2)}) collective-permute-start(bf16[896,1024]{1,0:T(8,128)(2,1)S(1)} %copy-done.1), channel_id=1, source_target_pairs={{0,1},{1,0},{2,3},{3,2},{4,5},{5,4},{6,7},{7,6},{8,9},{9,8},{10,11... | collective-permute-start | bytes 5505032 | tf_op jit(solution)/shard_map/ppermute | solution.py:36
  62.3 5.7 %gate.1 = (f32[128,896]{1,0:T(8,128)}, bf16[128,896]{1,0:T(8,128)(2,1)}, bf16[128,896]{1,0:T(8,128)(2,1)}, bf16[128,896]{1,0:T(8,128)(2,1)}) custom-call(s32[7]{0:T(128)} %copy-done.4, bf16[512,2048]{1,0:T(8,128)(2,1)} %get-tuple-element.101.t, bf16[1024,896]{1,0:T(8,128)(2,1)} %w_n, bf16[1024,896]{1,0:T(8,128)(2,1)} %copy-done.7), custom_call_target="tpu_custom_call" | custom-call | tf_op jit(solution)/shard_map/gate/pallas_call | solution.py:234
  68.0 2.2 %all-to-all-done = f32[32,32,128]{2,1,0:T(8,128)S(1)} async-done(((f32[32,32,128]{2,1,0:T(8,128)}), f32[32,32,128]{2,1,0:T(8,128)S(1)}, u32[]{:S(2)}, u32[]{:S(2)}) %all-to-all-start) | async-done | bytes 524320 | tf_op jit(solution)/shard_map/all_to_all | solution.py:244
  71.0 6.5 %all-to-all-start.1 = ((bf16[32,32,128]{2,1,0:T(8,128)(2,1)}), bf16[32,32,128]{2,1,0:T(8,128)(2,1)S(1)}, u32[]{:S(2)}, u32[]{:S(2)}) async-start(bf16[32,32,128]{2,1,0:T(8,128)(2,1)} %broadcast_in_dim.3), calls=%async_computation.1 | async-start | bytes 524288 | tf_op jit(solution)/shard_map/all_to_all | solution.py:248
  78.5 2.3 %collective-permute-start.17 = (bf16[128,896]{1,0:T(8,128)(2,1)}, bf16[128,896]{1,0:T(8,128)(2,1)S(1)}, u32[]{:S(2)}, u32[]{:S(2)}) collective-permute-start(bf16[128,896]{1,0:T(8,128)(2,1)} %get-tuple-element.98), channel_id=1, source_target_pairs={{0,4},{1,5},{2,6},{3,7},{4,0},{5,1},{6,2},{7,3},{8,12},{9,13},{10,... | collective-permute-start | bytes 688136 | tf_op jit(solution)/shard_map/ppermute | solution.py:28
  80.8 6.3 %base.1.up = f32[512,896]{1,0:T(8,128)} custom-call(bf16[512,2048]{1,0:T(8,128)(2,1)} %get-tuple-element.101.t, bf16[1024,896]{1,0:T(8,128)(2,1)} %w_n.1, bf16[1024,896]{1,0:T(8,128)(2,1)} %collective-permute-done.15.w_f), custom_call_target="tpu_custom_call" | custom-call | tf_op jit(solution)/shard_map/base/pallas_call | solution.py:250
  87.5 8.0 %up.1 = (f32[128,896]{1,0:T(8,128)S(1)}, bf16[128,896]{1,0:T(8,128)(2,1)S(1)}, bf16[128,896]{1,0:T(8,128)(2,1)S(1)}, bf16[128,896]{1,0:T(8,128)(2,1)S(1)}) custom-call(s32[7]{0:T(128)S(1)} %copy-done.5, s32[512,1]{1,0:T(8,128)S(1)} %copy-done, bf16[32,32,128]{2,1,0:T(8,128)(2,1)S(1)} %all-to-all-done.1.low, f32[512,896]{1,0:T(8,128)} %base.1.up, ...), custom_call_target="tpu_custom_call" | custom-call | tf_op jit(solution)/shard_map/up/pallas_call | solution.py:263
  95.5 1.2 collective-permute-start.19
  96.8 1.9 %collective-permute-start.20 = (bf16[128,896]{1,0:T(8,128)(2,1)S(1)}, bf16[128,896]{1,0:T(8,128)(2,1)S(1)}, u32[]{:S(2)}, u32[]{:S(2)}) collective-permute-start(bf16[128,896]{1,0:T(8,128)(2,1)S(1)} %get-tuple-element.105), channel_id=1, source_target_pairs={{0,4},{1,5},{2,6},{3,7},{4,0},{5,1},{6,2},{7,3},{8,12},{9,13},{10,... | collective-permute-start | bytes 688136 | tf_op jit(solution)/shard_map/ppermute | solution.py:28
  98.9 1.6 collective-permute-done.19
  100.5 2.8 %collective-permute-done.20 = bf16[128,896]{1,0:T(8,128)(2,1)S(1)} collective-permute-done((bf16[128,896]{1,0:T(8,128)(2,1)S(1)}, bf16[128,896]{1,0:T(8,128)(2,1)S(1)}, u32[]{:S(2)}, u32[]{:S(2)}) %collective-permute-start.20) | collective-permute-done | bytes 229408 | tf_op jit(solution)/shard_map/ppermute | solution.py:28
  103.2 3.5 %collective-permute-done.21 = bf16[128,896]{1,0:T(8,128)(2,1)S(1)} collective-permute-done((bf16[128,896]{1,0:T(8,128)(2,1)S(1)}, bf16[128,896]{1,0:T(8,128)(2,1)S(1)}, u32[]{:S(2)}, u32[]{:S(2)}) %collective-permute-start.21) | collective-permute-done | bytes 229408 | tf_op jit(solution)/shard_map/ppermute | solution.py:28
  107.3 1.4 collective-permute-start.23
  108.7 1.8 %collective-permute-start.22 = (bf16[128,896]{1,0:T(8,128)(2,1)S(1)}, bf16[128,896]{1,0:T(8,128)(2,1)S(1)}, u32[]{:S(2)}, u32[]{:S(2)}) collective-permute-start(bf16[128,896]{1,0:T(8,128)(2,1)S(1)} %multiply_convert_fusion.h0), channel_id=1, source_target_pairs={{0,6},{1,7},{2,0},{3,1},{4,2},{5,3},{6,4},{7,5},{8,14},{9,15},{10,... | collective-permute-start | bytes 688136 | tf_op jit(solution)/shard_map/ppermute | solution.py:28
  110.5 1.5 collective-permute-done.24.h3
  112.0 1.8 %collective-permute-done.23.h2 = bf16[128,896]{1,0:T(8,128)(2,1)S(1)} collective-permute-done((bf16[128,896]{1,0:T(8,128)(2,1)S(1)}, bf16[128,896]{1,0:T(8,128)(2,1)S(1)}, u32[]{:S(2)}, u32[]{:S(2)}) %collective-permute-start.23) | collective-permute-done | bytes 229408 | tf_op jit(solution)/shard_map/ppermute | solution.py:28
  113.8 2.6 %collective-permute-done.22.h1 = bf16[128,896]{1,0:T(8,128)(2,1)S(1)} collective-permute-done((bf16[128,896]{1,0:T(8,128)(2,1)S(1)}, bf16[128,896]{1,0:T(8,128)(2,1)S(1)}, u32[]{:S(2)}, u32[]{:S(2)}) %collective-permute-start.22) | collective-permute-done | bytes 229408 | tf_op jit(solution)/shard_map/ppermute | solution.py:28
  116.3 3.9 %mix.1 = (f32[128,1024]{1,0:T(8,128)S(1)}, bf16[128,1024]{1,0:T(8,128)(2,1)S(1)}, bf16[128,1024]{1,0:T(8,128)(2,1)S(1)}, bf16[128,1024]{1,0:T(8,128)(2,1)S(1)}, ...) custom-call(s32[7]{0:T(128)S(1)} %copy-done.5, bf16[128,896]{1,0:T(8,128)(2,1)S(1)} %multiply_convert_fusion.h0, ...), custom_call_target="tpu_custom_call" | custom-call | tf_op jit(solution)/shard_map/mix/pallas_call | solution.py:277
  120.3 3.1 %collective-permute-start.29 = (bf16[256,1024]{1,0:T(8,128)(2,1)S(1)}, bf16[256,1024]{1,0:T(8,128)(2,1)S(1)}, u32[]{:S(2)}, u32[]{:S(2)}) collective-permute-start(bf16[256,1024]{1,0:T(8,128)(2,1)S(1)} %get-tuple-element.112), channel_id=1, source_target_pairs={{0,8},{8,0},{16,24},{24,16},{32,40},{40,32},{48,56},{56,48},{64,72... | collective-permute-start | bytes 1572872 | tf_op jit(solution)/shard_map/ppermute | solution.py:32
  123.4 2.6 %collective-permute-start.26 = (bf16[128,1024]{1,0:T(8,128)(2,1)S(1)}, bf16[128,1024]{1,0:T(8,128)(2,1)S(1)}, u32[]{:S(2)}, u32[]{:S(2)}) collective-permute-start(bf16[128,1024]{1,0:T(8,128)(2,1)S(1)} %get-tuple-element.109), channel_id=1, source_target_pairs={{0,64},{8,72},{16,80},{24,88},{32,96},{40,104},{48,112},{56,120},{... | collective-permute-start | bytes 786440 | tf_op jit(solution)/shard_map/ppermute | solution.py:20
  126.0 2.5 %collective-permute-start.27 = (bf16[128,1024]{1,0:T(8,128)(2,1)S(1)}, bf16[128,1024]{1,0:T(8,128)(2,1)S(1)}, u32[]{:S(2)}, u32[]{:S(2)}) collective-permute-start(bf16[128,1024]{1,0:T(8,128)(2,1)S(1)} %get-tuple-element.110), channel_id=1, source_target_pairs={{0,128},{8,136},{16,144},{24,152},{32,160},{40,168},{48,176},{56,1... | collective-permute-start | bytes 786440 | tf_op jit(solution)/shard_map/ppermute | solution.py:20
  129.7 1.5 collective-permute-done.26
  131.1 5.4 %collective-permute-done.27 = bf16[128,1024]{1,0:T(8,128)(2,1)S(1)} collective-permute-done((bf16[128,1024]{1,0:T(8,128)(2,1)S(1)}, bf16[128,1024]{1,0:T(8,128)(2,1)S(1)}, u32[]{:S(2)}, u32[]{:S(2)}) %collective-permute-start.27) | collective-permute-done | bytes 262176 | tf_op jit(solution)/shard_map/ppermute | solution.py:20
  137.3 2.1 %collective-permute-start.33 = (bf16[64,1024]{1,0:T(8,128)(2,1)S(1)}, bf16[64,1024]{1,0:T(8,128)(2,1)S(1)}, u32[]{:S(2)}, u32[]{:S(2)}) collective-permute-start(bf16[64,1024]{1,0:T(8,128)(2,1)S(1)} %get-tuple-element.127), channel_id=1, source_target_pairs={{0,192},{8,200},{16,208},{24,216},{32,224},{40,232},{48,240},{56,2... | collective-permute-start | bytes 393224 | tf_op jit(solution)/shard_map/ppermute | solution.py:20
  139.5 3.3 %collective-permute-start.32 = (bf16[64,1024]{1,0:T(8,128)(2,1)S(1)}, bf16[64,1024]{1,0:T(8,128)(2,1)S(1)}, u32[]{:S(2)}, u32[]{:S(2)}) collective-permute-start(bf16[64,1024]{1,0:T(8,128)(2,1)S(1)} %get-tuple-element.128), channel_id=1, source_target_pairs={{0,128},{8,136},{16,144},{24,152},{32,160},{40,168},{48,176},{56,1... | collective-permute-start | bytes 393224 | tf_op jit(solution)/shard_map/ppermute | solution.py:20
  143.4 1.8 %collective-permute-done.32 = bf16[64,1024]{1,0:T(8,128)(2,1)S(1)} collective-permute-done((bf16[64,1024]{1,0:T(8,128)(2,1)S(1)}, bf16[64,1024]{1,0:T(8,128)(2,1)S(1)}, u32[]{:S(2)}, u32[]{:S(2)}) %collective-permute-start.32) | collective-permute-done | bytes 131104 | tf_op jit(solution)/shard_map/ppermute | solution.py:20
  145.1 2.7 %collective-permute-done.31 = bf16[64,1024]{1,0:T(8,128)(2,1)S(1)} collective-permute-done((bf16[64,1024]{1,0:T(8,128)(2,1)S(1)}, bf16[64,1024]{1,0:T(8,128)(2,1)S(1)}, u32[]{:S(2)}, u32[]{:S(2)}) %collective-permute-start.31) | collective-permute-done | bytes 131104 | tf_op jit(solution)/shard_map/ppermute | solution.py:20
  148.0 4.6 %collective-permute-start.36 = (bf16[16,2048]{1,0:T(8,128)(2,1)S(1)}, bf16[16,2048]{1,0:T(8,128)(2,1)S(1)}, u32[]{:S(2)}, u32[]{:S(2)}) collective-permute-start(bf16[16,2048]{1,0:T(8,128)(2,1)S(1)} %get-tuple-element.130), channel_id=1, source_target_pairs={{0,48},{8,56},{16,0},{24,8},{32,16},{40,24},{48,32},{56,40},{64,11... | collective-permute-start | bytes 196616 | tf_op jit(solution)/shard_map/ppermute | solution.py:24
  152.6 2.8 %collective-permute-start.35 = (bf16[16,2048]{1,0:T(8,128)(2,1)S(1)}, bf16[16,2048]{1,0:T(8,128)(2,1)S(1)}, u32[]{:S(2)}, u32[]{:S(2)}) collective-permute-start(bf16[16,2048]{1,0:T(8,128)(2,1)S(1)} %get-tuple-element.131), channel_id=1, source_target_pairs={{0,32},{8,40},{16,48},{24,56},{32,0},{40,8},{48,16},{56,24},{64,96... | collective-permute-start | bytes 196616 | tf_op jit(solution)/shard_map/ppermute | solution.py:24
  156.2 3.5 %collective-permute-done.35 = bf16[16,2048]{1,0:T(8,128)(2,1)S(1)} collective-permute-done((bf16[16,2048]{1,0:T(8,128)(2,1)S(1)}, bf16[16,2048]{1,0:T(8,128)(2,1)S(1)}, u32[]{:S(2)}, u32[]{:S(2)}) %collective-permute-start.35) | collective-permute-done | bytes 65568 | tf_op jit(solution)/shard_map/ppermute | solution.py:24
  160.7 5.7 %collective-permute-start.37 = (bf16[16,1024]{1,0:T(8,128)(2,1)S(1)}, bf16[16,1024]{1,0:T(8,128)(2,1)S(1)}, u32[]{:S(2)}, u32[]{:S(2)}) collective-permute-start(bf16[16,1024]{1,0:T(8,128)(2,1)S(1)} %get-tuple-element.134), channel_id=1, source_target_pairs={{0,1},{1,0},{2,3},{3,2},{4,5},{5,4},{6,7},{7,6},{8,9},{9,8},{10,11... | collective-permute-start | bytes 98312 | tf_op jit(solution)/shard_map/ppermute | solution.py:36
  (80 shorter events, 16.4 us)
Async XLA Ops:
  0.0 16.3 %collective-permute-start.3 = (bf16[2048,896]{1,0:T(8,128)(2,1)}, bf16[2048,896]{1,0:T(8,128)(2,1)}, u32[]{:S(2)}, u32[]{:S(2)}) collective-permute-start(bf16[2048,896]{1,0:T(8,128)(2,1)} %bitcast.9), channel_id=1, source_target_pairs={{0,1},{1,0},{2,3},{3,2},{4,5},{5,4},{6,7},{7,6},{8,9},{9,8},{10,11... | collective-permute-start | bytes 11010056 | tf_op jit(solution)/shard_map/ppermute | solution.py:36
  0.7 14.4 %collective-permute-start.4 = (bf16[1024,896]{1,0:T(8,128)(2,1)}, bf16[1024,896]{1,0:T(8,128)(2,1)S(1)}, u32[]{:S(2)}, u32[]{:S(2)}) collective-permute-start(bf16[1024,896]{1,0:T(8,128)(2,1)} %w_n), channel_id=1, source_target_pairs={{0,1},{1,0},{2,3},{3,2},{4,5},{5,4},{6,7},{7,6},{8,9},{9,8},{10,11... | collective-permute-start | bytes 5505032 | tf_op jit(solution)/shard_map/ppermute | solution.py:36
  0.7 10.3 %collective-permute-start.1 = (bf16[32,1024]{1,0:T(8,128)(2,1)}, bf16[32,1024]{1,0:T(8,128)(2,1)S(1)}, u32[]{:S(2)}, u32[]{:S(2)}) collective-permute-start(bf16[32,1024]{1,0:T(8,128)(2,1)} %q0.1), channel_id=1, source_target_pairs={{0,32},{8,40},{16,48},{24,56},{32,0},{40,8},{48,16},{56,24},{64,96... | collective-permute-start | bytes 196616 | tf_op jit(solution)/shard_map/ppermute | solution.py:24
  7.6 7.4 %collective-permute-start = (bf16[32,1024]{1,0:T(8,128)(2,1)}, bf16[32,1024]{1,0:T(8,128)(2,1)S(1)}, u32[]{:S(2)}, u32[]{:S(2)}) collective-permute-start(bf16[32,1024]{1,0:T(8,128)(2,1)} %q0.1), channel_id=1, source_target_pairs={{0,48},{8,56},{16,0},{24,8},{32,16},{40,24},{48,32},{56,40},{64,11... | collective-permute-start | bytes 196616 | tf_op jit(solution)/shard_map/ppermute | solution.py:24
  7.6 7.4 %collective-permute-start.2 = (bf16[32,1024]{1,0:T(8,128)(2,1)}, bf16[32,1024]{1,0:T(8,128)(2,1)S(1)}, u32[]{:S(2)}, u32[]{:S(2)}) collective-permute-start(bf16[32,1024]{1,0:T(8,128)(2,1)} %q0.1), channel_id=1, source_target_pairs={{0,16},{8,24},{16,32},{24,40},{32,48},{40,56},{48,0},{56,8},{64,80... | collective-permute-start | bytes 196616 | tf_op jit(solution)/shard_map/ppermute | solution.py:24
  11.0 35.9 %copy-start.4 = (s32[7]{0:T(128)}, s32[7]{0:T(128)S(1)}, u32[]{:S(2)}) copy-start(s32[7]{0:T(128)S(1)} %stack.31.place) | copy-start | bytes 88
  17.2 1.6 collective-permute-start.6
  18.8 28.0 %collective-permute-start.15 = (bf16[1024,896]{1,0:T(8,128)(2,1)}, bf16[1024,896]{1,0:T(8,128)(2,1)}, u32[]{:S(2)}, u32[]{:S(2)}) collective-permute-start(bf16[1024,896]{1,0:T(8,128)(2,1)} %w_n.1), channel_id=1, source_target_pairs={{0,1},{1,0},{2,3},{3,2},{4,5},{5,4},{6,7},{7,6},{8,9},{9,8},{10,11... | collective-permute-start | bytes 5505032 | tf_op jit(solution)/shard_map/ppermute | solution.py:36
  20.7 5.2 %collective-permute-start.10 = (bf16[1024,512]{1,0:T(8,128)(2,1)S(1)}, bf16[1024,512]{1,0:T(8,128)(2,1)S(1)}, u32[]{:S(2)}, u32[]{:S(2)}) collective-permute-start(bf16[1024,512]{1,0:T(8,128)(2,1)S(1)} %copy.9.a_n), channel_id=1, source_target_pairs={{0,1},{1,0},{2,3},{3,2},{4,5},{5,4},{6,7},{7,6},{8,9},{9,8},{10,11... | collective-permute-start | bytes 3145736 | tf_op jit(solution)/shard_map/ppermute | solution.py:36
  20.9 6.2 %collective-permute-start.5 = (bf16[64,1024]{1,0:T(8,128)(2,1)S(1)}, bf16[64,1024]{1,0:T(8,128)(2,1)S(1)}, u32[]{:S(2)}, u32[]{:S(2)}) collective-permute-start(bf16[64,1024]{1,0:T(8,128)(2,1)S(1)} %get-tuple-element.70.n0), channel_id=1, source_target_pairs={{0,8},{8,0},{16,24},{24,16},{32,40},{40,32},{48,56},{56,48},{64,72... | collective-permute-start | bytes 393224 | tf_op jit(solution)/shard_map/ppermute | solution.py:32
  22.2 5.6 %collective-permute-start.9 = (bf16[64,1024]{1,0:T(8,128)(2,1)S(1)}, bf16[64,1024]{1,0:T(8,128)(2,1)S(1)}, u32[]{:S(2)}, u32[]{:S(2)}) collective-permute-start(bf16[64,1024]{1,0:T(8,128)(2,1)S(1)} %collective-permute-done.6.f0), channel_id=1, source_target_pairs={{0,64},{8,72},{16,80},{24,88},{32,96},{40,104},{48,112},{56,120},{... | collective-permute-start | bytes 393224 | tf_op jit(solution)/shard_map/ppermute | solution.py:20
  23.4 8.2 %collective-permute-start.8 = (bf16[64,1024]{1,0:T(8,128)(2,1)S(1)}, bf16[64,1024]{1,0:T(8,128)(2,1)S(1)}, u32[]{:S(2)}, u32[]{:S(2)}) collective-permute-start(bf16[64,1024]{1,0:T(8,128)(2,1)S(1)} %collective-permute-done.6.f0), channel_id=1, source_target_pairs={{0,128},{8,136},{16,144},{24,152},{32,160},{40,168},{48,176},{56,1... | collective-permute-start | bytes 393224 | tf_op jit(solution)/shard_map/ppermute | solution.py:20
  25.9 5.7 %copy-start.8 = (bf16[1024,512]{1,0:T(8,128)(2,1)}, bf16[1024,512]{1,0:T(8,128)(2,1)S(1)}, u32[]{:S(2)}) copy-start(bf16[1024,512]{1,0:T(8,128)(2,1)S(1)} %collective-permute-done.10.a_f) | copy-start | bytes 3145732
  25.9 5.7 %collective-permute-start.7 = (bf16[64,1024]{1,0:T(8,128)(2,1)S(1)}, bf16[64,1024]{1,0:T(8,128)(2,1)S(1)}, u32[]{:S(2)}, u32[]{:S(2)}) collective-permute-start(bf16[64,1024]{1,0:T(8,128)(2,1)S(1)} %collective-permute-done.6.f0), channel_id=1, source_target_pairs={{0,192},{8,200},{16,208},{24,216},{32,224},{40,232},{48,240},{56,2... | collective-permute-start | bytes 393224 | tf_op jit(solution)/shard_map/ppermute | solution.py:20
  31.7 15.2 %copy-start.2 = (bf16[256,1024]{1,0:T(8,128)(2,1)}, bf16[256,1024]{1,0:T(8,128)(2,1)S(1)}, u32[]{:S(2)}) copy-start(bf16[256,1024]{1,0:T(8,128)(2,1)S(1)} %get-tuple-element.84.q0) | copy-start | bytes 1572868
  31.7 15.2 %copy-start.3 = (bf16[128,1024]{1,0:T(8,128)(2,1)}, bf16[128,1024]{1,0:T(8,128)(2,1)S(1)}, u32[]{:S(2)}) copy-start(bf16[128,1024]{1,0:T(8,128)(2,1)S(1)} %get-tuple-element.80.p0) | copy-start | bytes 786436
  31.7 15.1 %collective-permute-start.14 = (bf16[256,1024]{1,0:T(8,128)(2,1)S(1)}, bf16[256,1024]{1,0:T(8,128)(2,1)S(1)}, u32[]{:S(2)}, u32[]{:S(2)}) collective-permute-start(bf16[256,1024]{1,0:T(8,128)(2,1)S(1)} %get-tuple-element.84.q0), channel_id=1, source_target_pairs={{0,8},{8,0},{16,24},{24,16},{32,40},{40,32},{48,56},{56,48},{64,72... | collective-permute-start | bytes 1572872 | tf_op jit(solution)/shard_map/ppermute | solution.py:32
  32.0 7.6 %collective-permute-start.13 = (bf16[128,1024]{1,0:T(8,128)(2,1)S(1)}, bf16[128,1024]{1,0:T(8,128)(2,1)}, u32[]{:S(2)}, u32[]{:S(2)}) collective-permute-start(bf16[128,1024]{1,0:T(8,128)(2,1)S(1)} %get-tuple-element.80.p0), channel_id=1, source_target_pairs={{0,64},{8,72},{16,80},{24,88},{32,96},{40,104},{48,112},{56,120},{... | collective-permute-start | bytes 786440 | tf_op jit(solution)/shard_map/ppermute | solution.py:20
  34.7 12.1 %collective-permute-start.12 = (bf16[128,1024]{1,0:T(8,128)(2,1)S(1)}, bf16[128,1024]{1,0:T(8,128)(2,1)}, u32[]{:S(2)}, u32[]{:S(2)}) collective-permute-start(bf16[128,1024]{1,0:T(8,128)(2,1)S(1)} %get-tuple-element.80.p0), channel_id=1, source_target_pairs={{0,128},{8,136},{16,144},{24,152},{32,160},{40,168},{48,176},{56,1... | collective-permute-start | bytes 786440 | tf_op jit(solution)/shard_map/ppermute | solution.py:20
  36.0 10.8 %collective-permute-start.11 = (bf16[128,1024]{1,0:T(8,128)(2,1)S(1)}, bf16[128,1024]{1,0:T(8,128)(2,1)}, u32[]{:S(2)}, u32[]{:S(2)}) collective-permute-start(bf16[128,1024]{1,0:T(8,128)(2,1)S(1)} %get-tuple-element.80.p0), channel_id=1, source_target_pairs={{0,192},{8,200},{16,208},{24,216},{32,224},{40,232},{48,240},{56,2... | collective-permute-start | bytes 786440 | tf_op jit(solution)/shard_map/ppermute | solution.py:20
  38.0 22.5 %copy-start.1 = (bf16[896,1024]{1,0:T(8,128)(2,1)S(1)}, bf16[896,1024]{1,0:T(8,128)(2,1)}, u32[]{:S(2)}) copy-start(bf16[896,1024]{1,0:T(8,128)(2,1)} %d_n) | copy-start | bytes 5505028
  52.6 17.6 %all-to-all-start = ((f32[32,32,128]{2,1,0:T(8,128)}), f32[32,32,128]{2,1,0:T(8,128)S(1)}, u32[]{:S(2)}, u32[]{:S(2)}) async-start(f32[32,32,128]{2,1,0:T(8,128)} %get-tuple-element.87), calls=%async_computation | async-start | bytes 1048576 | tf_op jit(solution)/shard_map/all_to_all | solution.py:244
  60.5 49.9 %collective-permute-start.25 = (bf16[896,1024]{1,0:T(8,128)(2,1)S(1)}, bf16[896,1024]{1,0:T(8,128)(2,1)}, u32[]{:S(2)}, u32[]{:S(2)}) collective-permute-start(bf16[896,1024]{1,0:T(8,128)(2,1)S(1)} %copy-done.1), channel_id=1, source_target_pairs={{0,1},{1,0},{2,3},{3,2},{4,5},{5,4},{6,7},{7,6},{8,9},{9,8},{10,11... | collective-permute-start | bytes 5505032 | tf_op jit(solution)/shard_map/ppermute | solution.py:36
  71.0 16.5 %all-to-all-start.1 = ((bf16[32,32,128]{2,1,0:T(8,128)(2,1)}), bf16[32,32,128]{2,1,0:T(8,128)(2,1)S(1)}, u32[]{:S(2)}, u32[]{:S(2)}) async-start(bf16[32,32,128]{2,1,0:T(8,128)(2,1)} %broadcast_in_dim.3), calls=%async_computation.1 | async-start | bytes 524288 | tf_op jit(solution)/shard_map/all_to_all | solution.py:248
  77.5 10.0 %copy-start = (s32[512,1]{1,0:T(8,128)S(1)}, s32[512,1]{1,0:T(8,128)}, u32[]{:S(2)}) copy-start(s32[512,1]{1,0:T(8,128)} %copy.10.index) | copy-start | bytes 6148
  77.5 10.0 %copy-start.5 = (s32[7]{0:T(128)S(1)}, s32[7]{0:T(128)}, u32[]{:S(2)}) copy-start(s32[7]{0:T(128)} %copy-done.4) | copy-start | bytes 88
  77.5 19.3 %collective-permute-start.16 = (bf16[128,896]{1,0:T(8,128)(2,1)}, bf16[128,896]{1,0:T(8,128)(2,1)S(1)}, u32[]{:S(2)}, u32[]{:S(2)}) collective-permute-start(bf16[128,896]{1,0:T(8,128)(2,1)} %get-tuple-element.97), channel_id=1, source_target_pairs={{0,2},{1,3},{2,4},{3,5},{4,6},{5,7},{6,0},{7,1},{8,10},{9,11},{10,... | collective-permute-start | bytes 688136 | tf_op jit(solution)/shard_map/ppermute | solution.py:28
  78.5 20.1 %collective-permute-start.17 = (bf16[128,896]{1,0:T(8,128)(2,1)}, bf16[128,896]{1,0:T(8,128)(2,1)S(1)}, u32[]{:S(2)}, u32[]{:S(2)}) collective-permute-start(bf16[128,896]{1,0:T(8,128)(2,1)} %get-tuple-element.98), channel_id=1, source_target_pairs={{0,4},{1,5},{2,6},{3,7},{4,0},{5,1},{6,2},{7,3},{8,12},{9,13},{10,... | collective-permute-start | bytes 688136 | tf_op jit(solution)/shard_map/ppermute | solution.py:28
  87.1 19.6 %copy-start.10 = (f32[128,896]{1,0:T(8,128)S(1)}, f32[128,896]{1,0:T(8,128)}, u32[]{:S(2)}) copy-start(f32[128,896]{1,0:T(8,128)} %get-tuple-element.96) | copy-start | bytes 1376260
  87.1 11.8 %collective-permute-start.18 = (bf16[128,896]{1,0:T(8,128)(2,1)}, bf16[128,896]{1,0:T(8,128)(2,1)S(1)}, u32[]{:S(2)}, u32[]{:S(2)}) collective-permute-start(bf16[128,896]{1,0:T(8,128)(2,1)} %get-tuple-element.99), channel_id=1, source_target_pairs={{0,6},{1,7},{2,0},{3,1},{4,2},{5,3},{6,4},{7,5},{8,14},{9,15},{10,... | collective-permute-start | bytes 688136 | tf_op jit(solution)/shard_map/ppermute | solution.py:28
  95.5 4.9 %collective-permute-start.19 = (bf16[128,896]{1,0:T(8,128)(2,1)S(1)}, bf16[128,896]{1,0:T(8,128)(2,1)S(1)}, u32[]{:S(2)}, u32[]{:S(2)}) collective-permute-start(bf16[128,896]{1,0:T(8,128)(2,1)S(1)} %get-tuple-element.104), channel_id=1, source_target_pairs={{0,2},{1,3},{2,4},{3,5},{4,6},{5,7},{6,0},{7,1},{8,10},{9,11},{10,... | collective-permute-start | bytes 688136 | tf_op jit(solution)/shard_map/ppermute | solution.py:28
  96.8 6.5 %collective-permute-start.20 = (bf16[128,896]{1,0:T(8,128)(2,1)S(1)}, bf16[128,896]{1,0:T(8,128)(2,1)S(1)}, u32[]{:S(2)}, u32[]{:S(2)}) collective-permute-start(bf16[128,896]{1,0:T(8,128)(2,1)S(1)} %get-tuple-element.105), channel_id=1, source_target_pairs={{0,4},{1,5},{2,6},{3,7},{4,0},{5,1},{6,2},{7,3},{8,12},{9,13},{10,... | collective-permute-start | bytes 688136 | tf_op jit(solution)/shard_map/ppermute | solution.py:28
  98.6 8.1 %collective-permute-start.21 = (bf16[128,896]{1,0:T(8,128)(2,1)S(1)}, bf16[128,896]{1,0:T(8,128)(2,1)S(1)}, u32[]{:S(2)}, u32[]{:S(2)}) collective-permute-start(bf16[128,896]{1,0:T(8,128)(2,1)S(1)} %get-tuple-element.106), channel_id=1, source_target_pairs={{0,6},{1,7},{2,0},{3,1},{4,2},{5,3},{6,4},{7,5},{8,14},{9,15},{10,... | collective-permute-start | bytes 688136 | tf_op jit(solution)/shard_map/ppermute | solution.py:28
  107.0 4.9 %collective-permute-start.24 = (bf16[128,896]{1,0:T(8,128)(2,1)S(1)}, bf16[128,896]{1,0:T(8,128)(2,1)S(1)}, u32[]{:S(2)}, u32[]{:S(2)}) collective-permute-start(bf16[128,896]{1,0:T(8,128)(2,1)S(1)} %multiply_convert_fusion.h0), channel_id=1, source_target_pairs={{0,2},{1,3},{2,4},{3,5},{4,6},{5,7},{6,0},{7,1},{8,10},{9,11},{10,... | collective-permute-start | bytes 688136 | tf_op jit(solution)/shard_map/ppermute | solution.py:28
  107.3 6.5 %collective-permute-start.23 = (bf16[128,896]{1,0:T(8,128)(2,1)S(1)}, bf16[128,896]{1,0:T(8,128)(2,1)S(1)}, u32[]{:S(2)}, u32[]{:S(2)}) collective-permute-start(bf16[128,896]{1,0:T(8,128)(2,1)S(1)} %multiply_convert_fusion.h0), channel_id=1, source_target_pairs={{0,4},{1,5},{2,6},{3,7},{4,0},{5,1},{6,2},{7,3},{8,12},{9,13},{10,... | collective-permute-start | bytes 688136 | tf_op jit(solution)/shard_map/ppermute | solution.py:28
  108.7 7.6 %collective-permute-start.22 = (bf16[128,896]{1,0:T(8,128)(2,1)S(1)}, bf16[128,896]{1,0:T(8,128)(2,1)S(1)}, u32[]{:S(2)}, u32[]{:S(2)}) collective-permute-start(bf16[128,896]{1,0:T(8,128)(2,1)S(1)} %multiply_convert_fusion.h0), channel_id=1, source_target_pairs={{0,6},{1,7},{2,0},{3,1},{4,2},{5,3},{6,4},{7,5},{8,14},{9,15},{10,... | collective-permute-start | bytes 688136 | tf_op jit(solution)/shard_map/ppermute | solution.py:28
  120.3 16.3 %collective-permute-start.29 = (bf16[256,1024]{1,0:T(8,128)(2,1)S(1)}, bf16[256,1024]{1,0:T(8,128)(2,1)S(1)}, u32[]{:S(2)}, u32[]{:S(2)}) collective-permute-start(bf16[256,1024]{1,0:T(8,128)(2,1)S(1)} %get-tuple-element.112), channel_id=1, source_target_pairs={{0,8},{8,0},{16,24},{24,16},{32,40},{40,32},{48,56},{56,48},{64,72... | collective-permute-start | bytes 1572872 | tf_op jit(solution)/shard_map/ppermute | solution.py:32
  123.4 7.7 %collective-permute-start.26 = (bf16[128,1024]{1,0:T(8,128)(2,1)S(1)}, bf16[128,1024]{1,0:T(8,128)(2,1)S(1)}, u32[]{:S(2)}, u32[]{:S(2)}) collective-permute-start(bf16[128,1024]{1,0:T(8,128)(2,1)S(1)} %get-tuple-element.109), channel_id=1, source_target_pairs={{0,64},{8,72},{16,80},{24,88},{32,96},{40,104},{48,112},{56,120},{... | collective-permute-start | bytes 786440 | tf_op jit(solution)/shard_map/ppermute | solution.py:20
  126.0 10.5 %collective-permute-start.27 = (bf16[128,1024]{1,0:T(8,128)(2,1)S(1)}, bf16[128,1024]{1,0:T(8,128)(2,1)S(1)}, u32[]{:S(2)}, u32[]{:S(2)}) collective-permute-start(bf16[128,1024]{1,0:T(8,128)(2,1)S(1)} %get-tuple-element.110), channel_id=1, source_target_pairs={{0,128},{8,136},{16,144},{24,152},{32,160},{40,168},{48,176},{56,1... | collective-permute-start | bytes 786440 | tf_op jit(solution)/shard_map/ppermute | solution.py:20
  128.6 7.9 %collective-permute-start.28 = (bf16[128,1024]{1,0:T(8,128)(2,1)S(1)}, bf16[128,1024]{1,0:T(8,128)(2,1)S(1)}, u32[]{:S(2)}, u32[]{:S(2)}) collective-permute-start(bf16[128,1024]{1,0:T(8,128)(2,1)S(1)} %get-tuple-element.111), channel_id=1, source_target_pairs={{0,192},{8,200},{16,208},{24,216},{32,224},{40,232},{48,240},{56,2... | collective-permute-start | bytes 786440 | tf_op jit(solution)/shard_map/ppermute | solution.py:20
  136.7 6.1 %collective-permute-start.30 = (bf16[64,1024]{1,0:T(8,128)(2,1)S(1)}, bf16[64,1024]{1,0:T(8,128)(2,1)S(1)}, u32[]{:S(2)}, u32[]{:S(2)}) collective-permute-start(bf16[64,1024]{1,0:T(8,128)(2,1)S(1)} %slice.97), channel_id=1, source_target_pairs={{0,8},{8,0},{16,24},{24,16},{32,40},{40,32},{48,56},{56,48},{64,72... | collective-permute-start | bytes 393224 | tf_op jit(solution)/shard_map/ppermute | solution.py:32
  137.3 6.0 %collective-permute-start.33 = (bf16[64,1024]{1,0:T(8,128)(2,1)S(1)}, bf16[64,1024]{1,0:T(8,128)(2,1)S(1)}, u32[]{:S(2)}, u32[]{:S(2)}) collective-permute-start(bf16[64,1024]{1,0:T(8,128)(2,1)S(1)} %get-tuple-element.127), channel_id=1, source_target_pairs={{0,192},{8,200},{16,208},{24,216},{32,224},{40,232},{48,240},{56,2... | collective-permute-start | bytes 393224 | tf_op jit(solution)/shard_map/ppermute | solution.py:20
  139.5 5.7 %collective-permute-start.32 = (bf16[64,1024]{1,0:T(8,128)(2,1)S(1)}, bf16[64,1024]{1,0:T(8,128)(2,1)S(1)}, u32[]{:S(2)}, u32[]{:S(2)}) collective-permute-start(bf16[64,1024]{1,0:T(8,128)(2,1)S(1)} %get-tuple-element.128), channel_id=1, source_target_pairs={{0,128},{8,136},{16,144},{24,152},{32,160},{40,168},{48,176},{56,1... | collective-permute-start | bytes 393224 | tf_op jit(solution)/shard_map/ppermute | solution.py:20
  142.8 5.0 %collective-permute-start.31 = (bf16[64,1024]{1,0:T(8,128)(2,1)S(1)}, bf16[64,1024]{1,0:T(8,128)(2,1)S(1)}, u32[]{:S(2)}, u32[]{:S(2)}) collective-permute-start(bf16[64,1024]{1,0:T(8,128)(2,1)S(1)} %get-tuple-element.129), channel_id=1, source_target_pairs={{0,64},{8,72},{16,80},{24,88},{32,96},{40,104},{48,112},{56,120},{... | collective-permute-start | bytes 393224 | tf_op jit(solution)/shard_map/ppermute | solution.py:20
  148.0 8.2 %collective-permute-start.36 = (bf16[16,2048]{1,0:T(8,128)(2,1)S(1)}, bf16[16,2048]{1,0:T(8,128)(2,1)S(1)}, u32[]{:S(2)}, u32[]{:S(2)}) collective-permute-start(bf16[16,2048]{1,0:T(8,128)(2,1)S(1)} %get-tuple-element.130), channel_id=1, source_target_pairs={{0,48},{8,56},{16,0},{24,8},{32,16},{40,24},{48,32},{56,40},{64,11... | collective-permute-start | bytes 196616 | tf_op jit(solution)/shard_map/ppermute | solution.py:24
  152.6 7.1 %collective-permute-start.35 = (bf16[16,2048]{1,0:T(8,128)(2,1)S(1)}, bf16[16,2048]{1,0:T(8,128)(2,1)S(1)}, u32[]{:S(2)}, u32[]{:S(2)}) collective-permute-start(bf16[16,2048]{1,0:T(8,128)(2,1)S(1)} %get-tuple-element.131), channel_id=1, source_target_pairs={{0,32},{8,40},{16,48},{24,56},{32,0},{40,8},{48,16},{56,24},{64,96... | collective-permute-start | bytes 196616 | tf_op jit(solution)/shard_map/ppermute | solution.py:24
  155.4 5.3 %collective-permute-start.34 = (bf16[16,2048]{1,0:T(8,128)(2,1)S(1)}, bf16[16,2048]{1,0:T(8,128)(2,1)S(1)}, u32[]{:S(2)}, u32[]{:S(2)}) collective-permute-start(bf16[16,2048]{1,0:T(8,128)(2,1)S(1)} %get-tuple-element.132), channel_id=1, source_target_pairs={{0,16},{8,24},{16,32},{24,40},{32,48},{40,56},{48,0},{56,8},{64,80... | collective-permute-start | bytes 196616 | tf_op jit(solution)/shard_map/ppermute | solution.py:24
  160.7 6.5 %collective-permute-start.37 = (bf16[16,1024]{1,0:T(8,128)(2,1)S(1)}, bf16[16,1024]{1,0:T(8,128)(2,1)S(1)}, u32[]{:S(2)}, u32[]{:S(2)}) collective-permute-start(bf16[16,1024]{1,0:T(8,128)(2,1)S(1)} %get-tuple-element.134), channel_id=1, source_target_pairs={{0,1},{1,0},{2,3},{3,2},{4,5},{5,4},{6,7},{7,6},{8,9},{9,8},{10,11... | collective-permute-start | bytes 98312 | tf_op jit(solution)/shard_map/ppermute | solution.py:36
  (3 other events, 7.3 us)

commit v5 on v4

--- a/solution.py
+++ b/solution.py
@@ -49,6 +49,7 @@
 
 SMEM = pl.BlockSpec(memory_space=pltpu.SMEM)
 VMEM = pl.BlockSpec(memory_space=pltpu.VMEM)
+HBM = pl.BlockSpec(memory_space=pltpu.HBM)
 
 
 def params(limit=60 * MIB):
@@ -121,9 +122,31 @@
         ref[...] = part.astype(ref.dtype)
 
 
-def base_kernel(t, w_n, w_f, up):
-    width = w_n.shape[0]
-    up[...] = dot(t[:, :width], w_n[...]) + dot(t[:, width:], w_f[...])
+def base_kernel(t, w_n, w_f, up, v_t, v_n, v_f, v_up, sems):
+    width, rows = w_n.shape[0], t.shape[0] // 2
+    get = [
+        pltpu.make_async_copy(t.at[:, :width], v_t.at[:, :width], sems.at[0]),
+        pltpu.make_async_copy(w_n, v_n, sems.at[1]),
+        pltpu.make_async_copy(t.at[:, width:], v_t.at[:, width:], sems.at[2]),
+        pltpu.make_async_copy(w_f, v_f, sems.at[3]),
+    ]
+    for copy in get:
+        copy.start()
+    get[0].wait()
+    get[1].wait()
+    for i in range(2):
+        at = pl.ds(i * rows, rows)
+        v_up[at, :] = dot(v_t[at, :width], v_n[...])
+    get[2].wait()
+    get[3].wait()
+    put = []
+    for i in range(2):
+        at = pl.ds(i * rows, rows)
+        v_up[at, :] += dot(v_t[at, width:], v_f[...])
+        put.append(pltpu.make_async_copy(v_up.at[at, :], up.at[at, :], sems.at[4 + i]))
+        put[-1].start()
+    for copy in put:
+        copy.wait()
 
 
 def up_kernel(rank, place, index, low, up, b_n, b_f, mine, o1, o2, o3, total, wide_low):
@@ -250,8 +273,15 @@
     up_part = pl.pallas_call(
         base_kernel,
         out_shape=shape((everyone, hid), F32),
-        in_specs=[VMEM] * 3,
-        out_specs=VMEM,
+        in_specs=[HBM] * 3,
+        out_specs=HBM,
+        scratch_shapes=[
+            pltpu.VMEM((everyone, 2 * width), BF16),
+            pltpu.VMEM((width, hid), BF16),
+            pltpu.VMEM((width, hid), BF16),
+            pltpu.VMEM((everyone, hid), F32),
+            pltpu.SemaphoreType.DMA((6,)),
+        ],
         compiler_params=params(),
         name="base",
     )(t, up, up_f)

time: 168 us -> 170 us (1.012); the launches traced: 168 us -> 167 us
    ppermute x12, waiting for transfers between devices: 25.2 us -> 28.2 us  [send_x(): lax.ppermute(v, 'wide', [(x * NZ + z, (x + d) % NX * NZ + z) for x in ran...]
    ppermute x9, waiting for transfers between devices: 13.7 us -> 11.3 us  [send_y(): lax.ppermute(v, 'narrow', [(y * NC + c, (y + d) % NY * NC + c) for y in r...]
    ppermute x12, starting transfers between devices: 21.8 us -> 19.8 us  [send_x(): lax.ppermute(v, 'wide', [(x * NZ + z, (x + d) % NX * NZ + z) for x in ran...]
  transfers between devices with their start and end apart: 40 -> 40, of which waited for: 21 -> 22; matrix products, arithmetic and copies ran while one was open for 3% -> 3% of each run, Pallas kernels for 12% -> 11%
where the time goes in v5:
time: 170 us; the launch traced here: 167 us
  starting transfers between devices  78.6 us (46%)
  waiting for transfers between devices  51.8 us (30%)
  Pallas kernels  28.9 us (17%)
  local copies, waits for them, and re-layouts  6.26 us (4%)
    ppermute x12, waiting for transfers between devices, send_x(): lax.ppermute(v, 'wide', [(x * NZ + z, (x + d) % NX * NZ + z) for x in ran...  28.2 us
    ppermute x12, starting transfers between devices, send_x(): lax.ppermute(v, 'wide', [(x * NZ + z, (x + d) % NX * NZ + z) for x in ran...  19.8 us
    ppermute x6, starting transfers between devices, send_z(): lax.ppermute(v, 'wide', [(x * NZ + z, x * NZ + (z + d) % NZ) for x in ran...  17 us
    ppermute x9, starting transfers between devices, send_y(): lax.ppermute(v, 'narrow', [(y * NC + c, (y + d) % NY * NC + c) for y in r...  12.1 us
    ppermute x9, waiting for transfers between devices, send_y(): lax.ppermute(v, 'narrow', [(y * NC + c, (y + d) % NY * NC + c) for y in r...  11.3 us
    ppermute x7, starting transfers between devices, core(): return lax.ppermute(v, 'narrow', [(i, i ^ 1) for i in range(NY * NC)])  9.06 us
    pallas_call x1, Pallas kernels, body(): pl.pallas_call(functools.partial(up_kernel, rank), out_shape=blocks, grid...  8.04 us
    all_to_all x1, starting transfers between devices, body(): lax.all_to_all(low, ('wide', 'narrow'), 0, 0, tiled=True, axis_index_grou...  7.9 us
  transfers between devices with their start and end apart: 40, of which 22 were waited for; matrix products, arithmetic and copies ran while one was open for 3% of the time, Pallas kernels for 11%

profile of v5, /device:TPU:9, one launch (start us, length us, event | category | flops | bytes accessed | tf_op | source)
XLA Modules:
  0.0 167.3 jit_solution(6249486758691812154)
XLA Ops:
  0.7 6.9 %collective-permute-start.1 = (bf16[32,1024]{1,0:T(8,128)(2,1)}, bf16[32,1024]{1,0:T(8,128)(2,1)S(1)}, u32[]{:S(2)}, u32[]{:S(2)}) collective-permute-start(bf16[32,1024]{1,0:T(8,128)(2,1)} %q0.1), channel_id=1, source_target_pairs={{0,32},{8,40},{16,48},{24,56},{32,0},{40,8},{48,16},{56,24},{64,96... | collective-permute-start | bytes 196616 | tf_op jit(solution)/shard_map/ppermute | solution.py:24
  7.6 2.4 %collective-permute-start.2 = (bf16[32,1024]{1,0:T(8,128)(2,1)}, bf16[32,1024]{1,0:T(8,128)(2,1)S(1)}, u32[]{:S(2)}, u32[]{:S(2)}) collective-permute-start(bf16[32,1024]{1,0:T(8,128)(2,1)} %q0.1), channel_id=1, source_target_pairs={{0,16},{8,24},{16,32},{24,40},{32,48},{40,56},{48,0},{56,8},{64,80... | collective-permute-start | bytes 196616 | tf_op jit(solution)/shard_map/ppermute | solution.py:24
  11.0 4.0 %collective-permute-done.q1 = bf16[32,1024]{1,0:T(8,128)(2,1)S(1)} collective-permute-done((bf16[32,1024]{1,0:T(8,128)(2,1)}, bf16[32,1024]{1,0:T(8,128)(2,1)S(1)}, u32[]{:S(2)}, u32[]{:S(2)}) %collective-permute-start) | collective-permute-done | bytes 65568 | tf_op jit(solution)/shard_map/ppermute | solution.py:24
  15.0 1.3 copy-done.7
  19.2 1.5 copy.9.a_n
  20.9 1.3 collective-permute-start.5
  22.2 1.2 collective-permute-start.9
  23.4 2.5 %collective-permute-start.8 = (bf16[64,1024]{1,0:T(8,128)(2,1)S(1)}, bf16[64,1024]{1,0:T(8,128)(2,1)S(1)}, u32[]{:S(2)}, u32[]{:S(2)}) collective-permute-start(bf16[64,1024]{1,0:T(8,128)(2,1)S(1)} %collective-permute-done.6.f0), channel_id=1, source_target_pairs={{0,128},{8,136},{16,144},{24,152},{32,160},{40,168},{48,176},{56,1... | collective-permute-start | bytes 393224 | tf_op jit(solution)/shard_map/ppermute | solution.py:20
  25.9 1.2 collective-permute-start.7
  27.8 3.8 %collective-permute-done.8.f2 = bf16[64,1024]{1,0:T(8,128)(2,1)S(1)} collective-permute-done((bf16[64,1024]{1,0:T(8,128)(2,1)S(1)}, bf16[64,1024]{1,0:T(8,128)(2,1)S(1)}, u32[]{:S(2)}, u32[]{:S(2)}) %collective-permute-start.8) | collective-permute-done | bytes 131104 | tf_op jit(solution)/shard_map/ppermute | solution.py:20
  32.0 2.8 %collective-permute-start.13 = (bf16[128,1024]{1,0:T(8,128)(2,1)S(1)}, bf16[128,1024]{1,0:T(8,128)(2,1)}, u32[]{:S(2)}, u32[]{:S(2)}) collective-permute-start(bf16[128,1024]{1,0:T(8,128)(2,1)S(1)} %get-tuple-element.80.p0), channel_id=1, source_target_pairs={{0,64},{8,72},{16,80},{24,88},{32,96},{40,104},{48,112},{56,120},{... | collective-permute-start | bytes 786440 | tf_op jit(solution)/shard_map/ppermute | solution.py:20
  34.7 1.3 collective-permute-start.12
  36.0 1.1 collective-permute-start.11
  38.0 1.6 collective-permute-done.13.p3
  39.6 7.2 %collective-permute-done.12.p2 = bf16[128,1024]{1,0:T(8,128)(2,1)} collective-permute-done((bf16[128,1024]{1,0:T(8,128)(2,1)S(1)}, bf16[128,1024]{1,0:T(8,128)(2,1)}, u32[]{:S(2)}, u32[]{:S(2)}) %collective-permute-start.12) | collective-permute-done | bytes 262176 | tf_op jit(solution)/shard_map/ppermute | solution.py:20
  47.6 5.0 %shrink.1 = (bf16[512,2048]{1,0:T(8,128)(2,1)}, f32[32,32,128]{2,1,0:T(8,128)}) custom-call(s32[7]{0:T(128)} %copy-done.4, s32[512,1]{1,0:T(8,128)} %copy.10.index, bf16[128,1024]{1,0:T(8,128)(2,1)} %copy-done.3, bf16[128,1024]{1,0:T(8,128)(2,1)} %collective-permute-done.11.p1, bf16[128,1024]{1,0:T(8,128)(2,1)} %collective-permute-done.12.p2, ...), custom_call_target="tpu_custom_call" | custom-call | tf_op jit(solution)/shard_map/shrink/pallas_call | solution.py:241
  52.6 7.9 %all-to-all-start = ((f32[32,32,128]{2,1,0:T(8,128)}), f32[32,32,128]{2,1,0:T(8,128)S(1)}, u32[]{:S(2)}, u32[]{:S(2)}) async-start(f32[32,32,128]{2,1,0:T(8,128)} %get-tuple-element.87), calls=%async_computation | async-start | bytes 1048576 | tf_op jit(solution)/shard_map/all_to_all | solution.py:267
  60.5 1.8 %collective-permute-start.25 = (bf16[896,1024]{1,0:T(8,128)(2,1)S(1)}, bf16[896,1024]{1,0:T(8,128)(2,1)}, u32[]{:S(2)}, u32[]{:S(2)}) collective-permute-start(bf16[896,1024]{1,0:T(8,128)(2,1)S(1)} %copy-done.1), channel_id=1, source_target_pairs={{0,1},{1,0},{2,3},{3,2},{4,5},{5,4},{6,7},{7,6},{8,9},{9,8},{10,11... | collective-permute-start | bytes 5505032 | tf_op jit(solution)/shard_map/ppermute | solution.py:36
  62.3 5.7 %gate.1 = (f32[128,896]{1,0:T(8,128)}, bf16[128,896]{1,0:T(8,128)(2,1)}, bf16[128,896]{1,0:T(8,128)(2,1)}, bf16[128,896]{1,0:T(8,128)(2,1)}) custom-call(s32[7]{0:T(128)} %copy-done.4, bf16[512,2048]{1,0:T(8,128)(2,1)} %get-tuple-element.101.t, bf16[1024,896]{1,0:T(8,128)(2,1)} %w_n, bf16[1024,896]{1,0:T(8,128)(2,1)} %copy-done.7), custom_call_target="tpu_custom_call" | custom-call | tf_op jit(solution)/shard_map/gate/pallas_call | solution.py:257
  68.0 2.2 %all-to-all-done = f32[32,32,128]{2,1,0:T(8,128)S(1)} async-done(((f32[32,32,128]{2,1,0:T(8,128)}), f32[32,32,128]{2,1,0:T(8,128)S(1)}, u32[]{:S(2)}, u32[]{:S(2)}) %all-to-all-start) | async-done | bytes 524320 | tf_op jit(solution)/shard_map/all_to_all | solution.py:267
  71.0 6.5 %all-to-all-start.1 = ((bf16[32,32,128]{2,1,0:T(8,128)(2,1)}), bf16[32,32,128]{2,1,0:T(8,128)(2,1)S(1)}, u32[]{:S(2)}, u32[]{:S(2)}) async-start(bf16[32,32,128]{2,1,0:T(8,128)(2,1)} %broadcast_in_dim.3), calls=%async_computation.1 | async-start | bytes 524288 | tf_op jit(solution)/shard_map/all_to_all | solution.py:271
  77.5 1.0 collective-permute-start.16
  78.5 2.3 %collective-permute-start.17 = (bf16[128,896]{1,0:T(8,128)(2,1)}, bf16[128,896]{1,0:T(8,128)(2,1)S(1)}, u32[]{:S(2)}, u32[]{:S(2)}) collective-permute-start(bf16[128,896]{1,0:T(8,128)(2,1)} %get-tuple-element.98), channel_id=1, source_target_pairs={{0,4},{1,5},{2,6},{3,7},{4,0},{5,1},{6,2},{7,3},{8,12},{9,13},{10,... | collective-permute-start | bytes 688136 | tf_op jit(solution)/shard_map/ppermute | solution.py:28
  80.8 5.3 %base.1.up = f32[512,896]{1,0:T(8,128)} custom-call(bf16[512,2048]{1,0:T(8,128)(2,1)} %get-tuple-element.101.t, bf16[1024,896]{1,0:T(8,128)(2,1)} %w_n.1, bf16[1024,896]{1,0:T(8,128)(2,1)} %collective-permute-done.15.w_f), custom_call_target="tpu_custom_call" | custom-call | tf_op jit(solution)/shard_map/base/pallas_call | solution.py:273
  87.1 8.0 %up.1 = (f32[128,896]{1,0:T(8,128)S(1)}, bf16[128,896]{1,0:T(8,128)(2,1)S(1)}, bf16[128,896]{1,0:T(8,128)(2,1)S(1)}, bf16[128,896]{1,0:T(8,128)(2,1)S(1)}) custom-call(s32[7]{0:T(128)S(1)} %copy-done.5, s32[512,1]{1,0:T(8,128)S(1)} %copy-done, bf16[32,32,128]{2,1,0:T(8,128)(2,1)S(1)} %all-to-all-done.1.low, f32[512,896]{1,0:T(8,128)} %base.1.up, ...), custom_call_target="tpu_custom_call" | custom-call | tf_op jit(solution)/shard_map/up/pallas_call | solution.py:293
  96.2 2.3 %collective-permute-start.20 = (bf16[128,896]{1,0:T(8,128)(2,1)S(1)}, bf16[128,896]{1,0:T(8,128)(2,1)S(1)}, u32[]{:S(2)}, u32[]{:S(2)}) collective-permute-start(bf16[128,896]{1,0:T(8,128)(2,1)S(1)} %get-tuple-element.105), channel_id=1, source_target_pairs={{0,4},{1,5},{2,6},{3,7},{4,0},{5,1},{6,2},{7,3},{8,12},{9,13},{10,... | collective-permute-start | bytes 688136 | tf_op jit(solution)/shard_map/ppermute | solution.py:28
  98.9 1.2 collective-permute-done.19
  100.1 2.5 %collective-permute-done.20 = bf16[128,896]{1,0:T(8,128)(2,1)S(1)} collective-permute-done((bf16[128,896]{1,0:T(8,128)(2,1)S(1)}, bf16[128,896]{1,0:T(8,128)(2,1)S(1)}, u32[]{:S(2)}, u32[]{:S(2)}) %collective-permute-start.20) | collective-permute-done | bytes 229408 | tf_op jit(solution)/shard_map/ppermute | solution.py:28
  102.6 2.7 %collective-permute-done.21 = bf16[128,896]{1,0:T(8,128)(2,1)S(1)} collective-permute-done((bf16[128,896]{1,0:T(8,128)(2,1)S(1)}, bf16[128,896]{1,0:T(8,128)(2,1)S(1)}, u32[]{:S(2)}, u32[]{:S(2)}) %collective-permute-start.21) | collective-permute-done | bytes 229408 | tf_op jit(solution)/shard_map/ppermute | solution.py:28
  106.0 2.5 %collective-permute-start.23 = (bf16[128,896]{1,0:T(8,128)(2,1)S(1)}, bf16[128,896]{1,0:T(8,128)(2,1)S(1)}, u32[]{:S(2)}, u32[]{:S(2)}) collective-permute-start(bf16[128,896]{1,0:T(8,128)(2,1)S(1)} %multiply_convert_fusion.h0), channel_id=1, source_target_pairs={{0,4},{1,5},{2,6},{3,7},{4,0},{5,1},{6,2},{7,3},{8,12},{9,13},{10,... | collective-permute-start | bytes 688136 | tf_op jit(solution)/shard_map/ppermute | solution.py:28
  108.6 1.7 %collective-permute-start.22 = (bf16[128,896]{1,0:T(8,128)(2,1)S(1)}, bf16[128,896]{1,0:T(8,128)(2,1)S(1)}, u32[]{:S(2)}, u32[]{:S(2)}) collective-permute-start(bf16[128,896]{1,0:T(8,128)(2,1)S(1)} %multiply_convert_fusion.h0), channel_id=1, source_target_pairs={{0,6},{1,7},{2,0},{3,1},{4,2},{5,3},{6,4},{7,5},{8,14},{9,15},{10,... | collective-permute-start | bytes 688136 | tf_op jit(solution)/shard_map/ppermute | solution.py:28
  110.6 1.9 %collective-permute-done.23.h2 = bf16[128,896]{1,0:T(8,128)(2,1)S(1)} collective-permute-done((bf16[128,896]{1,0:T(8,128)(2,1)S(1)}, bf16[128,896]{1,0:T(8,128)(2,1)S(1)}, u32[]{:S(2)}, u32[]{:S(2)}) %collective-permute-start.23) | collective-permute-done | bytes 229408 | tf_op jit(solution)/shard_map/ppermute | solution.py:28
  112.5 2.6 %collective-permute-done.22.h1 = bf16[128,896]{1,0:T(8,128)(2,1)S(1)} collective-permute-done((bf16[128,896]{1,0:T(8,128)(2,1)S(1)}, bf16[128,896]{1,0:T(8,128)(2,1)S(1)}, u32[]{:S(2)}, u32[]{:S(2)}) %collective-permute-start.22) | collective-permute-done | bytes 229408 | tf_op jit(solution)/shard_map/ppermute | solution.py:28
  115.2 3.9 %mix.1 = (f32[128,1024]{1,0:T(8,128)S(1)}, bf16[128,1024]{1,0:T(8,128)(2,1)S(1)}, bf16[128,1024]{1,0:T(8,128)(2,1)S(1)}, bf16[128,1024]{1,0:T(8,128)(2,1)S(1)}, ...) custom-call(s32[7]{0:T(128)S(1)} %copy-done.5, bf16[128,896]{1,0:T(8,128)(2,1)S(1)} %multiply_convert_fusion.h0, ...), custom_call_target="tpu_custom_call" | custom-call | tf_op jit(solution)/shard_map/mix/pallas_call | solution.py:307
  119.1 4.5 %collective-permute-start.29 = (bf16[256,1024]{1,0:T(8,128)(2,1)S(1)}, bf16[256,1024]{1,0:T(8,128)(2,1)S(1)}, u32[]{:S(2)}, u32[]{:S(2)}) collective-permute-start(bf16[256,1024]{1,0:T(8,128)(2,1)S(1)} %get-tuple-element.112), channel_id=1, source_target_pairs={{0,8},{8,0},{16,24},{24,16},{32,40},{40,32},{48,56},{56,48},{64,72... | collective-permute-start | bytes 1572872 | tf_op jit(solution)/shard_map/ppermute | solution.py:32
  123.6 2.6 %collective-permute-start.26 = (bf16[128,1024]{1,0:T(8,128)(2,1)S(1)}, bf16[128,1024]{1,0:T(8,128)(2,1)S(1)}, u32[]{:S(2)}, u32[]{:S(2)}) collective-permute-start(bf16[128,1024]{1,0:T(8,128)(2,1)S(1)} %get-tuple-element.109), channel_id=1, source_target_pairs={{0,64},{8,72},{16,80},{24,88},{32,96},{40,104},{48,112},{56,120},{... | collective-permute-start | bytes 786440 | tf_op jit(solution)/shard_map/ppermute | solution.py:20
  126.2 2.7 %collective-permute-start.27 = (bf16[128,1024]{1,0:T(8,128)(2,1)S(1)}, bf16[128,1024]{1,0:T(8,128)(2,1)S(1)}, u32[]{:S(2)}, u32[]{:S(2)}) collective-permute-start(bf16[128,1024]{1,0:T(8,128)(2,1)S(1)} %get-tuple-element.110), channel_id=1, source_target_pairs={{0,128},{8,136},{16,144},{24,152},{32,160},{40,168},{48,176},{56,1... | collective-permute-start | bytes 786440 | tf_op jit(solution)/shard_map/ppermute | solution.py:20
  128.9 2.6 %collective-permute-done.26 = bf16[128,1024]{1,0:T(8,128)(2,1)S(1)} collective-permute-done((bf16[128,1024]{1,0:T(8,128)(2,1)S(1)}, bf16[128,1024]{1,0:T(8,128)(2,1)S(1)}, u32[]{:S(2)}, u32[]{:S(2)}) %collective-permute-start.26) | collective-permute-done | bytes 262176 | tf_op jit(solution)/shard_map/ppermute | solution.py:20
  131.5 6.5 %collective-permute-done.27 = bf16[128,1024]{1,0:T(8,128)(2,1)S(1)} collective-permute-done((bf16[128,1024]{1,0:T(8,128)(2,1)S(1)}, bf16[128,1024]{1,0:T(8,128)(2,1)S(1)}, u32[]{:S(2)}, u32[]{:S(2)}) %collective-permute-start.27) | collective-permute-done | bytes 262176 | tf_op jit(solution)/shard_map/ppermute | solution.py:20
  138.5 3.5 %collective-permute-start.33 = (bf16[64,1024]{1,0:T(8,128)(2,1)S(1)}, bf16[64,1024]{1,0:T(8,128)(2,1)S(1)}, u32[]{:S(2)}, u32[]{:S(2)}) collective-permute-start(bf16[64,1024]{1,0:T(8,128)(2,1)S(1)} %get-tuple-element.127), channel_id=1, source_target_pairs={{0,192},{8,200},{16,208},{24,216},{32,224},{40,232},{48,240},{56,2... | collective-permute-start | bytes 393224 | tf_op jit(solution)/shard_map/ppermute | solution.py:20
  142.9 2.3 %collective-permute-done.33 = bf16[64,1024]{1,0:T(8,128)(2,1)S(1)} collective-permute-done((bf16[64,1024]{1,0:T(8,128)(2,1)S(1)}, bf16[64,1024]{1,0:T(8,128)(2,1)S(1)}, u32[]{:S(2)}, u32[]{:S(2)}) %collective-permute-start.33) | collective-permute-done | bytes 131104 | tf_op jit(solution)/shard_map/ppermute | solution.py:20
  145.3 2.1 %collective-permute-done.32 = bf16[64,1024]{1,0:T(8,128)(2,1)S(1)} collective-permute-done((bf16[64,1024]{1,0:T(8,128)(2,1)S(1)}, bf16[64,1024]{1,0:T(8,128)(2,1)S(1)}, u32[]{:S(2)}, u32[]{:S(2)}) %collective-permute-start.32) | collective-permute-done | bytes 131104 | tf_op jit(solution)/shard_map/ppermute | solution.py:20
  147.4 1.3 collective-permute-done.31
  148.9 4.0 %collective-permute-start.36 = (bf16[16,2048]{1,0:T(8,128)(2,1)S(1)}, bf16[16,2048]{1,0:T(8,128)(2,1)S(1)}, u32[]{:S(2)}, u32[]{:S(2)}) collective-permute-start(bf16[16,2048]{1,0:T(8,128)(2,1)S(1)} %get-tuple-element.130), channel_id=1, source_target_pairs={{0,48},{8,56},{16,0},{24,8},{32,16},{40,24},{48,32},{56,40},{64,11... | collective-permute-start | bytes 196616 | tf_op jit(solution)/shard_map/ppermute | solution.py:24
  152.9 1.5 collective-permute-start.35
  154.4 2.3 %collective-permute-start.34 = (bf16[16,2048]{1,0:T(8,128)(2,1)S(1)}, bf16[16,2048]{1,0:T(8,128)(2,1)S(1)}, u32[]{:S(2)}, u32[]{:S(2)}) collective-permute-start(bf16[16,2048]{1,0:T(8,128)(2,1)S(1)} %get-tuple-element.132), channel_id=1, source_target_pairs={{0,16},{8,24},{16,32},{24,40},{32,48},{40,56},{48,0},{56,8},{64,80... | collective-permute-start | bytes 196616 | tf_op jit(solution)/shard_map/ppermute | solution.py:24
  156.6 3.4 %collective-permute-done.35 = bf16[16,2048]{1,0:T(8,128)(2,1)S(1)} collective-permute-done((bf16[16,2048]{1,0:T(8,128)(2,1)S(1)}, bf16[16,2048]{1,0:T(8,128)(2,1)S(1)}, u32[]{:S(2)}, u32[]{:S(2)}) %collective-permute-start.35) | collective-permute-done | bytes 65568 | tf_op jit(solution)/shard_map/ppermute | solution.py:24
  160.4 5.4 %collective-permute-start.37 = (bf16[16,1024]{1,0:T(8,128)(2,1)S(1)}, bf16[16,1024]{1,0:T(8,128)(2,1)S(1)}, u32[]{:S(2)}, u32[]{:S(2)}) collective-permute-start(bf16[16,1024]{1,0:T(8,128)(2,1)S(1)} %get-tuple-element.134), channel_id=1, source_target_pairs={{0,1},{1,0},{2,3},{3,2},{4,5},{5,4},{6,7},{7,6},{8,9},{9,8},{10,11... | collective-permute-start | bytes 98312 | tf_op jit(solution)/shard_map/ppermute | solution.py:36
  (80 shorter events, 15.1 us)
Async XLA Ops:
  0.0 16.3 %collective-permute-start.3 = (bf16[2048,896]{1,0:T(8,128)(2,1)}, bf16[2048,896]{1,0:T(8,128)(2,1)}, u32[]{:S(2)}, u32[]{:S(2)}) collective-permute-start(bf16[2048,896]{1,0:T(8,128)(2,1)} %bitcast.9), channel_id=1, source_target_pairs={{0,1},{1,0},{2,3},{3,2},{4,5},{5,4},{6,7},{7,6},{8,9},{9,8},{10,11... | collective-permute-start | bytes 11010056 | tf_op jit(solution)/shard_map/ppermute | solution.py:36
  0.7 14.4 %collective-permute-start.4 = (bf16[1024,896]{1,0:T(8,128)(2,1)}, bf16[1024,896]{1,0:T(8,128)(2,1)S(1)}, u32[]{:S(2)}, u32[]{:S(2)}) collective-permute-start(bf16[1024,896]{1,0:T(8,128)(2,1)} %w_n), channel_id=1, source_target_pairs={{0,1},{1,0},{2,3},{3,2},{4,5},{5,4},{6,7},{7,6},{8,9},{9,8},{10,11... | collective-permute-start | bytes 5505032 | tf_op jit(solution)/shard_map/ppermute | solution.py:36
  0.7 10.3 %collective-permute-start.1 = (bf16[32,1024]{1,0:T(8,128)(2,1)}, bf16[32,1024]{1,0:T(8,128)(2,1)S(1)}, u32[]{:S(2)}, u32[]{:S(2)}) collective-permute-start(bf16[32,1024]{1,0:T(8,128)(2,1)} %q0.1), channel_id=1, source_target_pairs={{0,32},{8,40},{16,48},{24,56},{32,0},{40,8},{48,16},{56,24},{64,96... | collective-permute-start | bytes 196616 | tf_op jit(solution)/shard_map/ppermute | solution.py:24
  7.6 7.4 %collective-permute-start = (bf16[32,1024]{1,0:T(8,128)(2,1)}, bf16[32,1024]{1,0:T(8,128)(2,1)S(1)}, u32[]{:S(2)}, u32[]{:S(2)}) collective-permute-start(bf16[32,1024]{1,0:T(8,128)(2,1)} %q0.1), channel_id=1, source_target_pairs={{0,48},{8,56},{16,0},{24,8},{32,16},{40,24},{48,32},{56,40},{64,11... | collective-permute-start | bytes 196616 | tf_op jit(solution)/shard_map/ppermute | solution.py:24
  7.6 7.4 %collective-permute-start.2 = (bf16[32,1024]{1,0:T(8,128)(2,1)}, bf16[32,1024]{1,0:T(8,128)(2,1)S(1)}, u32[]{:S(2)}, u32[]{:S(2)}) collective-permute-start(bf16[32,1024]{1,0:T(8,128)(2,1)} %q0.1), channel_id=1, source_target_pairs={{0,16},{8,24},{16,32},{24,40},{32,48},{40,56},{48,0},{56,8},{64,80... | collective-permute-start | bytes 196616 | tf_op jit(solution)/shard_map/ppermute | solution.py:24
  11.0 35.9 %copy-start.4 = (s32[7]{0:T(128)}, s32[7]{0:T(128)S(1)}, u32[]{:S(2)}) copy-start(s32[7]{0:T(128)S(1)} %stack.31.place) | copy-start | bytes 88
  17.2 1.6 collective-permute-start.6
  18.8 28.0 %collective-permute-start.15 = (bf16[1024,896]{1,0:T(8,128)(2,1)}, bf16[1024,896]{1,0:T(8,128)(2,1)}, u32[]{:S(2)}, u32[]{:S(2)}) collective-permute-start(bf16[1024,896]{1,0:T(8,128)(2,1)} %w_n.1), channel_id=1, source_target_pairs={{0,1},{1,0},{2,3},{3,2},{4,5},{5,4},{6,7},{7,6},{8,9},{9,8},{10,11... | collective-permute-start | bytes 5505032 | tf_op jit(solution)/shard_map/ppermute | solution.py:36
  20.7 5.2 %collective-permute-start.10 = (bf16[1024,512]{1,0:T(8,128)(2,1)S(1)}, bf16[1024,512]{1,0:T(8,128)(2,1)S(1)}, u32[]{:S(2)}, u32[]{:S(2)}) collective-permute-start(bf16[1024,512]{1,0:T(8,128)(2,1)S(1)} %copy.9.a_n), channel_id=1, source_target_pairs={{0,1},{1,0},{2,3},{3,2},{4,5},{5,4},{6,7},{7,6},{8,9},{9,8},{10,11... | collective-permute-start | bytes 3145736 | tf_op jit(solution)/shard_map/ppermute | solution.py:36
  20.9 6.2 %collective-permute-start.5 = (bf16[64,1024]{1,0:T(8,128)(2,1)S(1)}, bf16[64,1024]{1,0:T(8,128)(2,1)S(1)}, u32[]{:S(2)}, u32[]{:S(2)}) collective-permute-start(bf16[64,1024]{1,0:T(8,128)(2,1)S(1)} %get-tuple-element.70.n0), channel_id=1, source_target_pairs={{0,8},{8,0},{16,24},{24,16},{32,40},{40,32},{48,56},{56,48},{64,72... | collective-permute-start | bytes 393224 | tf_op jit(solution)/shard_map/ppermute | solution.py:32
  22.2 5.6 %collective-permute-start.9 = (bf16[64,1024]{1,0:T(8,128)(2,1)S(1)}, bf16[64,1024]{1,0:T(8,128)(2,1)S(1)}, u32[]{:S(2)}, u32[]{:S(2)}) collective-permute-start(bf16[64,1024]{1,0:T(8,128)(2,1)S(1)} %collective-permute-done.6.f0), channel_id=1, source_target_pairs={{0,64},{8,72},{16,80},{24,88},{32,96},{40,104},{48,112},{56,120},{... | collective-permute-start | bytes 393224 | tf_op jit(solution)/shard_map/ppermute | solution.py:20
  23.4 8.2 %collective-permute-start.8 = (bf16[64,1024]{1,0:T(8,128)(2,1)S(1)}, bf16[64,1024]{1,0:T(8,128)(2,1)S(1)}, u32[]{:S(2)}, u32[]{:S(2)}) collective-permute-start(bf16[64,1024]{1,0:T(8,128)(2,1)S(1)} %collective-permute-done.6.f0), channel_id=1, source_target_pairs={{0,128},{8,136},{16,144},{24,152},{32,160},{40,168},{48,176},{56,1... | collective-permute-start | bytes 393224 | tf_op jit(solution)/shard_map/ppermute | solution.py:20
  25.9 5.7 %copy-start.8 = (bf16[1024,512]{1,0:T(8,128)(2,1)}, bf16[1024,512]{1,0:T(8,128)(2,1)S(1)}, u32[]{:S(2)}) copy-start(bf16[1024,512]{1,0:T(8,128)(2,1)S(1)} %collective-permute-done.10.a_f) | copy-start | bytes 3145732
  25.9 5.7 %collective-permute-start.7 = (bf16[64,1024]{1,0:T(8,128)(2,1)S(1)}, bf16[64,1024]{1,0:T(8,128)(2,1)S(1)}, u32[]{:S(2)}, u32[]{:S(2)}) collective-permute-start(bf16[64,1024]{1,0:T(8,128)(2,1)S(1)} %collective-permute-done.6.f0), channel_id=1, source_target_pairs={{0,192},{8,200},{16,208},{24,216},{32,224},{40,232},{48,240},{56,2... | collective-permute-start | bytes 393224 | tf_op jit(solution)/shard_map/ppermute | solution.py:20
  31.7 15.2 %copy-start.2 = (bf16[256,1024]{1,0:T(8,128)(2,1)}, bf16[256,1024]{1,0:T(8,128)(2,1)S(1)}, u32[]{:S(2)}) copy-start(bf16[256,1024]{1,0:T(8,128)(2,1)S(1)} %get-tuple-element.84.q0) | copy-start | bytes 1572868
  31.7 15.2 %copy-start.3 = (bf16[128,1024]{1,0:T(8,128)(2,1)}, bf16[128,1024]{1,0:T(8,128)(2,1)S(1)}, u32[]{:S(2)}) copy-start(bf16[128,1024]{1,0:T(8,128)(2,1)S(1)} %get-tuple-element.80.p0) | copy-start | bytes 786436
  31.7 15.1 %collective-permute-start.14 = (bf16[256,1024]{1,0:T(8,128)(2,1)S(1)}, bf16[256,1024]{1,0:T(8,128)(2,1)S(1)}, u32[]{:S(2)}, u32[]{:S(2)}) collective-permute-start(bf16[256,1024]{1,0:T(8,128)(2,1)S(1)} %get-tuple-element.84.q0), channel_id=1, source_target_pairs={{0,8},{8,0},{16,24},{24,16},{32,40},{40,32},{48,56},{56,48},{64,72... | collective-permute-start | bytes 1572872 | tf_op jit(solution)/shard_map/ppermute | solution.py:32
  32.0 7.6 %collective-permute-start.13 = (bf16[128,1024]{1,0:T(8,128)(2,1)S(1)}, bf16[128,1024]{1,0:T(8,128)(2,1)}, u32[]{:S(2)}, u32[]{:S(2)}) collective-permute-start(bf16[128,1024]{1,0:T(8,128)(2,1)S(1)} %get-tuple-element.80.p0), channel_id=1, source_target_pairs={{0,64},{8,72},{16,80},{24,88},{32,96},{40,104},{48,112},{56,120},{... | collective-permute-start | bytes 786440 | tf_op jit(solution)/shard_map/ppermute | solution.py:20
  34.7 12.1 %collective-permute-start.12 = (bf16[128,1024]{1,0:T(8,128)(2,1)S(1)}, bf16[128,1024]{1,0:T(8,128)(2,1)}, u32[]{:S(2)}, u32[]{:S(2)}) collective-permute-start(bf16[128,1024]{1,0:T(8,128)(2,1)S(1)} %get-tuple-element.80.p0), channel_id=1, source_target_pairs={{0,128},{8,136},{16,144},{24,152},{32,160},{40,168},{48,176},{56,1... | collective-permute-start | bytes 786440 | tf_op jit(solution)/shard_map/ppermute | solution.py:20
  36.0 10.8 %collective-permute-start.11 = (bf16[128,1024]{1,0:T(8,128)(2,1)S(1)}, bf16[128,1024]{1,0:T(8,128)(2,1)}, u32[]{:S(2)}, u32[]{:S(2)}) collective-permute-start(bf16[128,1024]{1,0:T(8,128)(2,1)S(1)} %get-tuple-element.80.p0), channel_id=1, source_target_pairs={{0,192},{8,200},{16,208},{24,216},{32,224},{40,232},{48,240},{56,2... | collective-permute-start | bytes 786440 | tf_op jit(solution)/shard_map/ppermute | solution.py:20
  38.0 22.5 %copy-start.1 = (bf16[896,1024]{1,0:T(8,128)(2,1)S(1)}, bf16[896,1024]{1,0:T(8,128)(2,1)}, u32[]{:S(2)}) copy-start(bf16[896,1024]{1,0:T(8,128)(2,1)} %d_n) | copy-start | bytes 5505028
  52.6 17.6 %all-to-all-start = ((f32[32,32,128]{2,1,0:T(8,128)}), f32[32,32,128]{2,1,0:T(8,128)S(1)}, u32[]{:S(2)}, u32[]{:S(2)}) async-start(f32[32,32,128]{2,1,0:T(8,128)} %get-tuple-element.87), calls=%async_computation | async-start | bytes 1048576 | tf_op jit(solution)/shard_map/all_to_all | solution.py:267
  60.5 49.7 %collective-permute-start.25 = (bf16[896,1024]{1,0:T(8,128)(2,1)S(1)}, bf16[896,1024]{1,0:T(8,128)(2,1)}, u32[]{:S(2)}, u32[]{:S(2)}) collective-permute-start(bf16[896,1024]{1,0:T(8,128)(2,1)S(1)} %copy-done.1), channel_id=1, source_target_pairs={{0,1},{1,0},{2,3},{3,2},{4,5},{5,4},{6,7},{7,6},{8,9},{9,8},{10,11... | collective-permute-start | bytes 5505032 | tf_op jit(solution)/shard_map/ppermute | solution.py:36
  71.0 16.2 %all-to-all-start.1 = ((bf16[32,32,128]{2,1,0:T(8,128)(2,1)}), bf16[32,32,128]{2,1,0:T(8,128)(2,1)S(1)}, u32[]{:S(2)}, u32[]{:S(2)}) async-start(bf16[32,32,128]{2,1,0:T(8,128)(2,1)} %broadcast_in_dim.3), calls=%async_computation.1 | async-start | bytes 524288 | tf_op jit(solution)/shard_map/all_to_all | solution.py:271
  77.5 9.7 %copy-start = (s32[512,1]{1,0:T(8,128)S(1)}, s32[512,1]{1,0:T(8,128)}, u32[]{:S(2)}) copy-start(s32[512,1]{1,0:T(8,128)} %copy.10.index) | copy-start | bytes 6148
  77.5 9.7 %copy-start.5 = (s32[7]{0:T(128)S(1)}, s32[7]{0:T(128)}, u32[]{:S(2)}) copy-start(s32[7]{0:T(128)} %copy-done.4) | copy-start | bytes 88
  77.5 18.7 %collective-permute-start.16 = (bf16[128,896]{1,0:T(8,128)(2,1)}, bf16[128,896]{1,0:T(8,128)(2,1)S(1)}, u32[]{:S(2)}, u32[]{:S(2)}) collective-permute-start(bf16[128,896]{1,0:T(8,128)(2,1)} %get-tuple-element.97), channel_id=1, source_target_pairs={{0,2},{1,3},{2,4},{3,5},{4,6},{5,7},{6,0},{7,1},{8,10},{9,11},{10,... | collective-permute-start | bytes 688136 | tf_op jit(solution)/shard_map/ppermute | solution.py:28
  78.5 20.0 %collective-permute-start.17 = (bf16[128,896]{1,0:T(8,128)(2,1)}, bf16[128,896]{1,0:T(8,128)(2,1)S(1)}, u32[]{:S(2)}, u32[]{:S(2)}) collective-permute-start(bf16[128,896]{1,0:T(8,128)(2,1)} %get-tuple-element.98), channel_id=1, source_target_pairs={{0,4},{1,5},{2,6},{3,7},{4,0},{5,1},{6,2},{7,3},{8,12},{9,13},{10,... | collective-permute-start | bytes 688136 | tf_op jit(solution)/shard_map/ppermute | solution.py:28
  86.2 19.2 %copy-start.10 = (f32[128,896]{1,0:T(8,128)S(1)}, f32[128,896]{1,0:T(8,128)}, u32[]{:S(2)}) copy-start(f32[128,896]{1,0:T(8,128)} %get-tuple-element.96) | copy-start | bytes 1376260
  86.2 12.7 %collective-permute-start.18 = (bf16[128,896]{1,0:T(8,128)(2,1)}, bf16[128,896]{1,0:T(8,128)(2,1)S(1)}, u32[]{:S(2)}, u32[]{:S(2)}) collective-permute-start(bf16[128,896]{1,0:T(8,128)(2,1)} %get-tuple-element.99), channel_id=1, source_target_pairs={{0,6},{1,7},{2,0},{3,1},{4,2},{5,3},{6,4},{7,5},{8,14},{9,15},{10,... | collective-permute-start | bytes 688136 | tf_op jit(solution)/shard_map/ppermute | solution.py:28
  95.2 5.0 %collective-permute-start.19 = (bf16[128,896]{1,0:T(8,128)(2,1)S(1)}, bf16[128,896]{1,0:T(8,128)(2,1)S(1)}, u32[]{:S(2)}, u32[]{:S(2)}) collective-permute-start(bf16[128,896]{1,0:T(8,128)(2,1)S(1)} %get-tuple-element.104), channel_id=1, source_target_pairs={{0,2},{1,3},{2,4},{3,5},{4,6},{5,7},{6,0},{7,1},{8,10},{9,11},{10,... | collective-permute-start | bytes 688136 | tf_op jit(solution)/shard_map/ppermute | solution.py:28
  96.2 6.5 %collective-permute-start.20 = (bf16[128,896]{1,0:T(8,128)(2,1)S(1)}, bf16[128,896]{1,0:T(8,128)(2,1)S(1)}, u32[]{:S(2)}, u32[]{:S(2)}) collective-permute-start(bf16[128,896]{1,0:T(8,128)(2,1)S(1)} %get-tuple-element.105), channel_id=1, source_target_pairs={{0,4},{1,5},{2,6},{3,7},{4,0},{5,1},{6,2},{7,3},{8,12},{9,13},{10,... | collective-permute-start | bytes 688136 | tf_op jit(solution)/shard_map/ppermute | solution.py:28
  98.5 6.8 %collective-permute-start.21 = (bf16[128,896]{1,0:T(8,128)(2,1)S(1)}, bf16[128,896]{1,0:T(8,128)(2,1)S(1)}, u32[]{:S(2)}, u32[]{:S(2)}) collective-permute-start(bf16[128,896]{1,0:T(8,128)(2,1)S(1)} %get-tuple-element.106), channel_id=1, source_target_pairs={{0,6},{1,7},{2,0},{3,1},{4,2},{5,3},{6,4},{7,5},{8,14},{9,15},{10,... | collective-permute-start | bytes 688136 | tf_op jit(solution)/shard_map/ppermute | solution.py:28
  105.6 4.9 %collective-permute-start.24 = (bf16[128,896]{1,0:T(8,128)(2,1)S(1)}, bf16[128,896]{1,0:T(8,128)(2,1)S(1)}, u32[]{:S(2)}, u32[]{:S(2)}) collective-permute-start(bf16[128,896]{1,0:T(8,128)(2,1)S(1)} %multiply_convert_fusion.h0), channel_id=1, source_target_pairs={{0,2},{1,3},{2,4},{3,5},{4,6},{5,7},{6,0},{7,1},{8,10},{9,11},{10,... | collective-permute-start | bytes 688136 | tf_op jit(solution)/shard_map/ppermute | solution.py:28
  106.0 6.5 %collective-permute-start.23 = (bf16[128,896]{1,0:T(8,128)(2,1)S(1)}, bf16[128,896]{1,0:T(8,128)(2,1)S(1)}, u32[]{:S(2)}, u32[]{:S(2)}) collective-permute-start(bf16[128,896]{1,0:T(8,128)(2,1)S(1)} %multiply_convert_fusion.h0), channel_id=1, source_target_pairs={{0,4},{1,5},{2,6},{3,7},{4,0},{5,1},{6,2},{7,3},{8,12},{9,13},{10,... | collective-permute-start | bytes 688136 | tf_op jit(solution)/shard_map/ppermute | solution.py:28
  108.6 6.6 %collective-permute-start.22 = (bf16[128,896]{1,0:T(8,128)(2,1)S(1)}, bf16[128,896]{1,0:T(8,128)(2,1)S(1)}, u32[]{:S(2)}, u32[]{:S(2)}) collective-permute-start(bf16[128,896]{1,0:T(8,128)(2,1)S(1)} %multiply_convert_fusion.h0), channel_id=1, source_target_pairs={{0,6},{1,7},{2,0},{3,1},{4,2},{5,3},{6,4},{7,5},{8,14},{9,15},{10,... | collective-permute-start | bytes 688136 | tf_op jit(solution)/shard_map/ppermute | solution.py:28
  119.1 18.9 %collective-permute-start.29 = (bf16[256,1024]{1,0:T(8,128)(2,1)S(1)}, bf16[256,1024]{1,0:T(8,128)(2,1)S(1)}, u32[]{:S(2)}, u32[]{:S(2)}) collective-permute-start(bf16[256,1024]{1,0:T(8,128)(2,1)S(1)} %get-tuple-element.112), channel_id=1, source_target_pairs={{0,8},{8,0},{16,24},{24,16},{32,40},{40,32},{48,56},{56,48},{64,72... | collective-permute-start | bytes 1572872 | tf_op jit(solution)/shard_map/ppermute | solution.py:32
  123.6 7.9 %collective-permute-start.26 = (bf16[128,1024]{1,0:T(8,128)(2,1)S(1)}, bf16[128,1024]{1,0:T(8,128)(2,1)S(1)}, u32[]{:S(2)}, u32[]{:S(2)}) collective-permute-start(bf16[128,1024]{1,0:T(8,128)(2,1)S(1)} %get-tuple-element.109), channel_id=1, source_target_pairs={{0,64},{8,72},{16,80},{24,88},{32,96},{40,104},{48,112},{56,120},{... | collective-permute-start | bytes 786440 | tf_op jit(solution)/shard_map/ppermute | solution.py:20
  126.2 11.8 %collective-permute-start.27 = (bf16[128,1024]{1,0:T(8,128)(2,1)S(1)}, bf16[128,1024]{1,0:T(8,128)(2,1)S(1)}, u32[]{:S(2)}, u32[]{:S(2)}) collective-permute-start(bf16[128,1024]{1,0:T(8,128)(2,1)S(1)} %get-tuple-element.110), channel_id=1, source_target_pairs={{0,128},{8,136},{16,144},{24,152},{32,160},{40,168},{48,176},{56,1... | collective-permute-start | bytes 786440 | tf_op jit(solution)/shard_map/ppermute | solution.py:20
  128.9 9.1 %collective-permute-start.28 = (bf16[128,1024]{1,0:T(8,128)(2,1)S(1)}, bf16[128,1024]{1,0:T(8,128)(2,1)S(1)}, u32[]{:S(2)}, u32[]{:S(2)}) collective-permute-start(bf16[128,1024]{1,0:T(8,128)(2,1)S(1)} %get-tuple-element.111), channel_id=1, source_target_pairs={{0,192},{8,200},{16,208},{24,216},{32,224},{40,232},{48,240},{56,2... | collective-permute-start | bytes 786440 | tf_op jit(solution)/shard_map/ppermute | solution.py:20
  138.2 4.8 %collective-permute-start.30 = (bf16[64,1024]{1,0:T(8,128)(2,1)S(1)}, bf16[64,1024]{1,0:T(8,128)(2,1)S(1)}, u32[]{:S(2)}, u32[]{:S(2)}) collective-permute-start(bf16[64,1024]{1,0:T(8,128)(2,1)S(1)} %slice.97), channel_id=1, source_target_pairs={{0,8},{8,0},{16,24},{24,16},{32,40},{40,32},{48,56},{56,48},{64,72... | collective-permute-start | bytes 393224 | tf_op jit(solution)/shard_map/ppermute | solution.py:32
  138.5 6.8 %collective-permute-start.33 = (bf16[64,1024]{1,0:T(8,128)(2,1)S(1)}, bf16[64,1024]{1,0:T(8,128)(2,1)S(1)}, u32[]{:S(2)}, u32[]{:S(2)}) collective-permute-start(bf16[64,1024]{1,0:T(8,128)(2,1)S(1)} %get-tuple-element.127), channel_id=1, source_target_pairs={{0,192},{8,200},{16,208},{24,216},{32,224},{40,232},{48,240},{56,2... | collective-permute-start | bytes 393224 | tf_op jit(solution)/shard_map/ppermute | solution.py:20
  142.0 5.4 %collective-permute-start.32 = (bf16[64,1024]{1,0:T(8,128)(2,1)S(1)}, bf16[64,1024]{1,0:T(8,128)(2,1)S(1)}, u32[]{:S(2)}, u32[]{:S(2)}) collective-permute-start(bf16[64,1024]{1,0:T(8,128)(2,1)S(1)} %get-tuple-element.128), channel_id=1, source_target_pairs={{0,128},{8,136},{16,144},{24,152},{32,160},{40,168},{48,176},{56,1... | collective-permute-start | bytes 393224 | tf_op jit(solution)/shard_map/ppermute | solution.py:20
  142.9 5.8 %collective-permute-start.31 = (bf16[64,1024]{1,0:T(8,128)(2,1)S(1)}, bf16[64,1024]{1,0:T(8,128)(2,1)S(1)}, u32[]{:S(2)}, u32[]{:S(2)}) collective-permute-start(bf16[64,1024]{1,0:T(8,128)(2,1)S(1)} %get-tuple-element.129), channel_id=1, source_target_pairs={{0,64},{8,72},{16,80},{24,88},{32,96},{40,104},{48,112},{56,120},{... | collective-permute-start | bytes 393224 | tf_op jit(solution)/shard_map/ppermute | solution.py:20
  148.9 7.8 %collective-permute-start.36 = (bf16[16,2048]{1,0:T(8,128)(2,1)S(1)}, bf16[16,2048]{1,0:T(8,128)(2,1)S(1)}, u32[]{:S(2)}, u32[]{:S(2)}) collective-permute-start(bf16[16,2048]{1,0:T(8,128)(2,1)S(1)} %get-tuple-element.130), channel_id=1, source_target_pairs={{0,48},{8,56},{16,0},{24,8},{32,16},{40,24},{48,32},{56,40},{64,11... | collective-permute-start | bytes 196616 | tf_op jit(solution)/shard_map/ppermute | solution.py:24
  152.9 7.2 %collective-permute-start.35 = (bf16[16,2048]{1,0:T(8,128)(2,1)S(1)}, bf16[16,2048]{1,0:T(8,128)(2,1)S(1)}, u32[]{:S(2)}, u32[]{:S(2)}) collective-permute-start(bf16[16,2048]{1,0:T(8,128)(2,1)S(1)} %get-tuple-element.131), channel_id=1, source_target_pairs={{0,32},{8,40},{16,48},{24,56},{32,0},{40,8},{48,16},{56,24},{64,96... | collective-permute-start | bytes 196616 | tf_op jit(solution)/shard_map/ppermute | solution.py:24
  154.4 6.0 %collective-permute-start.34 = (bf16[16,2048]{1,0:T(8,128)(2,1)S(1)}, bf16[16,2048]{1,0:T(8,128)(2,1)S(1)}, u32[]{:S(2)}, u32[]{:S(2)}) collective-permute-start(bf16[16,2048]{1,0:T(8,128)(2,1)S(1)} %get-tuple-element.132), channel_id=1, source_target_pairs={{0,16},{8,24},{16,32},{24,40},{32,48},{40,56},{48,0},{56,8},{64,80... | collective-permute-start | bytes 196616 | tf_op jit(solution)/shard_map/ppermute | solution.py:24
  160.4 6.3 %collective-permute-start.37 = (bf16[16,1024]{1,0:T(8,128)(2,1)S(1)}, bf16[16,1024]{1,0:T(8,128)(2,1)S(1)}, u32[]{:S(2)}, u32[]{:S(2)}) collective-permute-start(bf16[16,1024]{1,0:T(8,128)(2,1)S(1)} %get-tuple-element.134), channel_id=1, source_target_pairs={{0,1},{1,0},{2,3},{3,2},{4,5},{5,4},{6,7},{7,6},{8,9},{9,8},{10,11... | collective-permute-start | bytes 98312 | tf_op jit(solution)/shard_map/ppermute | solution.py:36
  (3 other events, 7.3 us)
